TPU v7x, 32 devices: a whole 2x2x4 slice. The times are simulated.
32 devices in a mesh: dev: 32 (over z, y, x, core).
Axes of the slice: x: 2, y: 2, z: 4, core: 2. Of those that a mesh axis runs over, the one named last changes fastest.
Arguments:
- hidden_in: bfloat16 [2, 2048, 1280], P(None, 'dev'), may hold values from -6 to 6
- clip_lengths: int32 [2, 3], replicated, may hold values from 1 to 1024, 2048 in all within a row
- ln1_gain: bfloat16 [1280], P('dev'), may hold values from 0.5 to 1.5
- ln1_bias: bfloat16 [1280], P('dev'), may hold values from -1.75 to 1.75
- w_query: bfloat16 [1280, 1280], P('dev'), may hold values from -0.15625 to 0.15625
- b_query: bfloat16 [1280], P('dev'), may hold values from -3 to 3
- w_key: bfloat16 [1280, 1280], P('dev'), may hold values from -0.15625 to 0.15625
- w_value: bfloat16 [1280, 1280], P('dev'), may hold values from -0.15625 to 0.15625
- b_value: bfloat16 [1280], P('dev'), may hold values from -3 to 3
- w_out: bfloat16 [1280, 1280], P('dev'), may hold values from -1 to 1
- b_out: bfloat16 [1280], P('dev'), may hold values from -3 to 3
- ln2_gain: bfloat16 [1280], P('dev'), may hold values from 0.5 to 1.5
- ln2_bias: bfloat16 [1280], P('dev'), may hold values from -1.75 to 1.75
- w_fc1: bfloat16 [1280, 5120], P('dev'), may hold values from -0.15625 to 0.15625
- b_fc1: bfloat16 [5120], P('dev'), may hold values from -3 to 3
- w_fc2: bfloat16 [5120, 1280], P('dev'), may hold values from -0.078125 to 0.078125
- b_fc2: bfloat16 [1280], P('dev'), may hold values from -3 to 3
- cotangent: bfloat16 [2, 2048, 1280], P(None, 'dev'), may hold values from -6 to 6
Outputs:
- layer_out: float32 [2, 2048, 1280], P(None, 'dev')
- input_grad: float32 [2, 2048, 1280], P(None, 'dev')
- grad_ln1_gain: float32 [1280], P('dev')
- grad_ln1_bias: float32 [1280], P('dev')
- grad_w_query: float32 [1280, 1280], P('dev')
- grad_b_query: float32 [1280], P('dev')
- grad_w_key: float32 [1280, 1280], P('dev')
- grad_w_value: float32 [1280, 1280], P('dev')
- grad_b_value: float32 [1280], P('dev')
- grad_w_out: float32 [1280, 1280], P('dev')
- grad_b_out: float32 [1280], P('dev')
- grad_ln2_gain: float32 [1280], P('dev')
- grad_ln2_bias: float32 [1280], P('dev')
- grad_w_fc1: float32 [1280, 5120], P('dev')
- grad_b_fc1: float32 [5120], P('dev')
- grad_w_fc2: float32 [5120, 1280], P('dev')
- grad_b_fc2: float32 [1280], P('dev')
Inputs may be any that keep to these rules, and one draw needn't show every extreme that they name: `clip_lengths`: in each micro-batch the 3 lengths sum to 2048, and some clip has exactly 1024 frames.
All inputs are finite; a program needn't handle non-finite values.
Results may differ from a plain program's by a relative error of at most 0.013.
Values may be sent and summed in bfloat16 or wider, within the bound.
No kernel may reach another device: no remote copies, remote signals or barrier semaphores. Data moves between devices by JAX's collectives and lax.ppermute only.
A program may use at most 448 MiB of HBM per device.

v0:
```python
import jax
import jax.numpy as jnp
from jax import lax
from jax.sharding import PartitionSpec as P

D = 1280
HEADS = 16
HD = 80
REACH = 16


eps = 1e-05
head_group = 4


def passed_along(value, axis, steps):
    count = lax.axis_size(axis)
    initial, last = (max(0, -steps), min(count, count - steps))
    return lax.ppermute(value, axis, [(source, source + steps) for source in range(initial, last)])


def layer_norm(v, gain, shift):
    mean = jnp.mean(v, axis=-1, keepdims=True)
    cent = v - mean
    var = jnp.mean(cent * cent, axis=-1, keepdims=True)
    return cent * lax.rsqrt(var + eps) * gain + shift


def norm_back(v, gain, shift, grad):
    value, pull = jax.vjp(layer_norm, v, gain, shift)
    return pull(grad)


def exact_gelu(v):
    return jax.nn.gelu(v, approximate=False)


def matmul(a, b):
    return jnp.dot(a, b, preferred_element_type=jnp.float32)


def matmul_tn(a, b):
    return lax.dot_general(a, b, (((0,), (0,)), ((), ())), preferred_element_type=jnp.float32)


def matmul_nt(a, b):
    return lax.dot_general(a, b, (((1,), (1,)), ((), ())), preferred_element_type=jnp.float32)


def to_low(v):
    return v.astype(jnp.bfloat16)


def column_sum(v):
    return jnp.sum(v.astype(jnp.float32), axis=0)


def clip_ids(lengths, first, count, total):
    ends = jnp.cumsum(lengths)
    where_at = first + jnp.arange(count, dtype=jnp.int32)
    found = jnp.sum((ends[None, :] <= where_at[:, None]).astype(jnp.int32), axis=1)
    inside = (where_at >= 0) & (where_at < total)
    return jnp.where(inside, found, -1)


def neighbour_rows(local):
    pieces = []
    for position in range(2 * REACH + 1):
        offset = REACH - position
        if offset == 0:
            pieces.append(local)
        else:
            pieces.append(passed_along(local, "dev", offset))
    return jnp.concatenate(pieces, axis=0)


def group_scores(q_grp, k_grp, same):
    scores = jnp.einsum("qhd,khd->hqk", q_grp, k_grp, preferred_element_type=jnp.float32) * (
        1.0 / HD**0.5
    )
    return jnp.where(same[None], scores, -1e30)


def attention(q, kv, same):
    rows = q.shape[0]
    keys = kv[:, :D].reshape(-1, HEADS, HD)
    values = kv[:, D:].reshape(-1, HEADS, HD)
    queries = q.reshape(rows, HEADS, HD)
    pieces = []
    tops = []
    totals = []
    for head in range(0, HEADS, head_group):
        scores = group_scores(
            queries[:, head : head + head_group], keys[:, head : head + head_group], same
        )
        top = jnp.max(scores, axis=-1, keepdims=True)
        expo = jnp.exp(scores - top)
        total = jnp.sum(expo, axis=-1, keepdims=True)
        probs = to_low(expo / total)
        pieces.append(
            jnp.einsum(
                "hqk,khd->qhd",
                probs,
                values[:, head : head + head_group],
                preferred_element_type=jnp.float32,
            )
        )
        tops.append(top)
        totals.append(total)
    return (jnp.concatenate(pieces, axis=1).reshape(rows, D), (tops, totals))


def attention_back(q, kv, same, stats, grad_o):
    rows = q.shape[0]
    keys = kv[:, :D].reshape(-1, HEADS, HD)
    values = kv[:, D:].reshape(-1, HEADS, HD)
    queries = q.reshape(rows, HEADS, HD)
    grads = grad_o.reshape(rows, HEADS, HD)
    tops, totals = stats
    dq_parts = []
    dk_parts = []
    dv_parts = []
    for number, head in enumerate(range(0, HEADS, head_group)):
        q_grp = queries[:, head : head + head_group]
        k_grp = keys[:, head : head + head_group]
        v_grp = values[:, head : head + head_group]
        g_grp = grads[:, head : head + head_group]
        scores = group_scores(q_grp, k_grp, same)
        probs = jnp.exp(scores - tops[number]) / totals[number]
        grad_p = jnp.einsum("qhd,khd->hqk", g_grp, v_grp, preferred_element_type=jnp.float32)
        inner = jnp.sum(probs * grad_p, axis=-1, keepdims=True)
        grad_s = to_low(probs * (grad_p - inner) * (1.0 / HD**0.5))
        dv_parts.append(
            jnp.einsum("hqk,qhd->khd", to_low(probs), g_grp, preferred_element_type=jnp.float32)
        )
        dq_parts.append(
            jnp.einsum("hqk,khd->qhd", grad_s, k_grp, preferred_element_type=jnp.float32)
        )
        dk_parts.append(
            jnp.einsum("hqk,qhd->khd", grad_s, q_grp, preferred_element_type=jnp.float32)
        )
    keys_all = kv.shape[0]
    grad_q = jnp.concatenate(dq_parts, axis=1).reshape(rows, D)
    grad_k = jnp.concatenate(dk_parts, axis=1).reshape(keys_all, D)
    grad_v = jnp.concatenate(dv_parts, axis=1).reshape(keys_all, D)
    return (grad_q, jnp.concatenate([grad_k, grad_v], axis=1))


def forward(x, full, same, finish):
    g1, b1, wq, bq, wk, wv, bv, wo, bo, g2, b2, w1, c1, w2, c2 = full
    a1 = to_low(layer_norm(x, g1.astype(jnp.float32), b1.astype(jnp.float32)))
    q = to_low(matmul(a1, wq) + bq.astype(jnp.float32))
    k = to_low(matmul(a1, wk))
    v = to_low(matmul(a1, wv) + bv.astype(jnp.float32))
    kv = neighbour_rows(jnp.concatenate([k, v], axis=1))
    att, stats = attention(q, kv, same)
    att = to_low(att)
    x2 = x + (matmul(att, wo) + bo.astype(jnp.float32))
    a2 = to_low(layer_norm(x2, g2.astype(jnp.float32), b2.astype(jnp.float32)))
    u = matmul(a2, w1) + c1.astype(jnp.float32)
    hid = to_low(exact_gelu(u))
    if finish:
        return x2 + (matmul(hid, w2) + c2.astype(jnp.float32))
    return (a1, q, kv, stats, att, x2, a2, u, hid)


def backward(x, full, same, saved, grad):
    g1, b1, wq, bq, wk, wv, bv, wo, bo, g2, b2, w1, c1, w2, c2 = full
    a1, q, kv, stats, att, x2, a2, u, hid = saved
    rows = x.shape[0]
    span = REACH * rows
    grad_f = to_low(grad)
    d_w2 = matmul_tn(hid, grad_f)
    d_c2 = column_sum(grad_f)
    d_hid = matmul_nt(grad_f, w2)
    value, pull = jax.vjp(exact_gelu, u)
    grad_u = to_low(pull(d_hid)[0])
    d_w1 = matmul_tn(a2, grad_u)
    d_c1 = column_sum(grad_u)
    d_a2 = matmul_nt(grad_u, w1)
    d_x2n, d_g2, d_b2 = norm_back(x2, g2.astype(jnp.float32), b2.astype(jnp.float32), d_a2)
    d_x2 = grad + d_x2n
    grad_att = to_low(d_x2)
    d_wo = matmul_tn(att, grad_att)
    d_bo = column_sum(grad_att)
    grad_o = to_low(matmul_nt(grad_att, wo))
    grad_q, grad_kv = attention_back(q, kv, same, stats, grad_o)
    owned = grad_kv[span : span + rows]
    pieces = []
    for step in range(1, REACH + 1):
        pieces.append((grad_kv[(REACH - step) * rows : (REACH - step + 1) * rows], -step))
        pieces.append((grad_kv[(REACH + step) * rows : (REACH + step + 1) * rows], step))
    for piece, offset in pieces:
        owned = owned + passed_along(piece.astype(jnp.bfloat16), "dev", offset).astype(piece.dtype)
    kv_low = to_low(owned)
    grad_k = kv_low[:, :D]
    grad_v = kv_low[:, D:]
    q_low = to_low(grad_q)
    d_wq = matmul_tn(a1, q_low)
    d_bq = column_sum(q_low)
    d_wk = matmul_tn(a1, grad_k)
    d_wv = matmul_tn(a1, grad_v)
    d_bv = column_sum(grad_v)
    d_a1 = matmul_nt(q_low, wq) + matmul_nt(grad_k, wk) + matmul_nt(grad_v, wv)
    d_xn, d_g1, d_b1 = norm_back(x, g1.astype(jnp.float32), b1.astype(jnp.float32), d_a1)
    return (
        d_x2 + d_xn,
        (d_g1, d_b1, d_wq, d_bq, d_wk, d_wv, d_bv, d_wo, d_bo, d_g2, d_b2, d_w1, d_c1, d_w2, d_c2),
    )


def body(
    hidden_in,
    clip_lengths,
    ln1_gain,
    ln1_bias,
    w_query,
    b_query,
    w_key,
    w_value,
    b_value,
    w_out,
    b_out,
    ln2_gain,
    ln2_bias,
    w_fc1,
    b_fc1,
    w_fc2,
    b_fc2,
    cotangent,
):
    micro, rows, width = hidden_in.shape
    total = lax.axis_size("dev") * rows
    span = REACH * rows
    first = lax.axis_index("dev") * rows
    sums = None
    outputs = []
    in_grads = []
    for index in range(micro):
        x = hidden_in[index].astype(jnp.float32)
        q_ids = clip_ids(clip_lengths[index], first, rows, total)
        k_ids = clip_ids(clip_lengths[index], first - span, rows + 2 * span, total)
        same = q_ids[:, None] == k_ids[None, :]
        full = (
            lax.all_gather(ln1_gain, "dev", axis=0, tiled=True),
            lax.all_gather(ln1_bias, "dev", axis=0, tiled=True),
            lax.all_gather(w_query, "dev", axis=0, tiled=True),
            lax.all_gather(b_query, "dev", axis=0, tiled=True),
            lax.all_gather(w_key, "dev", axis=0, tiled=True),
            lax.all_gather(w_value, "dev", axis=0, tiled=True),
            lax.all_gather(b_value, "dev", axis=0, tiled=True),
            lax.all_gather(w_out, "dev", axis=0, tiled=True),
            lax.all_gather(b_out, "dev", axis=0, tiled=True),
            lax.all_gather(ln2_gain, "dev", axis=0, tiled=True),
            lax.all_gather(ln2_bias, "dev", axis=0, tiled=True),
            lax.all_gather(w_fc1, "dev", axis=0, tiled=True),
            lax.all_gather(b_fc1, "dev", axis=0, tiled=True),
            lax.all_gather(w_fc2, "dev", axis=0, tiled=True),
            lax.all_gather(b_fc2, "dev", axis=0, tiled=True),
        )
        outputs.append(forward(x, full, same, True))
        full = (
            lax.all_gather(ln1_gain, "dev", axis=0, tiled=True),
            lax.all_gather(ln1_bias, "dev", axis=0, tiled=True),
            lax.all_gather(w_query, "dev", axis=0, tiled=True),
            lax.all_gather(b_query, "dev", axis=0, tiled=True),
            lax.all_gather(w_key, "dev", axis=0, tiled=True),
            lax.all_gather(w_value, "dev", axis=0, tiled=True),
            lax.all_gather(b_value, "dev", axis=0, tiled=True),
            lax.all_gather(w_out, "dev", axis=0, tiled=True),
            lax.all_gather(b_out, "dev", axis=0, tiled=True),
            lax.all_gather(ln2_gain, "dev", axis=0, tiled=True),
            lax.all_gather(ln2_bias, "dev", axis=0, tiled=True),
            lax.all_gather(w_fc1, "dev", axis=0, tiled=True),
            lax.all_gather(b_fc1, "dev", axis=0, tiled=True),
            lax.all_gather(w_fc2, "dev", axis=0, tiled=True),
            lax.all_gather(b_fc2, "dev", axis=0, tiled=True),
        )
        saved = forward(x, full, same, False)
        grad_x, terms = backward(x, full, same, saved, cotangent[index].astype(jnp.float32))
        in_grads.append(grad_x)
        sums = terms if sums is None else tuple((a + b for a, b in zip(sums, terms)))
    reduced = (
        lax.psum_scatter(sums[0], "dev", scatter_dimension=0, tiled=True),
        lax.psum_scatter(sums[1], "dev", scatter_dimension=0, tiled=True),
        lax.psum_scatter(sums[2], "dev", scatter_dimension=0, tiled=True),
        lax.psum_scatter(sums[3], "dev", scatter_dimension=0, tiled=True),
        lax.psum_scatter(sums[4], "dev", scatter_dimension=0, tiled=True),
        lax.psum_scatter(sums[5], "dev", scatter_dimension=0, tiled=True),
        lax.psum_scatter(sums[6], "dev", scatter_dimension=0, tiled=True),
        lax.psum_scatter(sums[7], "dev", scatter_dimension=0, tiled=True),
        lax.psum_scatter(sums[8], "dev", scatter_dimension=0, tiled=True),
        lax.psum_scatter(sums[9], "dev", scatter_dimension=0, tiled=True),
        lax.psum_scatter(sums[10], "dev", scatter_dimension=0, tiled=True),
        lax.psum_scatter(sums[11], "dev", scatter_dimension=0, tiled=True),
        lax.psum_scatter(sums[12], "dev", scatter_dimension=0, tiled=True),
        lax.psum_scatter(sums[13], "dev", scatter_dimension=0, tiled=True),
        lax.psum_scatter(sums[14], "dev", scatter_dimension=0, tiled=True),
    )
    return (jnp.stack(outputs), jnp.stack(in_grads)) + tuple(reduced)


def solution(mesh):
    placed = (
        P(None, "dev", None),
        P(),
        P("dev"),
        P("dev"),
        P("dev", None),
        P("dev"),
        P("dev", None),
        P("dev", None),
        P("dev"),
        P("dev", None),
        P("dev"),
        P("dev"),
        P("dev"),
        P("dev", None),
        P("dev"),
        P("dev", None),
        P("dev"),
        P(None, "dev", None),
    )
    return jax.shard_map(
        body,
        mesh=mesh,
        in_specs=placed,
        out_specs=(
            P(None, "dev", None),
            P(None, "dev", None),
            P("dev"),
            P("dev"),
            P("dev", None),
            P("dev"),
            P("dev", None),
            P("dev", None),
            P("dev"),
            P("dev", None),
            P("dev"),
            P("dev"),
            P("dev"),
            P("dev", None),
            P("dev"),
            P("dev", None),
            P("dev"),
        ),
        check_vma=False,
    )
```

profile of v0, /device:TPU:0, one launch (start us, length us, event | category | flops | bytes accessed | tf_op | source)
XLA Modules:
  0.0 2456.7 jit_solution(7745624722676032865)
XLA Ops:
  18.8 43.5 %all-reduce.19 = (bf16[1280]{0:T(1024)(128)(2,1)S(1)}, bf16[1280]{0:T(1024)(128)(2,1)S(1)}, bf16[1280]{0:T(1024)(128)(2,1)S(1)}, bf16[1280]{0:T(1024)(128)(2,1)S...) all-reduce(bf16[1280]{0:T(1024)(128)(2,1)S(1)} %dynamic-update-slic, ...), channel_id=1, replica_groups=mesh['dev'=32] {'dev'}, use_global_device_ids=true, to_apply=%add.2 | all-reduce | flops 15360 | bytes 61440
  75.9 58.3 %all-gather.9.cloned.1.call-done = bf16[1280,1280]{1,0:T(8,128)(2,1)} async-done(((bf16[40,1280]{1,0:T(8,128)(2,1)}), bf16[1280,1280]{1,0:T(8,128)(2,1)}) %all-gather.9.cloned.1.call-update) | async-done | bytes 3276816 | tf_op jit(solution)/shard_map/all_gather | solution.py:250
  149.3 74.0 %all-gather.11.cloned.1.call-done = bf16[1280,1280]{1,0:T(8,128)(2,1)} async-done(((bf16[40,1280]{1,0:T(8,128)(2,1)}), bf16[1280,1280]{1,0:T(8,128)(2,1)}) %all-gather.11.cloned.1.call-update) | async-done | bytes 3276816 | tf_op jit(solution)/shard_map/all_gather | solution.py:247
  243.9 8.4 collective-permute-start.39
  266.0 12.6 collective-permute-start.44
  281.5 11.0 collective-permute-start.46
  309.3 15.2 collective-permute-done.49
  330.6 18.8 collective-permute-done.52
  355.5 34.6 %collective-permute-done.55 = bf16[64,2560]{1,0:T(8,128)(2,1)S(1)} collective-permute-done((bf16[64,2560]{1,0:T(8,128)(2,1)S(1)}, bf16[64,2560]{1,0:T(8,128)(2,1)S(1)}, u32[]{:S(2)}, u32[]{:S(2)}) %collective-permute-start.55) | collective-permute-done | bytes 327712 | tf_op jit(solution)/shard_map/ppermute | solution.py:19
  398.8 16.1 collective-permute-done.57
  416.9 12.6 collective-permute-done.58
  431.6 11.7 collective-permute-done.59
  443.3 96.8 %collective-permute-start = (bf16[64,2560]{1,0:T(8,128)(2,1)S(1)}, bf16[64,2560]{1,0:T(8,128)(2,1)S(1)}, u32[]{:S(2)}, u32[]{:S(2)}) collective-permute-start(bf16[64,2560]{1,0:T(8,128)(2,1)S(1)} %pad_maximum_fusion.8), channel_id=1, source_target_pairs={{0,16},{1,17},{2,18},{3,19},{4,20},{5,21},{6,22},{7,23},{8,24},{9,... | collective-permute-start | bytes 983048 | tf_op jit(solution)/shard_map/ppermute | solution.py:19
  547.0 19.6 collective-permute-done.63
  568.7 9.0 fusion.488
  577.7 8.5 copy.126
  586.2 8.5 copy.128
  637.8 9.8 collective-permute-done.6
  651.7 10.0 collective-permute-done.7
  666.9 8.8 collective-permute-done.8
  705.0 12.0 collective-permute-done.17
  734.4 14.7 collective-permute-done.21
  753.1 17.5 collective-permute-done.23
  774.7 9.0 collective-permute-done.25
  800.4 8.8 collective-permute-done.29
  812.2 72.1 %collective-permute-done.31 = bf16[64,2560]{1,0:T(8,128)(2,1)S(1)} collective-permute-done((bf16[64,2560]{1,0:T(8,128)(2,1)S(1)}, bf16[64,2560]{1,0:T(8,128)(2,1)S(1)}, u32[]{:S(2)}, u32[]{:S(2)}) %collective-permute-start.31) | collective-permute-done | bytes 327712 | tf_op jit(solution)/shard_map/ppermute | solution.py:19
  885.1 8.9 fusion.487
  894.1 8.5 copy.119
  902.5 8.6 copy.121
  949.0 11.4 convert_reduce_fusion
  960.4 9.1 fusion.536
  969.5 11.2 convert_reduce_fusion.1
  980.7 10.2 multiply_reduce_fusion.9
  1081.2 12.6 copy.146
  1119.2 9.3 pad_maximum_fusion.4
  1128.5 12.5 copy.145
  1145.8 12.5 fusion.16
  1207.9 13.7 collective-permute-start.115
  1235.7 18.3 collective-permute-start.113
  1255.4 9.5 collective-permute-start.111
  1266.2 7.7 collective-permute-start.109
  1274.0 9.3 pad_maximum_fusion.2
  1283.3 12.5 copy.139
  1295.8 12.5 copy.138
  1318.6 14.2 fusion.17
  1355.9 19.2 collective-permute-done.103
  1381.2 14.7 collective-permute-start.95
  1397.2 9.4 collective-permute-start.93
  1407.9 8.5 collective-permute-start.91
  1427.0 14.8 collective-permute-start.87
  1459.4 10.2 collective-permute-start.81
  1471.7 16.8 collective-permute-start.79
  1493.8 13.9 collective-permute-start.77
  1541.4 10.3 collective-permute-done.73
  1554.3 14.9 collective-permute-done.71
  1592.5 10.7 fusion.468
  1603.2 17.4 convolution_add_fusion.1
  1621.6 16.3 fusion.280
  1637.9 16.9 convolution_add_fusion
  1663.3 7.5 fusion.79
  1680.9 50.9 %all-reduce.18 = (f32[1280]{0:T(1024)S(1)}, f32[1280]{0:T(1024)S(1)}, f32[1280]{0:T(1024)S(1)}, f32[1280]{0:T(1024)S(1)}, f32[1280]{0:T(1024)S(1)}, /*index=5*/f...) all-reduce(f32[1280]{0:T(1024)S(1)} %add.653, ...), channel_id=2, replica_groups=mesh['dev'=32] {'dev'}, use_global_device_ids=true, to_apply=%region_48.49.clone | all-reduce | flops 15360 | bytes 122880
  1739.2 144.3 %reduce-scatter.11.cloned.1.call-done = f32[40,1280]{1,0:T(8,128)} async-done(((f32[1280,1280]{1,0:T(8,128)}), f32[40,1280]{1,0:T(8,128)}) %reduce-scatter.11.cloned.1.call-update) | async-done | bytes 204816 | tf_op jit(solution)/shard_map/reduce_scatter | solution.py:289
  1883.5 277.8 %reduce-scatter.15.cloned.1.call-done = f32[40,5120]{1,0:T(8,128)} async-done(((f32[1280,5120]{1,0:T(8,128)}), f32[40,5120]{1,0:T(8,128)}) %reduce-scatter.15.cloned.1.call-update) | async-done | bytes 819216 | tf_op jit(solution)/shard_map/reduce_scatter | solution.py:295
  2161.4 288.0 %reduce-scatter.17.cloned.1.call-done = f32[160,1280]{1,0:T(8,128)} async-done(((f32[5120,1280]{1,0:T(8,128)}), f32[160,1280]{1,0:T(8,128)}) %reduce-scatter.17.cloned.1.call-update) | async-done | bytes 819216 | tf_op jit(solution)/shard_map/reduce_scatter | solution.py:297
  (834 shorter events, 641.0 us)
Async XLA Ops:
  7.2 66.1 %all-gather.7.cloned.1.call-start = ((), (), s32[]{:S(2)}) async-start(), calls=%async_computation.6 | async-start | bytes 3379200 | tf_op jit(solution)/shard_map/all_gather | solution.py:249
  7.9 126.3 %all-gather.9.cloned.1.call-start = ((), (), s32[]{:S(2)}) async-start(), calls=%async_computation.7 | async-start | bytes 3379200 | tf_op jit(solution)/shard_map/all_gather | solution.py:250
  8.7 214.6 %all-gather.11.cloned.1.call-start = ((), (), s32[]{:S(2)}) async-start(), calls=%async_computation.8 | async-start | bytes 3379200 | tf_op jit(solution)/shard_map/all_gather | solution.py:247
  9.4 923.3 %all-gather.13.cloned.1.call-start = ((), (), s32[]{:S(2)}) async-start(), calls=%async_computation.9 | async-start | bytes 3379200 | tf_op jit(solution)/shard_map/all_gather | solution.py:252
  10.0 926.9 %all-gather.15.cloned.1.call-start = ((), (), s32[]{:S(2)}) async-start(), calls=%async_computation.10 | async-start | bytes 13516800 | tf_op jit(solution)/shard_map/all_gather | solution.py:256
  10.6 938.4 %all-gather.17.cloned.1.call-start = ((), (), s32[]{:S(2)}) async-start(), calls=%async_computation.11 | async-start | bytes 13516800 | tf_op jit(solution)/shard_map/all_gather | solution.py:258
  11.2 1727.2 %reduce-scatter.7.cloned.1.call-start = ((), (), s32[]{:S(2)}) async-start(), calls=%async_computation.12 | async-start | bytes 6758400 | tf_op jit(solution)/shard_map/reduce_scatter | solution.py:286
  137.0 97.8 %collective-permute-start.32 = (bf16[64,2560]{1,0:T(8,128)(2,1)S(1)}, bf16[64,2560]{1,0:T(8,128)(2,1)S(1)}, u32[]{:S(2)}, u32[]{:S(2)}) collective-permute-start(bf16[64,2560]{1,0:T(8,128)(2,1)S(1)} %pad_maximum_fusion.9), channel_id=1, source_target_pairs={{0,16},{1,17},{2,18},{3,19},{4,20},{5,21},{6,22},{7,23},{8,24},{9,... | collective-permute-start | bytes 983048 | tf_op jit(solution)/shard_map/ppermute | solution.py:19
  139.8 101.9 %collective-permute-start.33 = (bf16[64,2560]{1,0:T(8,128)(2,1)S(1)}, bf16[64,2560]{1,0:T(8,128)(2,1)S(1)}, u32[]{:S(2)}, u32[]{:S(2)}) collective-permute-start(bf16[64,2560]{1,0:T(8,128)(2,1)S(1)} %pad_maximum_fusion.9), channel_id=1, source_target_pairs={{0,15},{1,16},{2,17},{3,18},{4,19},{5,20},{6,21},{7,22},{8,23},{9,... | collective-permute-start | bytes 983048 | tf_op jit(solution)/shard_map/ppermute | solution.py:19
  144.1 99.8 %collective-permute-start.34 = (bf16[64,2560]{1,0:T(8,128)(2,1)S(1)}, bf16[64,2560]{1,0:T(8,128)(2,1)S(1)}, u32[]{:S(2)}, u32[]{:S(2)}) collective-permute-start(bf16[64,2560]{1,0:T(8,128)(2,1)S(1)} %pad_maximum_fusion.9), channel_id=1, source_target_pairs={{0,14},{1,15},{2,16},{3,17},{4,18},{5,19},{6,20},{7,21},{8,22},{9,... | collective-permute-start | bytes 983048 | tf_op jit(solution)/shard_map/ppermute | solution.py:19
  146.6 106.5 %collective-permute-start.35 = (bf16[64,2560]{1,0:T(8,128)(2,1)S(1)}, bf16[64,2560]{1,0:T(8,128)(2,1)S(1)}, u32[]{:S(2)}, u32[]{:S(2)}) collective-permute-start(bf16[64,2560]{1,0:T(8,128)(2,1)S(1)} %pad_maximum_fusion.9), channel_id=1, source_target_pairs={{0,13},{1,14},{2,15},{3,16},{4,17},{5,18},{6,19},{7,20},{8,21},{9,... | collective-permute-start | bytes 983048 | tf_op jit(solution)/shard_map/ppermute | solution.py:19
  147.9 107.3 %collective-permute-start.36 = (bf16[64,2560]{1,0:T(8,128)(2,1)S(1)}, bf16[64,2560]{1,0:T(8,128)(2,1)S(1)}, u32[]{:S(2)}, u32[]{:S(2)}) collective-permute-start(bf16[64,2560]{1,0:T(8,128)(2,1)S(1)} %pad_maximum_fusion.9), channel_id=1, source_target_pairs={{0,12},{1,13},{2,14},{3,15},{4,16},{5,17},{6,18},{7,19},{8,20},{9,... | collective-permute-start | bytes 983048 | tf_op jit(solution)/shard_map/ppermute | solution.py:19
  304.4 44.9 %collective-permute-start.52 = (bf16[64,2560]{1,0:T(8,128)(2,1)S(1)}, bf16[64,2560]{1,0:T(8,128)(2,1)S(1)}, u32[]{:S(2)}, u32[]{:S(2)}) collective-permute-start(bf16[64,2560]{1,0:T(8,128)(2,1)S(1)} %pad_maximum_fusion.9), channel_id=1, source_target_pairs={{5,0},{6,1},{7,2},{8,3},{9,4},{10,5},{11,6},{12,7},{13,8},{14,9},{... | collective-permute-start | bytes 983048 | tf_op jit(solution)/shard_map/ppermute | solution.py:19
  307.2 44.2 %collective-permute-start.53 = (bf16[64,2560]{1,0:T(8,128)(2,1)S(1)}, bf16[64,2560]{1,0:T(8,128)(2,1)S(1)}, u32[]{:S(2)}, u32[]{:S(2)}) collective-permute-start(bf16[64,2560]{1,0:T(8,128)(2,1)S(1)} %pad_maximum_fusion.9), channel_id=1, source_target_pairs={{6,0},{7,1},{8,2},{9,3},{10,4},{11,5},{12,6},{13,7},{14,8},{15,9},... | collective-permute-start | bytes 983048 | tf_op jit(solution)/shard_map/ppermute | solution.py:19
  326.5 63.6 %collective-permute-start.55 = (bf16[64,2560]{1,0:T(8,128)(2,1)S(1)}, bf16[64,2560]{1,0:T(8,128)(2,1)S(1)}, u32[]{:S(2)}, u32[]{:S(2)}) collective-permute-start(bf16[64,2560]{1,0:T(8,128)(2,1)S(1)} %pad_maximum_fusion.9), channel_id=1, source_target_pairs={{8,0},{9,1},{10,2},{11,3},{12,4},{13,5},{14,6},{15,7},{16,8},{17,9... | collective-permute-start | bytes 983048 | tf_op jit(solution)/shard_map/ppermute | solution.py:19
  328.6 67.9 %collective-permute-start.56 = (bf16[64,2560]{1,0:T(8,128)(2,1)S(1)}, bf16[64,2560]{1,0:T(8,128)(2,1)S(1)}, u32[]{:S(2)}, u32[]{:S(2)}) collective-permute-start(bf16[64,2560]{1,0:T(8,128)(2,1)S(1)} %pad_maximum_fusion.9), channel_id=1, source_target_pairs={{9,0},{10,1},{11,2},{12,3},{13,4},{14,5},{15,6},{16,7},{17,8},{18,... | collective-permute-start | bytes 983048 | tf_op jit(solution)/shard_map/ppermute | solution.py:19
  349.4 65.5 %collective-permute-start.57 = (bf16[64,2560]{1,0:T(8,128)(2,1)S(1)}, bf16[64,2560]{1,0:T(8,128)(2,1)S(1)}, u32[]{:S(2)}, u32[]{:S(2)}) collective-permute-start(bf16[64,2560]{1,0:T(8,128)(2,1)S(1)} %pad_maximum_fusion.9), channel_id=1, source_target_pairs={{10,0},{11,1},{12,2},{13,3},{14,4},{15,5},{16,6},{17,7},{18,8},{19... | collective-permute-start | bytes 983048 | tf_op jit(solution)/shard_map/ppermute | solution.py:19
  351.4 78.1 %collective-permute-start.58 = (bf16[64,2560]{1,0:T(8,128)(2,1)S(1)}, bf16[64,2560]{1,0:T(8,128)(2,1)S(1)}, u32[]{:S(2)}, u32[]{:S(2)}) collective-permute-start(bf16[64,2560]{1,0:T(8,128)(2,1)S(1)} %pad_maximum_fusion.9), channel_id=1, source_target_pairs={{11,0},{12,1},{13,2},{14,3},{15,4},{16,5},{17,6},{18,7},{19,8},{20... | collective-permute-start | bytes 983048 | tf_op jit(solution)/shard_map/ppermute | solution.py:19
  353.4 89.8 %collective-permute-start.59 = (bf16[64,2560]{1,0:T(8,128)(2,1)S(1)}, bf16[64,2560]{1,0:T(8,128)(2,1)S(1)}, u32[]{:S(2)}, u32[]{:S(2)}) collective-permute-start(bf16[64,2560]{1,0:T(8,128)(2,1)S(1)} %pad_maximum_fusion.9), channel_id=1, source_target_pairs={{12,0},{13,1},{14,2},{15,3},{16,4},{17,5},{18,6},{19,7},{20,8},{21... | collective-permute-start | bytes 983048 | tf_op jit(solution)/shard_map/ppermute | solution.py:19
  390.2 150.6 %collective-permute-start.60 = (bf16[64,2560]{1,0:T(8,128)(2,1)S(1)}, bf16[64,2560]{1,0:T(8,128)(2,1)S(1)}, u32[]{:S(2)}, u32[]{:S(2)}) collective-permute-start(bf16[64,2560]{1,0:T(8,128)(2,1)S(1)} %pad_maximum_fusion.9), channel_id=1, source_target_pairs={{13,0},{14,1},{15,2},{16,3},{17,4},{18,5},{19,6},{20,7},{21,8},{22... | collective-permute-start | bytes 983048 | tf_op jit(solution)/shard_map/ppermute | solution.py:19
  396.5 146.4 %collective-permute-start.61 = (bf16[64,2560]{1,0:T(8,128)(2,1)S(1)}, bf16[64,2560]{1,0:T(8,128)(2,1)S(1)}, u32[]{:S(2)}, u32[]{:S(2)}) collective-permute-start(bf16[64,2560]{1,0:T(8,128)(2,1)S(1)} %pad_maximum_fusion.9), channel_id=1, source_target_pairs={{14,0},{15,1},{16,2},{17,3},{18,4},{19,5},{20,6},{21,7},{22,8},{23... | collective-permute-start | bytes 983048 | tf_op jit(solution)/shard_map/ppermute | solution.py:19
  414.9 130.0 %collective-permute-start.62 = (bf16[64,2560]{1,0:T(8,128)(2,1)S(1)}, bf16[64,2560]{1,0:T(8,128)(2,1)S(1)}, u32[]{:S(2)}, u32[]{:S(2)}) collective-permute-start(bf16[64,2560]{1,0:T(8,128)(2,1)S(1)} %pad_maximum_fusion.9), channel_id=1, source_target_pairs={{15,0},{16,1},{17,2},{18,3},{19,4},{20,5},{21,6},{22,7},{23,8},{24... | collective-permute-start | bytes 983048 | tf_op jit(solution)/shard_map/ppermute | solution.py:19
  429.6 137.1 %collective-permute-start.63 = (bf16[64,2560]{1,0:T(8,128)(2,1)S(1)}, bf16[64,2560]{1,0:T(8,128)(2,1)S(1)}, u32[]{:S(2)}, u32[]{:S(2)}) collective-permute-start(bf16[64,2560]{1,0:T(8,128)(2,1)S(1)} %pad_maximum_fusion.9), channel_id=1, source_target_pairs={{16,0},{17,1},{18,2},{19,3},{20,4},{21,5},{22,6},{23,7},{24,8},{25... | collective-permute-start | bytes 983048 | tf_op jit(solution)/shard_map/ppermute | solution.py:19
  443.3 174.3 %collective-permute-start = (bf16[64,2560]{1,0:T(8,128)(2,1)S(1)}, bf16[64,2560]{1,0:T(8,128)(2,1)S(1)}, u32[]{:S(2)}, u32[]{:S(2)}) collective-permute-start(bf16[64,2560]{1,0:T(8,128)(2,1)S(1)} %pad_maximum_fusion.8), channel_id=1, source_target_pairs={{0,16},{1,17},{2,18},{3,19},{4,20},{5,21},{6,22},{7,23},{8,24},{9,... | collective-permute-start | bytes 983048 | tf_op jit(solution)/shard_map/ppermute | solution.py:19
  540.8 78.9 %collective-permute-start.1 = (bf16[64,2560]{1,0:T(8,128)(2,1)S(1)}, bf16[64,2560]{1,0:T(8,128)(2,1)S(1)}, u32[]{:S(2)}, u32[]{:S(2)}) collective-permute-start(bf16[64,2560]{1,0:T(8,128)(2,1)S(1)} %pad_maximum_fusion.8), channel_id=1, source_target_pairs={{0,15},{1,16},{2,17},{3,18},{4,19},{5,20},{6,21},{7,22},{8,23},{9,... | collective-permute-start | bytes 983048 | tf_op jit(solution)/shard_map/ppermute | solution.py:19
  542.8 78.9 %collective-permute-start.2 = (bf16[64,2560]{1,0:T(8,128)(2,1)S(1)}, bf16[64,2560]{1,0:T(8,128)(2,1)S(1)}, u32[]{:S(2)}, u32[]{:S(2)}) collective-permute-start(bf16[64,2560]{1,0:T(8,128)(2,1)S(1)} %pad_maximum_fusion.8), channel_id=1, source_target_pairs={{0,14},{1,15},{2,16},{3,17},{4,18},{5,19},{6,20},{7,21},{8,22},{9,... | collective-permute-start | bytes 983048 | tf_op jit(solution)/shard_map/ppermute | solution.py:19
  544.9 78.9 %collective-permute-start.3 = (bf16[64,2560]{1,0:T(8,128)(2,1)S(1)}, bf16[64,2560]{1,0:T(8,128)(2,1)S(1)}, u32[]{:S(2)}, u32[]{:S(2)}) collective-permute-start(bf16[64,2560]{1,0:T(8,128)(2,1)S(1)} %pad_maximum_fusion.8), channel_id=1, source_target_pairs={{0,13},{1,14},{2,15},{3,16},{4,17},{5,18},{6,19},{7,20},{8,21},{9,... | collective-permute-start | bytes 983048 | tf_op jit(solution)/shard_map/ppermute | solution.py:19
  566.6 61.5 %collective-permute-start.4 = (bf16[64,2560]{1,0:T(8,128)(2,1)S(1)}, bf16[64,2560]{1,0:T(8,128)(2,1)S(1)}, u32[]{:S(2)}, u32[]{:S(2)}) collective-permute-start(bf16[64,2560]{1,0:T(8,128)(2,1)S(1)} %pad_maximum_fusion.8), channel_id=1, source_target_pairs={{0,12},{1,13},{2,14},{3,15},{4,16},{5,17},{6,18},{7,19},{8,20},{9,... | collective-permute-start | bytes 983048 | tf_op jit(solution)/shard_map/ppermute | solution.py:19
  621.8 39.9 %collective-permute-start.7 = (bf16[64,2560]{1,0:T(8,128)(2,1)S(1)}, bf16[64,2560]{1,0:T(8,128)(2,1)S(1)}, u32[]{:S(2)}, u32[]{:S(2)}) collective-permute-start(bf16[64,2560]{1,0:T(8,128)(2,1)S(1)} %pad_maximum_fusion.8), channel_id=1, source_target_pairs={{0,9},{1,10},{2,11},{3,12},{4,13},{5,14},{6,15},{7,16},{8,17},{9,1... | collective-permute-start | bytes 983048 | tf_op jit(solution)/shard_map/ppermute | solution.py:19
  623.8 51.9 %collective-permute-start.8 = (bf16[64,2560]{1,0:T(8,128)(2,1)S(1)}, bf16[64,2560]{1,0:T(8,128)(2,1)S(1)}, u32[]{:S(2)}, u32[]{:S(2)}) collective-permute-start(bf16[64,2560]{1,0:T(8,128)(2,1)S(1)} %pad_maximum_fusion.8), channel_id=1, source_target_pairs={{0,8},{1,9},{2,10},{3,11},{4,12},{5,13},{6,14},{7,15},{8,16},{9,17... | collective-permute-start | bytes 983048 | tf_op jit(solution)/shard_map/ppermute | solution.py:19
  628.1 49.6 %collective-permute-start.9 = (bf16[64,2560]{1,0:T(8,128)(2,1)S(1)}, bf16[64,2560]{1,0:T(8,128)(2,1)S(1)}, u32[]{:S(2)}, u32[]{:S(2)}) collective-permute-start(bf16[64,2560]{1,0:T(8,128)(2,1)S(1)} %pad_maximum_fusion.8), channel_id=1, source_target_pairs={{0,7},{1,8},{2,9},{3,10},{4,11},{5,12},{6,13},{7,14},{8,15},{9,16}... | collective-permute-start | bytes 983048 | tf_op jit(solution)/shard_map/ppermute | solution.py:19
  633.6 50.3 %collective-permute-start.10 = (bf16[64,2560]{1,0:T(8,128)(2,1)S(1)}, bf16[64,2560]{1,0:T(8,128)(2,1)S(1)}, u32[]{:S(2)}, u32[]{:S(2)}) collective-permute-start(bf16[64,2560]{1,0:T(8,128)(2,1)S(1)} %pad_maximum_fusion.8), channel_id=1, source_target_pairs={{0,6},{1,7},{2,8},{3,9},{4,10},{5,11},{6,12},{7,13},{8,14},{9,15},... | collective-permute-start | bytes 983048 | tf_op jit(solution)/shard_map/ppermute | solution.py:19
  647.6 44.4 %collective-permute-start.11 = (bf16[64,2560]{1,0:T(8,128)(2,1)S(1)}, bf16[64,2560]{1,0:T(8,128)(2,1)S(1)}, u32[]{:S(2)}, u32[]{:S(2)}) collective-permute-start(bf16[64,2560]{1,0:T(8,128)(2,1)S(1)} %pad_maximum_fusion.8), channel_id=1, source_target_pairs={{0,5},{1,6},{2,7},{3,8},{4,9},{5,10},{6,11},{7,12},{8,13},{9,14},{... | collective-permute-start | bytes 983048 | tf_op jit(solution)/shard_map/ppermute | solution.py:19
  703.0 46.1 %collective-permute-start.21 = (bf16[64,2560]{1,0:T(8,128)(2,1)S(1)}, bf16[64,2560]{1,0:T(8,128)(2,1)S(1)}, u32[]{:S(2)}, u32[]{:S(2)}) collective-permute-start(bf16[64,2560]{1,0:T(8,128)(2,1)S(1)} %pad_maximum_fusion.8), channel_id=1, source_target_pairs={{6,0},{7,1},{8,2},{9,3},{10,4},{11,5},{12,6},{13,7},{14,8},{15,9},... | collective-permute-start | bytes 983048 | tf_op jit(solution)/shard_map/ppermute | solution.py:19
  720.0 50.6 %collective-permute-start.23 = (bf16[64,2560]{1,0:T(8,128)(2,1)S(1)}, bf16[64,2560]{1,0:T(8,128)(2,1)S(1)}, u32[]{:S(2)}, u32[]{:S(2)}) collective-permute-start(bf16[64,2560]{1,0:T(8,128)(2,1)S(1)} %pad_maximum_fusion.8), channel_id=1, source_target_pairs={{8,0},{9,1},{10,2},{11,3},{12,4},{13,5},{14,6},{15,7},{16,8},{17,9... | collective-permute-start | bytes 983048 | tf_op jit(solution)/shard_map/ppermute | solution.py:19
  729.3 43.4 %collective-permute-start.24 = (bf16[64,2560]{1,0:T(8,128)(2,1)S(1)}, bf16[64,2560]{1,0:T(8,128)(2,1)S(1)}, u32[]{:S(2)}, u32[]{:S(2)}) collective-permute-start(bf16[64,2560]{1,0:T(8,128)(2,1)S(1)} %pad_maximum_fusion.8), channel_id=1, source_target_pairs={{9,0},{10,1},{11,2},{12,3},{13,4},{14,5},{15,6},{16,7},{17,8},{18,... | collective-permute-start | bytes 983048 | tf_op jit(solution)/shard_map/ppermute | solution.py:19
  732.3 51.4 %collective-permute-start.25 = (bf16[64,2560]{1,0:T(8,128)(2,1)S(1)}, bf16[64,2560]{1,0:T(8,128)(2,1)S(1)}, u32[]{:S(2)}, u32[]{:S(2)}) collective-permute-start(bf16[64,2560]{1,0:T(8,128)(2,1)S(1)} %pad_maximum_fusion.8), channel_id=1, source_target_pairs={{10,0},{11,1},{12,2},{13,3},{14,4},{15,5},{16,6},{17,7},{18,8},{19... | collective-permute-start | bytes 983048 | tf_op jit(solution)/shard_map/ppermute | solution.py:19
  751.1 43.5 %collective-permute-start.27 = (bf16[64,2560]{1,0:T(8,128)(2,1)S(1)}, bf16[64,2560]{1,0:T(8,128)(2,1)S(1)}, u32[]{:S(2)}, u32[]{:S(2)}) collective-permute-start(bf16[64,2560]{1,0:T(8,128)(2,1)S(1)} %pad_maximum_fusion.8), channel_id=1, source_target_pairs={{12,0},{13,1},{14,2},{15,3},{16,4},{17,5},{18,6},{19,7},{20,8},{21... | collective-permute-start | bytes 983048 | tf_op jit(solution)/shard_map/ppermute | solution.py:19
  785.8 98.6 %collective-permute-start.31 = (bf16[64,2560]{1,0:T(8,128)(2,1)S(1)}, bf16[64,2560]{1,0:T(8,128)(2,1)S(1)}, u32[]{:S(2)}, u32[]{:S(2)}) collective-permute-start(bf16[64,2560]{1,0:T(8,128)(2,1)S(1)} %pad_maximum_fusion.8), channel_id=1, source_target_pairs={{16,0},{17,1},{18,2},{19,3},{20,4},{21,5},{22,6},{23,7},{24,8},{25... | collective-permute-start | bytes 983048 | tf_op jit(solution)/shard_map/ppermute | solution.py:19
  1070.1 668.3 %reduce-scatter.13.cloned.1.call-start = ((), (), s32[]{:S(2)}) async-start(), calls=%async_computation.15 | async-start | bytes 6758400 | tf_op jit(solution)/shard_map/reduce_scatter | solution.py:291
  1158.3 580.9 %reduce-scatter.9.cloned.1.call-start = ((), (), s32[]{:S(2)}) async-start(), calls=%async_computation.13 | async-start | bytes 6758400 | tf_op jit(solution)/shard_map/reduce_scatter | solution.py:288
  1204.3 49.8 %collective-permute-start.117 = (bf16[64,2560]{1,0:T(8,128)(2,1)}, bf16[64,2560]{1,0:T(8,128)(2,1)}, u32[]{:S(2)}, u32[]{:S(2)}) collective-permute-start(bf16[64,2560]{1,0:T(8,128)(2,1)} %get-tuple-element.84), channel_id=1, source_target_pairs={{0,11},{1,12},{2,13},{3,14},{4,15},{5,16},{6,17},{7,18},{8,19},{9,... | collective-permute-start | bytes 983048 | tf_op jit(solution)/shard_map/ppermute | solution.py:19
  1206.6 48.8 %collective-permute-start.116 = (bf16[64,2560]{1,0:T(8,128)(2,1)}, bf16[64,2560]{1,0:T(8,128)(2,1)}, u32[]{:S(2)}, u32[]{:S(2)}) collective-permute-start(bf16[64,2560]{1,0:T(8,128)(2,1)} %get-tuple-element.85), channel_id=1, source_target_pairs={{11,0},{12,1},{13,2},{14,3},{15,4},{16,5},{17,6},{18,7},{19,8},{20... | collective-permute-start | bytes 983048 | tf_op jit(solution)/shard_map/ppermute | solution.py:19
  1207.9 57.0 %collective-permute-start.115 = (bf16[64,2560]{1,0:T(8,128)(2,1)}, bf16[64,2560]{1,0:T(8,128)(2,1)}, u32[]{:S(2)}, u32[]{:S(2)}) collective-permute-start(bf16[64,2560]{1,0:T(8,128)(2,1)} %get-tuple-element.86), channel_id=1, source_target_pairs={{0,10},{1,11},{2,12},{3,13},{4,14},{5,15},{6,16},{7,17},{8,18},{9,... | collective-permute-start | bytes 983048 | tf_op jit(solution)/shard_map/ppermute | solution.py:19
  1221.6 44.6 %collective-permute-start.114 = (bf16[64,2560]{1,0:T(8,128)(2,1)}, bf16[64,2560]{1,0:T(8,128)(2,1)}, u32[]{:S(2)}, u32[]{:S(2)}) collective-permute-start(bf16[64,2560]{1,0:T(8,128)(2,1)} %get-tuple-element.87), channel_id=1, source_target_pairs={{10,0},{11,1},{12,2},{13,3},{14,4},{15,5},{16,6},{17,7},{18,8},{19... | collective-permute-start | bytes 983048 | tf_op jit(solution)/shard_map/ppermute | solution.py:19
  1235.7 72.6 %collective-permute-start.113 = (bf16[64,2560]{1,0:T(8,128)(2,1)}, bf16[64,2560]{1,0:T(8,128)(2,1)S(1)}, u32[]{:S(2)}, u32[]{:S(2)}) collective-permute-start(bf16[64,2560]{1,0:T(8,128)(2,1)} %get-tuple-element.88), channel_id=1, source_target_pairs={{0,9},{1,10},{2,11},{3,12},{4,13},{5,14},{6,15},{7,16},{8,17},{9,1... | collective-permute-start | bytes 983048 | tf_op jit(solution)/shard_map/ppermute | solution.py:19
  1254.1 55.5 %collective-permute-start.112 = (bf16[64,2560]{1,0:T(8,128)(2,1)}, bf16[64,2560]{1,0:T(8,128)(2,1)}, u32[]{:S(2)}, u32[]{:S(2)}) collective-permute-start(bf16[64,2560]{1,0:T(8,128)(2,1)} %get-tuple-element.89), channel_id=1, source_target_pairs={{9,0},{10,1},{11,2},{12,3},{13,4},{14,5},{15,6},{16,7},{17,8},{18,... | collective-permute-start | bytes 983048 | tf_op jit(solution)/shard_map/ppermute | solution.py:19
  1255.4 55.7 %collective-permute-start.111 = (bf16[64,2560]{1,0:T(8,128)(2,1)}, bf16[64,2560]{1,0:T(8,128)(2,1)}, u32[]{:S(2)}, u32[]{:S(2)}) collective-permute-start(bf16[64,2560]{1,0:T(8,128)(2,1)} %get-tuple-element.90), channel_id=1, source_target_pairs={{0,8},{1,9},{2,10},{3,11},{4,12},{5,13},{6,14},{7,15},{8,16},{9,17... | collective-permute-start | bytes 983048 | tf_op jit(solution)/shard_map/ppermute | solution.py:19
  1264.9 47.5 %collective-permute-start.110 = (bf16[64,2560]{1,0:T(8,128)(2,1)}, bf16[64,2560]{1,0:T(8,128)(2,1)}, u32[]{:S(2)}, u32[]{:S(2)}) collective-permute-start(bf16[64,2560]{1,0:T(8,128)(2,1)} %get-tuple-element.91), channel_id=1, source_target_pairs={{8,0},{9,1},{10,2},{11,3},{12,4},{13,5},{14,6},{15,7},{16,8},{17,9... | collective-permute-start | bytes 983048 | tf_op jit(solution)/shard_map/ppermute | solution.py:19
  1266.2 50.9 %collective-permute-start.109 = (bf16[64,2560]{1,0:T(8,128)(2,1)}, bf16[64,2560]{1,0:T(8,128)(2,1)}, u32[]{:S(2)}, u32[]{:S(2)}) collective-permute-start(bf16[64,2560]{1,0:T(8,128)(2,1)} %get-tuple-element.93), channel_id=1, source_target_pairs={{0,7},{1,8},{2,9},{3,10},{4,11},{5,12},{6,13},{7,14},{8,15},{9,16}... | collective-permute-start | bytes 983048 | tf_op jit(solution)/shard_map/ppermute | solution.py:19
  1332.9 42.2 %collective-permute-start.103 = (bf16[64,2560]{1,0:T(8,128)(2,1)S(1)}, bf16[64,2560]{1,0:T(8,128)(2,1)S(1)}, u32[]{:S(2)}, u32[]{:S(2)}) collective-permute-start(bf16[64,2560]{1,0:T(8,128)(2,1)S(1)} %copy-done.79), channel_id=1, source_target_pairs={{0,4},{1,5},{2,6},{3,7},{4,8},{5,9},{6,10},{7,11},{8,12},{9,13},{1... | collective-permute-start | bytes 983048 | tf_op jit(solution)/shard_map/ppermute | solution.py:19
  1339.3 37.1 %collective-permute-start.102 = (bf16[64,2560]{1,0:T(8,128)(2,1)S(1)}, bf16[64,2560]{1,0:T(8,128)(2,1)S(1)}, u32[]{:S(2)}, u32[]{:S(2)}) collective-permute-start(bf16[64,2560]{1,0:T(8,128)(2,1)S(1)} %copy-done.78), channel_id=1, source_target_pairs={{4,0},{5,1},{6,2},{7,3},{8,4},{9,5},{10,6},{11,7},{12,8},{13,9},{1... | collective-permute-start | bytes 983048 | tf_op jit(solution)/shard_map/ppermute | solution.py:19
  1340.6 39.2 %collective-permute-start.101 = (bf16[64,2560]{1,0:T(8,128)(2,1)S(1)}, bf16[64,2560]{1,0:T(8,128)(2,1)S(1)}, u32[]{:S(2)}, u32[]{:S(2)}) collective-permute-start(bf16[64,2560]{1,0:T(8,128)(2,1)S(1)} %copy-done.77), channel_id=1, source_target_pairs={{0,3},{1,4},{2,5},{3,6},{4,7},{5,8},{6,9},{7,10},{8,11},{9,12},{10... | collective-permute-start | bytes 983048 | tf_op jit(solution)/shard_map/ppermute | solution.py:19
  1346.3 49.5 %collective-permute-start.99 = (bf16[64,2560]{1,0:T(8,128)(2,1)S(1)}, bf16[64,2560]{1,0:T(8,128)(2,1)S(1)}, u32[]{:S(2)}, u32[]{:S(2)}) collective-permute-start(bf16[64,2560]{1,0:T(8,128)(2,1)S(1)} %copy-done.75), channel_id=1, source_target_pairs={{0,2},{1,3},{2,4},{3,5},{4,6},{5,7},{6,8},{7,9},{8,10},{9,11},{10,... | collective-permute-start | bytes 983048 | tf_op jit(solution)/shard_map/ppermute | solution.py:19
  1447.3 45.2 %collective-permute-start.83 = (bf16[64,2560]{1,0:T(8,128)(2,1)}, bf16[64,2560]{1,0:T(8,128)(2,1)S(1)}, u32[]{:S(2)}, u32[]{:S(2)}) collective-permute-start(bf16[64,2560]{1,0:T(8,128)(2,1)} %get-tuple-element.118), channel_id=1, source_target_pairs={{0,10},{1,11},{2,12},{3,13},{4,14},{5,15},{6,16},{7,17},{8,18},{9,... | collective-permute-start | bytes 983048 | tf_op jit(solution)/shard_map/ppermute | solution.py:19
  1459.4 48.3 %collective-permute-start.81 = (bf16[64,2560]{1,0:T(8,128)(2,1)}, bf16[64,2560]{1,0:T(8,128)(2,1)S(1)}, u32[]{:S(2)}, u32[]{:S(2)}) collective-permute-start(bf16[64,2560]{1,0:T(8,128)(2,1)} %get-tuple-element.120), channel_id=1, source_target_pairs={{0,9},{1,10},{2,11},{3,12},{4,13},{5,14},{6,15},{7,16},{8,17},{9,1... | collective-permute-start | bytes 983048 | tf_op jit(solution)/shard_map/ppermute | solution.py:19
  1469.7 39.4 %collective-permute-start.80 = (bf16[64,2560]{1,0:T(8,128)(2,1)}, bf16[64,2560]{1,0:T(8,128)(2,1)S(1)}, u32[]{:S(2)}, u32[]{:S(2)}) collective-permute-start(bf16[64,2560]{1,0:T(8,128)(2,1)} %get-tuple-element.121), channel_id=1, source_target_pairs={{9,0},{10,1},{11,2},{12,3},{13,4},{14,5},{15,6},{16,7},{17,8},{18,... | collective-permute-start | bytes 983048 | tf_op jit(solution)/shard_map/ppermute | solution.py:19
  1471.7 43.6 %collective-permute-start.79 = (bf16[64,2560]{1,0:T(8,128)(2,1)}, bf16[64,2560]{1,0:T(8,128)(2,1)S(1)}, u32[]{:S(2)}, u32[]{:S(2)}) collective-permute-start(bf16[64,2560]{1,0:T(8,128)(2,1)} %get-tuple-element.122), channel_id=1, source_target_pairs={{0,8},{1,9},{2,10},{3,11},{4,12},{5,13},{6,14},{7,15},{8,16},{9,17... | collective-permute-start | bytes 983048 | tf_op jit(solution)/shard_map/ppermute | solution.py:19
  1521.9 47.3 %collective-permute-start.71 = (bf16[64,2560]{1,0:T(8,128)(2,1)}, bf16[64,2560]{1,0:T(8,128)(2,1)}, u32[]{:S(2)}, u32[]{:S(2)}) collective-permute-start(bf16[64,2560]{1,0:T(8,128)(2,1)} %get-tuple-element.131), channel_id=1, source_target_pairs={{0,4},{1,5},{2,6},{3,7},{4,8},{5,9},{6,10},{7,11},{8,12},{9,13},{1... | collective-permute-start | bytes 983048 | tf_op jit(solution)/shard_map/ppermute | solution.py:19
  1530.2 40.4 %collective-permute-start.70 = (bf16[64,2560]{1,0:T(8,128)(2,1)}, bf16[64,2560]{1,0:T(8,128)(2,1)}, u32[]{:S(2)}, u32[]{:S(2)}) collective-permute-start(bf16[64,2560]{1,0:T(8,128)(2,1)} %get-tuple-element.132), channel_id=1, source_target_pairs={{4,0},{5,1},{6,2},{7,3},{8,4},{9,5},{10,6},{11,7},{12,8},{13,9},{1... | collective-permute-start | bytes 983048 | tf_op jit(solution)/shard_map/ppermute | solution.py:19
  1532.2 39.7 %collective-permute-start.69 = (bf16[64,2560]{1,0:T(8,128)(2,1)}, bf16[64,2560]{1,0:T(8,128)(2,1)}, u32[]{:S(2)}, u32[]{:S(2)}) collective-permute-start(bf16[64,2560]{1,0:T(8,128)(2,1)} %get-tuple-element.133), channel_id=1, source_target_pairs={{0,3},{1,4},{2,5},{3,6},{4,7},{5,8},{6,9},{7,10},{8,11},{9,12},{10... | collective-permute-start | bytes 983048 | tf_op jit(solution)/shard_map/ppermute | solution.py:19
  1586.2 297.4 %reduce-scatter.11.cloned.1.call-start = ((), (), s32[]{:S(2)}) async-start(), calls=%async_computation.14 | async-start | bytes 6758400 | tf_op jit(solution)/shard_map/reduce_scatter | solution.py:289
  1591.4 570.0 %reduce-scatter.15.cloned.1.call-start = ((), (), s32[]{:S(2)}) async-start(), calls=%async_computation.16 | async-start | bytes 27033600 | tf_op jit(solution)/shard_map/reduce_scatter | solution.py:295
  1620.7 828.8 %reduce-scatter.17.cloned.1.call-start = ((), (), s32[]{:S(2)}) async-start(), calls=%async_computation.17 | async-start | bytes 27033600 | tf_op jit(solution)/shard_map/reduce_scatter | solution.py:297
  (237 other events, 8386.3 us)
Sparse Core Ops, SparseCore 0:
  10.9 62.3 all-gather.6
  76.1 58.1 all-gather.8
  137.1 86.1 all-gather.10
  226.0 85.4 all-gather.12
  314.3 194.6 all-gather.14
  511.7 173.9 all-gather.16
  1070.2 159.5 reduce-scatter.6
  1232.7 183.3 reduce-scatter.12
  1586.3 152.8 reduce-scatter.8
  1741.9 141.5 reduce-scatter.10
  1886.4 274.8 reduce-scatter.14
  2164.1 285.2 reduce-scatter.16
where the time goes:
time: 2480 us; the launch traced here: 2460 us
  waiting for transfers between devices  1240 us (50%)
  starting transfers between devices  490 us (20%)
  matrix products  340 us (14%)
  local copies, waits for them, and re-layouts  202 us (8%)
  blocking collectives  94.4 us (4%)
  other arithmetic  73.8 us (3%)
    ppermute x128, starting transfers between devices, passed_along(): lax.ppermute(value, axis, [(source, source + steps) for source in range(i...  489 us
    ppermute x128, waiting for transfers between devices, passed_along(): lax.ppermute(value, axis, [(source, source + steps) for source in range(i...  386 us
    reduce_scatter x1, waiting for transfers between devices, body(): lax.psum_scatter(sums[13], 'dev', scatter_dimension=0, tiled=True)  288 us
    reduce_scatter x1, waiting for transfers between devices, body(): lax.psum_scatter(sums[11], 'dev', scatter_dimension=0, tiled=True)  278 us
    reduce_scatter x1, waiting for transfers between devices, body(): lax.psum_scatter(sums[5], 'dev', scatter_dimension=0, tiled=True)  144 us
    unnamed x2, blocking collectives  94.4 us
    dot_general x12, matrix products, matmul_tn(): lax.dot_general(a, b, (((0,), (0,)), ((), ())), preferred_element_type=jn...  81.2 us
    unnamed x411, local copies, waits for them, and re-layouts  74.4 us
  transfers between devices with their start and end apart: 140, of which 44 were waited for; matrix products, arithmetic and copies ran while one was open for 20% of the time, Pallas kernels for 0%

commit v1 on v0

v1 whole, which is shorter than its diff:
```python
import functools
import math

import jax
import jax.numpy as jnp
from jax import lax
from jax.experimental import pallas as pl
from jax.experimental.pallas import tpu as pltpu
from jax.sharding import PartitionSpec as P

eps = 1e-05
heads = 16
low = jnp.bfloat16
far = -1e30
lanes = 128
exact = jnp.float32


def layer_norm(v, gain, shift):
    mean = jnp.mean(v, axis=-1, keepdims=True)
    cent = v - mean
    var = jnp.mean(cent * cent, axis=-1, keepdims=True)
    return cent * lax.rsqrt(var + eps) * gain + shift


def norm_back(v, gain, shift, grad):
    value, pull = jax.vjp(layer_norm, v, gain, shift)
    return pull(grad)


def exact_gelu(v):
    return jax.nn.gelu(v, approximate=False)


def dot(a, b, ca, cb):
    return lax.dot_general(a, b, (((ca,), (cb,)), ((), ())), preferred_element_type=exact)


class Layout:
    def __init__(self, micro):
        self.count = lax.axis_size("dev")
        self.half = heads
        self.block = micro * heads
        self.blocks = self.count // self.block
        self.me = lax.axis_index("dev")
        self.rank = self.me % self.block
        self.mine = self.rank // self.half
        self.head = self.rank % self.half
        self.odd = self.rank % 2
        self.halves = [list(range(s, s + self.half)) for s in range(0, self.count, self.half)]
        self.whole = [list(range(s, s + self.block)) for s in range(0, self.count, self.block)]
        self.rows = [list(range(s, s + self.blocks)) for s in range(0, self.count, self.blocks)]
        self.even_first = [(d, self.target(d, d % 2)) for d in range(self.count)]
        self.odd_first = [(d, self.target(d, 1 - d % 2)) for d in range(self.count)]

    def target(self, d, half):
        base, rank = d // self.block * self.block, d % self.block
        return base + half * self.half + rank // 2

    def send(self, value, pairs):
        return lax.ppermute(value, "dev", pairs)

    def swapped(self, value, bit):
        return self.send(value, [(d, d ^ bit) for d in range(self.count)])

    def to_block(self, value):
        if self.blocks == 1:
            return value
        value = lax.all_gather(value, "dev", axis=0, tiled=True, axis_index_groups=self.rows)
        return self.send(value, [(d, d % self.blocks * self.block + d // self.blocks) for d in range(self.count)])

    def from_block(self, value):
        if self.blocks == 1:
            return value
        value = self.send(value, [(d % self.blocks * self.block + d // self.blocks, d) for d in range(self.count)])
        return lax.psum_scatter(value, "dev", scatter_dimension=0, tiled=True, axis_index_groups=self.rows)

    def pair_up(self, for_first, for_second):
        a = self.send(for_first, self.even_first)
        b = self.send(for_second, self.odd_first)
        return jnp.where(self.mine == 0, a, b), jnp.where(self.mine == 0, b, a)

    def pair_up_micro(self, value):
        first = lax.dynamic_index_in_dim(value, self.odd, 0, False)
        second = lax.dynamic_index_in_dim(value, 1 - self.odd, 0, False)
        return self.pair_up(first, second)

    def pair_back(self, value):
        first = lax.dynamic_index_in_dim(value, self.mine, 0, False)
        second = lax.dynamic_index_in_dim(value, 1 - self.mine, 0, False)
        a = self.send(first, [(t, s) for s, t in self.even_first])
        b = self.send(second, [(t, s) for s, t in self.odd_first])
        return jnp.where(self.odd == 0, a, b), jnp.where(self.odd == 0, b, a)

    def gather_half(self, value):
        return lax.all_gather(value, "dev", axis=0, axis_index_groups=self.halves)

    def exchange_half(self, value):
        return lax.all_to_all(value, "dev", 0, 0, tiled=True, axis_index_groups=self.halves)

    def exchange_block(self, value):
        return lax.all_to_all(value, "dev", 0, 0, tiled=True, axis_index_groups=self.whole)

    def bit(self, number):
        return (self.me // number) % 2

    def reduce_half(self, make):
        core = self.bit(1)
        got = self.swapped(make(1 - core).astype(low), 1)
        value = make(core) + got.astype(exact)
        tokens, width = value.shape[1:]
        value = value.reshape(2, 2, 2, tokens, width)
        cut = tokens * 3 // 8 // 8 * 8
        parts = [(0, cut, (8, 4, 2)), (cut, 2 * cut, (4, 2, 8)), (2 * cut, tokens, (2, 8, 4))]
        held = [(value[:, :, :, s:e], [8, 4, 2], order) for s, e, order in parts]
        for stage in range(3):
            after = []
            for piece, axes, order in held:
                bit = order[stage]
                at = axes.index(bit)
                side = self.bit(bit)
                away = lax.dynamic_index_in_dim(piece, 1 - side, at, False).astype(low)
                kept = lax.dynamic_index_in_dim(piece, side, at, False)
                after.append((kept.astype(exact) + self.swapped(away, bit).astype(exact), [x for x in axes if x != bit], order))
            held = after
        return jnp.concatenate([piece for piece, _, _ in held], axis=0)


def attend_kernel(hd, coef, q_ref, k_ref, v_ref, o_ref, lse_ref, vt_ref):
    @pl.when(pl.program_id(0) == 0)
    def _():
        vt_ref[...] = v_ref[...].T

    s = dot(k_ref[...], q_ref[...], 1, 1)
    top = jnp.max(s, axis=0, keepdims=True)
    e = jnp.exp2((s - top) * coef)
    total = jnp.sum(e, axis=0, keepdims=True)
    o = dot(vt_ref[...], e.astype(low), 1, 0) / total
    o = o.astype(low)
    for piece in range(o_ref.shape[0]):
        o_ref[piece] = o[:hd, piece * lanes : (piece + 1) * lanes]
    lse_ref[0] = top * coef + jnp.log2(total)


def attend(q, k, v, hd, rows):
    tokens, keys = q.shape[0], k.shape[0]
    coef = math.log2(math.e) / hd**0.5
    steps = tokens // rows
    return pl.pallas_call(
        functools.partial(attend_kernel, hd, coef),
        grid=(steps,),
        in_specs=[
            pl.BlockSpec((rows, lanes), lambda i: (i, 0)),
            pl.BlockSpec((keys, lanes), lambda i: (0, 0)),
            pl.BlockSpec((keys, lanes), lambda i: (0, 0)),
        ],
        out_specs=[
            pl.BlockSpec((rows // lanes, hd, lanes), lambda i: (i, 0, 0)),
            pl.BlockSpec((1, 1, rows), lambda i: (i, 0, 0)),
        ],
        out_shape=[
            jax.ShapeDtypeStruct((tokens // lanes, hd, lanes), low),
            jax.ShapeDtypeStruct((steps, 1, rows), exact),
        ],
        scratch_shapes=[pltpu.VMEM((lanes, keys), low)],
        compiler_params=pltpu.CompilerParams(vmem_limit_bytes=48 << 20),
        cost_estimate=pl.CostEstimate(flops=4 * tokens * keys * lanes, bytes_accessed=6 * keys * lanes, transcendentals=tokens * keys),
        name="attend",
    )(q, k, v)


def attend_back_kernel(hd, coef, scale, q_ref, k_ref, v_ref, do_ref, lse_ref, dq_ref, dk_ref, dv_ref, kt_ref, dk_sum, dv_sum):
    step = pl.program_id(0)

    @pl.when(step == 0)
    def _():
        kt_ref[...] = k_ref[...].T
        dk_sum[...] = jnp.zeros_like(dk_sum)
        dv_sum[...] = jnp.zeros_like(dv_sum)

    pieces = do_ref.shape[0]
    dot_t = jnp.concatenate([do_ref[piece] for piece in range(pieces)], axis=1)
    fill = jnp.zeros((lanes - hd, dot_t.shape[1]), low)
    dot_t = jnp.concatenate([dot_t, fill], axis=0)
    q = q_ref[...]
    s = dot(k_ref[...], q, 1, 1)
    p = jnp.exp2(s * coef - lse_ref[0])
    dp = dot(v_ref[...], dot_t, 1, 0)
    r = jnp.sum(p * dp, axis=0, keepdims=True)
    ds = (p * (dp - r)).astype(low)
    dv_sum[...] += dot(p.astype(low), dot_t.T, 1, 0)
    dk_sum[...] += dot(ds, q, 1, 0)
    dq = dot(kt_ref[...], ds, 1, 0) * scale
    head = lax.broadcasted_iota(jnp.int32, dq.shape, 0) < hd
    dq_ref[...] = jnp.where(head, dq, 0.0).T.astype(low)

    @pl.when(step == pl.num_programs(0) - 1)
    def _():
        head = lax.broadcasted_iota(jnp.int32, dk_sum.shape, 1) < hd
        dk_ref[...] = jnp.where(head, dk_sum[...] * scale, 0.0).astype(dk_ref.dtype)
        dv_ref[...] = dv_sum[...].astype(dv_ref.dtype)


def attend_back(q, k, v, do, lse, hd, rows, kind):
    tokens, keys = q.shape[0], k.shape[0]
    scale = 1.0 / hd**0.5
    coef = math.log2(math.e) * scale
    steps = tokens // rows
    whole = pl.BlockSpec((keys, lanes), lambda i: (0, 0))
    return pl.pallas_call(
        functools.partial(attend_back_kernel, hd, coef, scale),
        grid=(steps,),
        in_specs=[
            pl.BlockSpec((rows, lanes), lambda i: (i, 0)),
            whole,
            whole,
            pl.BlockSpec((rows // lanes, hd, lanes), lambda i: (i, 0, 0)),
            pl.BlockSpec((1, 1, rows), lambda i: (i, 0, 0)),
        ],
        out_specs=[pl.BlockSpec((rows, lanes), lambda i: (i, 0)), whole, whole],
        out_shape=[
            jax.ShapeDtypeStruct((tokens, lanes), low),
            jax.ShapeDtypeStruct((keys, lanes), kind),
            jax.ShapeDtypeStruct((keys, lanes), kind),
        ],
        scratch_shapes=[
            pltpu.VMEM((lanes, keys), low),
            pltpu.VMEM((keys, lanes), exact),
            pltpu.VMEM((keys, lanes), exact),
        ],
        compiler_params=pltpu.CompilerParams(vmem_limit_bytes=48 << 20),
        cost_estimate=pl.CostEstimate(flops=10 * tokens * keys * lanes, bytes_accessed=10 * keys * lanes, transcendentals=tokens * keys),
        name="attend_back",
    )(q, k, v, do, lse)


def body(
    hidden_in,
    clip_lengths,
    ln1_gain,
    ln1_bias,
    w_query,
    b_query,
    w_key,
    w_value,
    b_value,
    w_out,
    b_out,
    ln2_gain,
    ln2_bias,
    w_fc1,
    b_fc1,
    w_fc2,
    b_fc2,
    cotangent,
):
    micro, rows, width = hidden_in.shape
    at = Layout(micro)
    hd = width // heads
    own = 2 * rows
    tokens = at.half * own
    clips = clip_lengths.shape[1]
    chunk = width // at.block

    vectors = [at.to_block(v) for v in (ln1_gain, ln1_bias, b_query, b_value, b_out, ln2_gain, ln2_bias, b_fc2)]
    ff_bias = at.to_block(b_fc1)
    names = len(vectors)
    small = jnp.concatenate(vectors + [ff_bias])
    row = jnp.pad(small, (0, width - small.shape[0]))[None]
    with_row = jnp.concatenate([hidden_in, jnp.broadcast_to(row, (micro, 1, width))], axis=1)
    x_even, x_odd = at.pair_up_micro(with_row)
    x_own = jnp.concatenate([x_even[:rows], x_odd[:rows]], axis=0)
    packed = jnp.concatenate([x_own, x_even[rows:], x_odd[rows:]], axis=0)
    packed = at.gather_half(packed)
    x_all = packed[:, :own].reshape(tokens, width)
    table = packed[:, own:].reshape(at.block, width)[:, : chunk * names].reshape(at.block, names, chunk)
    g1, b1, bq, bv, bo, g2, b2, bf2 = (table[:, i].reshape(width).astype(exact) for i in range(names))
    ff_rows = ff_bias.shape[0]
    start = chunk * names
    c1 = jnp.concatenate([x_even[rows, start : start + ff_rows], x_odd[rows, start : start + ff_rows]]).astype(exact)

    w_in = jnp.stack([at.to_block(w) for w in (w_query, w_key, w_value)], axis=1)
    w_in = w_in.reshape(chunk, 3, heads, hd).transpose(2, 0, 1, 3).reshape(heads, chunk, 3 * hd)
    w_in = at.exchange_block(jnp.concatenate([w_in] * micro, axis=0)).reshape(width, 3, hd)
    w_in = jnp.pad(w_in, ((0, 0), (0, 0), (0, lanes - hd))).reshape(width, 3 * lanes)
    w1 = at.to_block(w_fc1)
    ff = w1.shape[1] // heads
    w1 = w1.reshape(chunk, heads, ff).transpose(1, 0, 2)
    w1 = at.exchange_block(jnp.concatenate([w1] * micro, axis=0)).reshape(width, ff)
    wo_shard = at.to_block(w_out)
    lower = jnp.concatenate([wo_shard, at.to_block(w_fc2)], axis=0)
    low_even, low_odd = at.pair_up(lower, lower)
    wo_head = jnp.concatenate([low_even[:chunk], low_odd[:chunk]], axis=0)
    w2 = jnp.concatenate([low_even[chunk:], low_odd[chunk:]], axis=0)
    wo = at.gather_half(wo_head).reshape(width, width)
    g_even, g_odd = at.pair_up_micro(cotangent)
    g_own = jnp.concatenate([g_even, g_odd], axis=0)
    g_all = at.gather_half(g_own).reshape(tokens, width)

    lengths = lax.dynamic_index_in_dim(clip_lengths, at.mine, 0, False)
    ends = jnp.cumsum(lengths)
    where_at = at.me // at.block * tokens + jnp.arange(tokens, dtype=jnp.int32)
    ids = jnp.sum((ends[None, :] <= where_at[:, None]).astype(jnp.int32), axis=1)
    column = jnp.arange(lanes, dtype=jnp.int32)[None] - hd
    matches = ids[:, None] == column
    marked = (column >= 0) & (column <= clips)
    q_mark = jnp.where(marked & ~matches, far, 0.0)
    k_mark = jnp.where(marked & matches, 1.0, 0.0)
    marks = jnp.concatenate([q_mark, k_mark, jnp.zeros_like(k_mark)], axis=1)

    a1 = layer_norm(x_all.astype(exact), g1, b1).astype(low)
    bias = jnp.stack([bq, jnp.zeros_like(bq), bv]).reshape(3, heads, hd)
    bias = lax.dynamic_index_in_dim(bias, at.head, 1, False)
    bias = jnp.pad(bias, ((0, 0), (0, lanes - hd))).reshape(3 * lanes)
    qkv = (dot(a1, w_in, 1, 0) + bias + marks).astype(low)
    q, k, v = (qkv[:, i * lanes : (i + 1) * lanes] for i in range(3))
    if at.blocks > 1:
        span = tokens // 2
        ahead = [(d, d + at.block) for d in range(at.count - at.block)]
        behind = [(d + at.block, d) for d in range(at.count - at.block)]
        nothing = jnp.where(column == clips, 1.0, 0.0).astype(low)
        kv = jnp.stack([k, v])
        before = at.send(kv[:, tokens - span :], ahead)
        after = at.send(kv[:, :span], behind)
        is_first = at.me < at.block
        is_last = at.me >= at.count - at.block
        k = jnp.concatenate([jnp.where(is_first, nothing, before[0]), k, jnp.where(is_last, nothing, after[0])], axis=0)
        v = jnp.concatenate([before[1], v, after[1]], axis=0)
    step_rows = 256
    o_head, lse = attend(q, k, v, hd, step_rows)
    o_own = at.exchange_half(o_head).reshape(width, own)

    x2 = x_own.astype(exact) + (dot(o_own, wo, 0, 0) + bo)
    a2_own = layer_norm(x2, g2, b2).astype(low)
    a2 = at.gather_half(a2_own).reshape(tokens, width)
    u = dot(a2, w1, 1, 0) + c1
    hid = exact_gelu(u).astype(low)

    d_hid = dot(g_all, w2, 1, 1)
    du = jax.vjp(exact_gelu, u)[1](d_hid)[0].astype(low)

    def half_terms(left, right, contract):
        split = left.reshape(8, 2, own, left.shape[1])

        def make(part):
            piece = lax.dynamic_index_in_dim(split, part, 1, False).reshape(8 * own, left.shape[1])
            return dot(piece, right, 1, contract).reshape(8, own, width)

        return make

    da2 = at.reduce_half(half_terms(du, w1, 1))
    d_x2n, d_g2, d_b2 = norm_back(x2, g2, b2, da2)
    dx2 = g_own.astype(exact) + d_x2n
    ga_own = dx2.astype(low)
    do_own = dot(wo, ga_own, 1, 1).astype(low).reshape(heads, hd, own)
    do_head = at.exchange_half(do_own)
    ga = at.gather_half(ga_own)

    kind = low if at.blocks == 1 else exact
    dq, dk, dv = attend_back(q, k, v, do_head, lse, hd, step_rows, kind)
    if at.blocks > 1:
        span = tokens // 2
        dkv = jnp.stack([dk, dv])
        to_before = at.send(dkv[:, :span].astype(low), behind).astype(exact)
        to_after = at.send(dkv[:, span + tokens :].astype(low), ahead).astype(exact)
        dkv = dkv[:, span : span + tokens] + jnp.concatenate([to_after, to_before], axis=1)
        dk, dv = dkv[0].astype(low), dkv[1].astype(low)
    dqkv = jnp.concatenate([dq, dk, dv], axis=1)
    da1 = at.reduce_half(half_terms(dqkv, w_in, 1))
    d_xn, d_g1, d_b1 = norm_back(x_own.astype(exact), g1, b1, da1)
    dx = dx2 + d_xn

    y = at.reduce_half(half_terms(hid, w2, 0))
    out = x2 + (y + bf2)

    d_w2 = dot(hid, g_all, 0, 0)
    d_w1 = dot(a2, du, 0, 0)
    d_wo = jnp.einsum("ckt,ctn->kn", o_head, ga, preferred_element_type=exact)
    d_in = dot(a1, dqkv, 0, 0).reshape(width, 3, lanes)[:, :, :hd].reshape(width, 3 * hd)

    back = jnp.concatenate([d_w2.reshape(2, -1, width), d_wo.reshape(2, chunk, width)], axis=1).astype(low)
    first, second = at.pair_back(back)
    total = first.astype(exact) + second.astype(exact)
    grad_w2 = at.from_block(total[:-chunk])
    grad_wo = at.from_block(total[-chunk:])

    wide = jnp.concatenate([d_w1, d_in], axis=1).astype(low).reshape(at.block, chunk, ff + 3 * hd)
    wide = at.exchange_block(wide).astype(exact)
    wide = jnp.sum(wide.reshape(micro, heads, chunk, ff + 3 * hd), axis=0)
    grad_w1 = at.from_block(wide[:, :, :ff].transpose(1, 0, 2).reshape(chunk, heads * ff))
    d_in = wide[:, :, ff:].reshape(heads, chunk, 3, hd).transpose(2, 1, 0, 3).reshape(3, chunk, width)
    grad_wq, grad_wk, grad_wv = (at.from_block(d_in[i]) for i in range(3))

    def spread(value, size):
        zeros = jnp.zeros((heads, size), exact)
        return lax.dynamic_update_index_in_dim(zeros, value, at.head, 0).reshape(heads * size)

    d_bq = spread(jnp.sum(dq[:, :hd].astype(exact), axis=0), hd)
    d_bv = spread(jnp.sum(dv[:, :hd].astype(exact), axis=0), hd)
    d_c1 = spread(jnp.sum(du.astype(exact), axis=0), ff)
    d_bo = jnp.sum(ga_own.astype(exact), axis=0)
    d_bf2 = jnp.sum(g_own.astype(exact), axis=0)
    parts = [d_g1, d_b1, d_bq, d_bv, d_bo, d_g2, d_b2, d_bf2]
    vector = jnp.stack(parts).reshape(names, at.block, chunk).transpose(1, 0, 2).reshape(at.block, names * chunk)
    vector = jnp.concatenate([vector, d_c1.reshape(at.block, ff_rows)], axis=1)
    vector = jnp.sum(at.exchange_block(vector), axis=0)
    pieces = [at.from_block(vector[i * chunk : (i + 1) * chunk]) for i in range(names)]
    grad_g1, grad_b1, grad_bq, grad_bv, grad_bo, grad_g2, grad_b2, grad_bf2 = pieces
    grad_c1 = at.from_block(vector[names * chunk :])

    ends_out = jnp.stack([out, dx], axis=0).astype(low).reshape(2, 2, rows, width).transpose(1, 0, 2, 3)
    first, second = at.pair_back(ends_out)
    layer_out = jnp.stack([first[0], second[0]]).astype(exact)
    input_grad = jnp.stack([first[1], second[1]]).astype(exact)
    return (
        layer_out,
        input_grad,
        grad_g1,
        grad_b1,
        grad_wq,
        grad_bq,
        grad_wk,
        grad_wv,
        grad_bv,
        grad_wo,
        grad_bo,
        grad_g2,
        grad_b2,
        grad_w1,
        grad_c1,
        grad_w2,
        grad_bf2,
    )


def solution(mesh):
    tokens, vector, matrix = P(None, "dev", None), P("dev"), P("dev", None)
    grads = (vector, vector, matrix, vector, matrix, matrix, vector, matrix, vector, vector, vector, matrix, vector, matrix, vector)
    return jax.shard_map(
        body,
        mesh=mesh,
        in_specs=(tokens, P()) + grads + (tokens,),
        out_specs=(tokens, tokens) + grads,
        check_vma=False,
    )
```

time: 2480 us -> 577 us (0.23)
  waiting for transfers between devices: 1240 us -> 203 us
  starting transfers between devices: 490 us -> 113 us
  matrix products: 340 us -> 70.3 us
  local copies, waits for them, and re-layouts: 202 us -> 88.7 us
  blocking collectives: 94.4 us -> 0 us
  Pallas kernels: 0 us -> 27.1 us
    reduce_scatter x6 -> x0, waiting for transfers between devices: 711 us -> none  [the longest x1 288 us: body(): lax.psum_scatter(sums[13], 'dev', scatter_dimension=0, tiled=True)]
    ppermute x128 -> x40, starting transfers between devices: 489 us -> 58.2 us  [send(): return lax.ppermute(value, 'dev', pairs)]
    ppermute x128 -> x40, waiting for transfers between devices: 386 us -> 95 us  [send(): return lax.ppermute(value, 'dev', pairs)]
    dot_general x76 -> x15, matrix products: 313 us -> 70.3 us  [the longest x14 66.7 us: dot(): lax.dot_general(a, b, (((ca,), (cb,)), ((), ())), preferred_element_type=...]
    all_gather x6 -> x5, waiting for transfers between devices: 138 us -> 35.9 us  [gather_half(): return lax.all_gather(value, 'dev', axis=0, axis_index_groups=self.halves)]
    unnamed x2 -> x0, blocking collectives: 94.4 us -> none
    all_to_all x0 -> x6, waiting for transfers between devices: none -> 72.2 us  [the longest x4 59.4 us: exchange_block(): lax.all_to_all(value, 'dev', 0, 0, tiled=True, axis_index_groups=self.whole)]
    unnamed x411 -> x137, local copies, waits for them, and re-layouts: 74.4 us -> 7.19 us
  transfers between devices with their start and end apart: 140 -> 51, of which waited for: 44 -> 31; matrix products, arithmetic and copies ran while one was open for 20% -> 28% of each run, Pallas kernels for 0% -> 2%
where the time goes in v1:
time: 577 us; the launch traced here: 570 us
  waiting for transfers between devices  203 us (35%)
  starting transfers between devices  113 us (20%)
  local copies, waits for them, and re-layouts  88.7 us (15%)
  matrix products  70.3 us (12%)
  other arithmetic  51.8 us (9%)
  Pallas kernels  27.1 us (5%)
  between operations  15.8 us (3%)
    ppermute x40, waiting for transfers between devices, send(): return lax.ppermute(value, 'dev', pairs)  95 us
    dot_general x14, matrix products, dot(): lax.dot_general(a, b, (((ca,), (cb,)), ((), ())), preferred_element_type=...  66.7 us
    all_to_all x4, waiting for transfers between devices, exchange_block(): lax.all_to_all(value, 'dev', 0, 0, tiled=True, axis_index_groups=self.whole)  59.4 us
    ppermute x40, starting transfers between devices, send(): return lax.ppermute(value, 'dev', pairs)  58.2 us
    all_to_all x4, starting transfers between devices, exchange_block(): lax.all_to_all(value, 'dev', 0, 0, tiled=True, axis_index_groups=self.whole)  47.8 us
    all_gather x5, waiting for transfers between devices, gather_half(): return lax.all_gather(value, 'dev', axis=0, axis_index_groups=self.halves)  35.9 us
    pallas_call x1, Pallas kernels, attend_back(): pl.pallas_call(functools.partial(attend_back_kernel, hd, coef, scale), gr...  15.9 us
    all_to_all x2, waiting for transfers between devices, exchange_half(): lax.all_to_all(value, 'dev', 0, 0, tiled=True, axis_index_groups=self.hal...  12.8 us
  transfers between devices with their start and end apart: 51, of which 31 were waited for; matrix products, arithmetic and copies ran while one was open for 28% of the time, Pallas kernels for 2%

profile of v1, /device:TPU:0, one launch (start us, length us, event | category | flops | bytes accessed | tf_op | source)
XLA Modules:
  0.0 570.2 jit_solution(9033298067234965404)
XLA Ops:
  7.3 6.2 %concatenate.76 = bf16[480]{0:T(512)(128)(2,1)S(1)} concatenate(bf16[40]{0:T(256)(128)(2,1)} %param.20, bf16[40]{0:T(256)(128)(2,1)} %param.21, bf16[40]{0:T(256)(128)(2,1)} %param.23, bf16[40]{0:T(256)(128)(2,1)} %param.26, bf16[40]{0:T(256)(128)(2,1)} %param.28, bf16[40]{0:T(256)(128)(2,1)} %param.29, bf16[40]{0:T(256)(128)(2,1)} %param.30, bf16[40]{0:T(256)(128)(2,1)} %param.34, ...), dimensions={0} | concatenate | bytes 1920 | tf_op jit(solution)/shard_map/concatenate | solution.py:268
  15.4 5.8 %collective-permute-start.1 = (bf16[65,1280]{1,0:T(8,128)(2,1)S(1)}, bf16[65,1280]{1,0:T(8,128)(2,1)S(1)}, u32[]{:S(2)}, u32[]{:S(2)}) collective-permute-start(bf16[65,1280]{1,0:T(8,128)(2,1)S(1)} %get-tuple-element.87), channel_id=1, source_target_pairs={{0,16},{1,0},{2,17},{3,1},{4,18},{5,2},{6,19},{7,3},{8,20},{9,4},{... | collective-permute-start | bytes 499208 | tf_op jit(solution)/shard_map/ppermute | solution.py:61
  21.2 4.0 collective-permute-done.1
  28.3 3.4 collective-permute-start.3
  31.7 5.3 collective-permute-start.2
  40.2 3.1 collective-permute-done.3
  47.1 31.1 %all-to-all-start = ((bf16[32,40,240]{2,1,0:T(8,128)(2,1)}), bf16[32,40,240]{2,1,0:T(8,128)(2,1)S(1)}, u32[]{:S(2)}, u32[]{:S(2)}) async-start(bf16[32,40,240]{2,1,0:T(8,128)(2,1)} %pad_maximum_fusion.3), calls=%async_computation | async-start | bytes 1310720 | tf_op jit(solution)/shard_map/all_to_all | solution.py:102
  80.4 18.6 %all-to-all-done = bf16[32,40,240]{2,1,0:T(8,128)(2,1)S(1)} async-done(((bf16[32,40,240]{2,1,0:T(8,128)(2,1)}), bf16[32,40,240]{2,1,0:T(8,128)(2,1)S(1)}, u32[]{:S(2)}, u32[]{:S(2)}) %all-to-all-start) | async-done | bytes 614432 | tf_op jit(solution)/shard_map/all_to_all | solution.py:102
  105.6 3.4 convert_reduce_fusion
  109.0 4.0 fusion.2
  115.4 3.0 fusion.8
  118.7 11.1 %attend.1 = (bf16[16,80,128]{2,1,0:T(8,128)(2,1)}, f32[8,1,256]{2,1,0:T(1,128)S(1)}) custom-call(bf16[2048,128]{1,0:T(8,128)(2,1)S(1)} %get-tuple-element.67.q_ref, bf16[2048,128]{1,0:T(8,128)(2,1)S(1)} %get-tuple-element.66.k_ref, bf16[2048,128]{1,0:T(8,128)(2,1)S(1)} %get-tuple-element.65.v_ref), custom_call_target="tpu_custom_call" | custom-call | flops 2147483648 | bytes 1572864 | tf_op jit(solution)/shard_map/attend/pallas_call | solution.py:149
  129.8 3.5 all-to-all-start.1
  133.7 2.8 all-gather.12.cloned.1.call-done
  136.5 5.3 all-to-all-done.1
  141.8 2.7 fusion.154
  146.5 3.7 collective-permute-start.15
  150.2 5.5 collective-permute-done.15
  158.8 7.2 %all-to-all-start.2 = ((bf16[32,40,320]{2,1,0:T(8,128)(2,1)}), bf16[32,40,320]{2,1,0:T(8,128)(2,1)S(1)}, u32[]{:S(2)}, u32[]{:S(2)}) async-start(bf16[32,40,320]{2,1,0:T(8,128)(2,1)} %pad_maximum_fusion.1), calls=%async_computation.2 | async-start | bytes 1966080 | tf_op jit(solution)/shard_map/all_to_all | solution.py:102
  170.5 24.2 %all-to-all-done.2 = bf16[32,40,320]{2,1,0:T(8,128)(2,1)S(1)} async-done(((bf16[32,40,320]{2,1,0:T(8,128)(2,1)}), bf16[32,40,320]{2,1,0:T(8,128)(2,1)S(1)}, u32[]{:S(2)}, u32[]{:S(2)}) %all-to-all-start.2) | async-done | bytes 819232 | tf_op jit(solution)/shard_map/all_to_all | solution.py:102
  194.7 6.3 %all-gather.14.cloned.1.call-done = bf16[2048,1280]{1,0:T(8,128)(2,1)} async-done(((bf16[128,1280]{1,0:T(8,128)(2,1)}), bf16[2048,1280]{1,0:T(8,128)(2,1)}) %all-gather.14.cloned.1.call-update) | async-done | bytes 5242896 | tf_op jit(solution)/shard_map/all_gather | solution.py:96
  201.0 11.0 %multiply_convert_fusion = (bf16[2048,320]{0,1:T(8,128)(2,1)}, f32[2048,320]{0,1:T(8,128)}, f32[2048,320]{0,1:T(8,128)}) fusion(f32[320]{0:T(512)S(1)} %maximum_convert_fusion.2, bf16[2048,1280]{1,0:T(8,128)(2,1)} %all-gather.14.cloned.1.call-done, bf16[1280,320]{1,0:T(8,128)(2,1)S(1)} %bitcast.361), kind=kOutput, calls=%fused_computation.46 | convolution fusion | flops 1720975360 | bytes 12616960 | tf_op jit(solution)/shard_map/dot_general | solution.py:36
  212.0 24.8 %all-gather.16.cloned.1.call-done = bf16[2048,1280]{1,0:T(8,128)(2,1)} async-done(((bf16[128,1280]{1,0:T(8,128)(2,1)}), bf16[2048,1280]{1,0:T(8,128)(2,1)}) %all-gather.16.cloned.1.call-update) | async-done | bytes 5242896 | tf_op jit(solution)/shard_map/all_gather | solution.py:96
  236.8 8.4 %convert_reduce_fusion.2 = (f32[320]{0:T(512)}, bf16[2048,320]{0,1:T(8,128)(2,1)}) fusion(f32[2048,320]{0,1:T(8,128)} %get-tuple-element.58, f32[2048,320]{0,1:T(8,128)} %get-tuple-element.109, bf16[2048,1280]{1,0:T(8,128)(2,1)} %all-gather.16.cloned.1.call-done, bf16[160,1280]{1,0:T(8,128)(2,1)} %slice.250, bf16[160,1280]{1,0:T(8,128)(2,1)} %slice.249), kind=kOutput, calls=%fused_computation.44 | convolution fusion | flops 1689845504 | bytes 12616960 | tf_op jit(solution)/shard_map/dot_general | solution.py:36
  245.2 3.6 reshape.553
  248.8 3.8 constant_dynamic-slice_fusion.5
  252.6 3.2 convolution_convert_fusion.1
  256.0 3.7 reshape.550
  259.7 3.8 constant_dynamic-slice_fusion.9
  263.5 3.1 convolution_convert_fusion.2
  267.0 3.9 convert_add_fusion.1
  272.5 3.4 convert_add_fusion.2
  281.5 5.5 collective-permute-done.23
  287.6 5.8 %collective-permute-done.11 = bf16[2,2,32,1280]{3,2,1,0:T(8,128)(2,1)S(1)} collective-permute-done((bf16[2,2,32,1280]{3,2,1,0:T(8,128)(2,1)S(1)}, bf16[2,2,32,1280]{3,2,1,0:T(8,128)(2,1)S(1)}, u32[]{:S(2)}, u32[]{:S(2)}) %collective-permute-start.11) | collective-permute-done | bytes 327712 | tf_op jit(solution)/shard_map/ppermute | solution.py:61
  293.9 11.2 %collective-permute-done.24 = bf16[2,32,1280]{2,1,0:T(8,128)(2,1)S(1)} collective-permute-done((bf16[2,32,1280]{2,1,0:T(8,128)(2,1)S(1)}, bf16[2,32,1280]{2,1,0:T(8,128)(2,1)S(1)}, u32[]{:S(2)}, u32[]{:S(2)}) %collective-permute-start.24) | collective-permute-done | bytes 163872 | tf_op jit(solution)/shard_map/ppermute | solution.py:61
  306.1 4.4 collective-permute-done.12
  333.0 3.8 convolution_convert_fusion.3
  336.8 3.6 all-to-all-start.3
  341.4 7.5 %all-to-all-done.3.do_ref = bf16[16,80,128]{2,1,0:T(8,128)(2,1)S(1)} async-done(((bf16[16,80,128]{2,1,0:T(8,128)(2,1)}), bf16[16,80,128]{2,1,0:T(8,128)(2,1)S(1)}, u32[]{:S(2)}, u32[]{:S(2)}) %all-to-all-start.3) | async-done | bytes 327712 | tf_op jit(solution)/shard_map/all_to_all | solution.py:99
  348.9 15.9 %attend_back.1 = (bf16[2048,128]{1,0:T(8,128)(2,1)S(1)}, bf16[2048,128]{1,0:T(8,128)(2,1)S(1)}, bf16[2048,128]{1,0:T(8,128)(2,1)S(1)}) custom-call(bf16[2048,128]{1,0:T(8,128)(2,1)S(1)} %get-tuple-element.67.q_ref, bf16[2048,128]{1,0:T(8,128)(2,1)S(1)} %get-tuple-element.66.k_ref, bf16[2048,128]{1,0:T(8,128)(2,1)S(1)} %get-tuple-element.65.v_ref, ...), custom_call_target="tpu_custom_call" | custom-call | flops 5368709120 | bytes 2621440 | tf_op jit(solution)/shard_map/attend_back/pallas_call | solution.py:210
  366.0 3.0 convolution_convert_fusion
  369.0 6.4 %fusion.15 = bf16[320,2048]{1,0:T(8,128)(2,1)} fusion(f32[2048,320]{0,1:T(8,128)S(1)} %copy-done.29), kind=kLoop, calls=%fused_computation.26 | loop fusion | flops 42598400 | bytes 3932160 | tf_op jit(solution)/shard_map/convert_element_type | solution.py:337
  375.4 8.0 %copy.140 = bf16[1280,2048]{1,0:T(8,128)(2,1)} copy(bf16[1280,2048]{0,1:T(8,128)(2,1)} %bitcast.354) | data formatting | bytes 10485760 | tf_op jit(solution)/shard_map/dot_general | solution.py:36
  384.2 6.8 %convolution_convert_fusion.4 = bf16[32,40,320]{2,1,0:T(8,128)(2,1)} fusion(bf16[32,40,2048]{2,1,0:T(8,128)(2,1)} %bitcast.356, bf16[2048,320]{0,1:T(8,128)(2,1)} %get-tuple-element.111), kind=kOutput, calls=%fused_computation.68 | convolution fusion | flops 1678131200 | bytes 7372800 | tf_op jit(solution)/shard_map/dot_general | solution.py:36
  393.0 5.2 fusion.155
  399.0 3.3 copy.142
  402.3 3.5 concatenate.95
  405.8 3.1 pad_maximum_fusion
  408.9 3.4 all-to-all-start.5
  412.3 5.6 fusion.9
  422.8 3.6 convert_add_fusion
  434.0 16.6 %all-to-all-done.5 = bf16[32,40,560]{2,1,0:T(8,128)(2,1)} async-done(((bf16[32,40,560]{2,1,0:T(8,128)(2,1)}), bf16[32,40,560]{2,1,0:T(8,128)(2,1)}, u32[]{:S(2)}, u32[]{:S(2)}) %all-to-all-start.5) | async-done | bytes 1433632 | tf_op jit(solution)/shard_map/all_to_all | solution.py:102
  453.6 2.6 reshape.562
  457.5 2.6 collective-permute-start.34
  460.1 4.2 fusion.150
  464.2 8.3 %collective-permute-done.34 = bf16[2,32,1280]{2,1,0:T(8,128)(2,1)S(1)} collective-permute-done((bf16[2,32,1280]{2,1,0:T(8,128)(2,1)S(1)}, bf16[2,32,1280]{2,1,0:T(8,128)(2,1)S(1)}, u32[]{:S(2)}, u32[]{:S(2)}) %collective-permute-start.34) | collective-permute-done | bytes 163872 | tf_op jit(solution)/shard_map/ppermute | solution.py:61
  472.6 2.8 collective-permute-start.35
  478.6 5.6 collective-permute-done.31
  500.8 6.1 %all-to-all-start.4 = ((f32[32,1,480]{2,1,0:T(1,128)}), f32[32,1,480]{2,1,0:T(1,128)}, u32[]{:S(2)}, u32[]{:S(2)}) async-start(f32[32,1,480]{2,1,0:T(1,128)} %copy.139), calls=%async_computation.4 | async-start | bytes 131072 | tf_op jit(solution)/shard_map/all_to_all | solution.py:102
  510.0 3.9 collective-permute-start.36
  521.2 8.8 %collective-permute-done.37 = bf16[2,64,1280]{2,1,0:T(8,128)(2,1)} collective-permute-done((bf16[2,64,1280]{2,1,0:T(8,128)(2,1)}, bf16[2,64,1280]{2,1,0:T(8,128)(2,1)}, u32[]{:S(2)}, u32[]{:S(2)}) %collective-permute-start.37) | collective-permute-done | bytes 327712 | tf_op jit(solution)/shard_map/ppermute | solution.py:61
  531.2 3.7 fusion.37
  535.7 3.3 collective-permute-start.39
  540.9 20.8 %collective-permute-done.39 = bf16[200,1280]{1,0:T(8,128)(2,1)S(1)} collective-permute-done((bf16[200,1280]{1,0:T(8,128)(2,1)S(1)}, bf16[200,1280]{1,0:T(8,128)(2,1)S(1)}, u32[]{:S(2)}, u32[]{:S(2)}) %collective-permute-start.39) | collective-permute-done | bytes 512032 | tf_op jit(solution)/shard_map/ppermute | solution.py:61
  (404 shorter events, 122.9 us)
Async XLA Ops:
  7.2 71.1 %copy-start = (s32[2,3]{1,0:T(2,128)S(1)}, s32[2,3]{1,0:T(2,128)}, u32[]{:S(2)}) copy-start(s32[2,3]{1,0:T(2,128)} %param.19) | copy-start | bytes 76
  7.2 29.8 %copy-start.50 = (bf16[40,1280]{1,0:T(8,128)(2,1)S(1)}, bf16[40,1280]{1,0:T(8,128)(2,1)}, u32[]{:S(2)}) copy-start(bf16[40,1280]{1,0:T(8,128)(2,1)} %param.22) | copy-start | bytes 307204
  7.2 30.3 %copy-start.51 = (bf16[40,1280]{1,0:T(8,128)(2,1)S(1)}, bf16[40,1280]{1,0:T(8,128)(2,1)}, u32[]{:S(2)}) copy-start(bf16[40,1280]{1,0:T(8,128)(2,1)} %param.24) | copy-start | bytes 307204
  7.3 96.0 %all-gather.20.cloned.1.call-start = ((), (), s32[]{:S(2)}) async-start(), calls=%async_computation.10 | async-start | bytes 5918720 | tf_op jit(solution)/shard_map/all_gather | solution.py:96
  14.6 23.4 %copy-start.52 = (bf16[40,1280]{1,0:T(8,128)(2,1)S(1)}, bf16[40,1280]{1,0:T(8,128)(2,1)}, u32[]{:S(2)}) copy-start(bf16[40,1280]{1,0:T(8,128)(2,1)} %param.25) | copy-start | bytes 307204
  14.6 6.6 %collective-permute-start = (bf16[65,1280]{1,0:T(8,128)(2,1)S(1)}, bf16[65,1280]{1,0:T(8,128)(2,1)S(1)}, u32[]{:S(2)}, u32[]{:S(2)}) collective-permute-start(bf16[65,1280]{1,0:T(8,128)(2,1)S(1)} %get-tuple-element.86), channel_id=1, source_target_pairs={{0,0},{1,16},{2,1},{3,17},{4,2},{5,18},{6,3},{7,19},{8,4},{9,20},{... | collective-permute-start | bytes 499208 | tf_op jit(solution)/shard_map/ppermute | solution.py:61
  15.4 9.8 %collective-permute-start.1 = (bf16[65,1280]{1,0:T(8,128)(2,1)S(1)}, bf16[65,1280]{1,0:T(8,128)(2,1)S(1)}, u32[]{:S(2)}, u32[]{:S(2)}) collective-permute-start(bf16[65,1280]{1,0:T(8,128)(2,1)S(1)} %get-tuple-element.87), channel_id=1, source_target_pairs={{0,16},{1,0},{2,17},{3,1},{4,18},{5,2},{6,19},{7,3},{8,20},{9,4},{... | collective-permute-start | bytes 499208 | tf_op jit(solution)/shard_map/ppermute | solution.py:61
  25.3 116.5 %copy-start.2 = (bf16[64,1280]{1,0:T(8,128)(2,1)}, bf16[64,1280]{1,0:T(8,128)(2,1)S(1)}, u32[]{:S(2)}) copy-start(bf16[64,1280]{1,0:T(8,128)(2,1)S(1)} %slice.228) | copy-start | bytes 491524
  26.0 115.8 %copy-start.4 = (bf16[64,1280]{1,0:T(8,128)(2,1)}, bf16[64,1280]{1,0:T(8,128)(2,1)S(1)}, u32[]{:S(2)}) copy-start(bf16[64,1280]{1,0:T(8,128)(2,1)S(1)} %slice.229) | copy-start | bytes 491524
  26.8 109.7 %all-gather.12.cloned.1.call-start = ((), (), s32[]{:S(2)}) async-start(), calls=%async_computation.6 | async-start | bytes 3481600 | tf_op jit(solution)/shard_map/all_gather | solution.py:96
  28.3 15.1 %collective-permute-start.3 = (bf16[200,1280]{1,0:T(8,128)(2,1)}, bf16[200,1280]{1,0:T(8,128)(2,1)S(1)}, u32[]{:S(2)}, u32[]{:S(2)}) collective-permute-start(bf16[200,1280]{1,0:T(8,128)(2,1)} %constant_dynamic-update-slice_fusion), channel_id=1, source_target_pairs={{0,16},{1,0},{2,17},{3,1},{4,18},{5,2},{6,19},{7,3},{8,20},{9,4},{... | collective-permute-start | bytes 1536008 | tf_op jit(solution)/shard_map/ppermute | solution.py:61
  31.7 11.6 %collective-permute-start.2 = (bf16[200,1280]{1,0:T(8,128)(2,1)}, bf16[200,1280]{1,0:T(8,128)(2,1)}, u32[]{:S(2)}, u32[]{:S(2)}) collective-permute-start(bf16[200,1280]{1,0:T(8,128)(2,1)} %constant_dynamic-update-slice_fusion), channel_id=1, source_target_pairs={{0,0},{1,16},{2,1},{3,17},{4,2},{5,18},{6,3},{7,19},{8,4},{9,20},{... | collective-permute-start | bytes 1536008 | tf_op jit(solution)/shard_map/ppermute | solution.py:61
  47.1 51.9 %all-to-all-start = ((bf16[32,40,240]{2,1,0:T(8,128)(2,1)}), bf16[32,40,240]{2,1,0:T(8,128)(2,1)S(1)}, u32[]{:S(2)}, u32[]{:S(2)}) async-start(bf16[32,40,240]{2,1,0:T(8,128)(2,1)} %pad_maximum_fusion.3), calls=%async_computation | async-start | bytes 1310720 | tf_op jit(solution)/shard_map/all_to_all | solution.py:102
  129.8 12.0 %all-to-all-start.1 = ((bf16[16,80,128]{2,1,0:T(8,128)(2,1)}), bf16[16,80,128]{2,1,0:T(8,128)(2,1)S(1)}, u32[]{:S(2)}, u32[]{:S(2)}) async-start(bf16[16,80,128]{2,1,0:T(8,128)(2,1)} %get-tuple-element.22), calls=%async_computation.1 | async-start | bytes 655360 | tf_op jit(solution)/shard_map/all_to_all | solution.py:99
  133.4 67.6 %all-gather.14.cloned.1.call-start = ((), (), s32[]{:S(2)}) async-start(), calls=%async_computation.7 | async-start | bytes 5570560 | tf_op jit(solution)/shard_map/all_gather | solution.py:96
  145.7 91.1 %all-gather.16.cloned.1.call-start = ((), (), s32[]{:S(2)}) async-start(), calls=%async_computation.8 | async-start | bytes 5570560 | tf_op jit(solution)/shard_map/all_gather | solution.py:96
  145.8 4.4 collective-permute-start.14
  146.5 9.2 %collective-permute-start.15 = (bf16[64,1280]{1,0:T(8,128)(2,1)S(1)}, bf16[64,1280]{1,0:T(8,128)(2,1)S(1)}, u32[]{:S(2)}, u32[]{:S(2)}) collective-permute-start(bf16[64,1280]{1,0:T(8,128)(2,1)S(1)} %get-tuple-element.96), channel_id=1, source_target_pairs={{0,16},{1,0},{2,17},{3,1},{4,18},{5,2},{6,19},{7,3},{8,20},{9,4},{... | collective-permute-start | bytes 491528 | tf_op jit(solution)/shard_map/ppermute | solution.py:61
  158.8 35.8 %all-to-all-start.2 = ((bf16[32,40,320]{2,1,0:T(8,128)(2,1)}), bf16[32,40,320]{2,1,0:T(8,128)(2,1)S(1)}, u32[]{:S(2)}, u32[]{:S(2)}) async-start(bf16[32,40,320]{2,1,0:T(8,128)(2,1)} %pad_maximum_fusion.1), calls=%async_computation.2 | async-start | bytes 1966080 | tf_op jit(solution)/shard_map/all_to_all | solution.py:102
  255.7 11.2 %collective-permute-start.16 = (bf16[8,128,1280]{2,1,0:T(8,128)(2,1)}, bf16[8,128,1280]{2,1,0:T(8,128)(2,1)}, u32[]{:S(2)}, u32[]{:S(2)}) collective-permute-start(bf16[8,128,1280]{2,1,0:T(8,128)(2,1)} %convolution_convert_fusion.1), channel_id=1, source_target_pairs={{0,1},{1,0},{2,3},{3,2},{4,5},{5,4},{6,7},{7,6},{8,9},{9,8},{10,11... | collective-permute-start | bytes 7864328 | tf_op jit(solution)/shard_map/ppermute | solution.py:61
  266.6 5.3 collective-permute-start.4
  276.4 10.6 %collective-permute-start.23 = (bf16[2,2,32,1280]{3,2,1,0:T(8,128)(2,1)S(1)}, bf16[2,2,32,1280]{3,2,1,0:T(8,128)(2,1)S(1)}, u32[]{:S(2)}, u32[]{:S(2)}) collective-permute-start(bf16[2,2,32,1280]{3,2,1,0:T(8,128)(2,1)S(1)} %fusion.89), channel_id=1, source_target_pairs={{0,2},{1,3},{2,0},{3,1},{4,6},{5,7},{6,4},{7,5},{8,10},{9,11},{10,... | collective-permute-start | bytes 983048 | tf_op jit(solution)/shard_map/ppermute | solution.py:61
  277.1 34.4 %collective-permute-start.20 = (bf16[2,2,48,1280]{3,2,0,1:T(8,128)(2,1)S(1)}, bf16[2,2,48,1280]{3,2,0,1:T(8,128)(2,1)S(1)}, u32[]{:S(2)}, u32[]{:S(2)}) collective-permute-start(bf16[2,2,48,1280]{3,2,0,1:T(8,128)(2,1)S(1)} %fusion.86), channel_id=1, source_target_pairs={{0,4},{1,5},{2,6},{3,7},{4,0},{5,1},{6,2},{7,3},{8,12},{9,13},{10,... | collective-permute-start | bytes 1474568 | tf_op jit(solution)/shard_map/ppermute | solution.py:61
  278.2 34.6 %collective-permute-start.17 = (bf16[2,2,48,1280]{3,2,1,0:T(8,128)(2,1)S(1)}, bf16[2,2,48,1280]{3,2,1,0:T(8,128)(2,1)S(1)}, u32[]{:S(2)}, u32[]{:S(2)}) collective-permute-start(bf16[2,2,48,1280]{3,2,1,0:T(8,128)(2,1)S(1)} %fusion.83), channel_id=1, source_target_pairs={{0,8},{1,9},{2,10},{3,11},{4,12},{5,13},{6,14},{7,15},{8,0},{9,1},... | collective-permute-start | bytes 1474568 | tf_op jit(solution)/shard_map/ppermute | solution.py:61
  279.2 14.1 %collective-permute-start.11 = (bf16[2,2,32,1280]{3,2,1,0:T(8,128)(2,1)S(1)}, bf16[2,2,32,1280]{3,2,1,0:T(8,128)(2,1)S(1)}, u32[]{:S(2)}, u32[]{:S(2)}) collective-permute-start(bf16[2,2,32,1280]{3,2,1,0:T(8,128)(2,1)S(1)} %fusion.90), channel_id=1, source_target_pairs={{0,2},{1,3},{2,0},{3,1},{4,6},{5,7},{6,4},{7,5},{8,10},{9,11},{10,... | collective-permute-start | bytes 983048 | tf_op jit(solution)/shard_map/ppermute | solution.py:61
  280.6 33.3 %collective-permute-start.8 = (bf16[2,2,48,1280]{3,2,0,1:T(8,128)(2,1)S(1)}, bf16[2,2,48,1280]{3,2,0,1:T(8,128)(2,1)S(1)}, u32[]{:S(2)}, u32[]{:S(2)}) collective-permute-start(bf16[2,2,48,1280]{3,2,0,1:T(8,128)(2,1)S(1)} %fusion.85), channel_id=1, source_target_pairs={{0,4},{1,5},{2,6},{3,7},{4,0},{5,1},{6,2},{7,3},{8,12},{9,13},{10,... | collective-permute-start | bytes 1474568 | tf_op jit(solution)/shard_map/ppermute | solution.py:61
  287.0 28.6 %collective-permute-start.5 = (bf16[2,2,48,1280]{3,2,1,0:T(8,128)(2,1)S(1)}, bf16[2,2,48,1280]{3,2,1,0:T(8,128)(2,1)S(1)}, u32[]{:S(2)}, u32[]{:S(2)}) collective-permute-start(bf16[2,2,48,1280]{3,2,1,0:T(8,128)(2,1)S(1)} %fusion.82), channel_id=1, source_target_pairs={{0,8},{1,9},{2,10},{3,11},{4,12},{5,13},{6,14},{7,15},{8,0},{9,1},... | collective-permute-start | bytes 1474568 | tf_op jit(solution)/shard_map/ppermute | solution.py:61
  293.4 11.8 %collective-permute-start.24 = (bf16[2,32,1280]{2,1,0:T(8,128)(2,1)S(1)}, bf16[2,32,1280]{2,1,0:T(8,128)(2,1)S(1)}, u32[]{:S(2)}, u32[]{:S(2)}) collective-permute-start(bf16[2,32,1280]{2,1,0:T(8,128)(2,1)S(1)} %fusion.108), channel_id=1, source_target_pairs={{0,8},{1,9},{2,10},{3,11},{4,12},{5,13},{6,14},{7,15},{8,0},{9,1},... | collective-permute-start | bytes 491528 | tf_op jit(solution)/shard_map/ppermute | solution.py:61
  305.1 5.3 collective-permute-start.12
  310.5 8.2 %collective-permute-start.25 = (bf16[32,1280]{1,0:T(8,128)(2,1)S(1)}, bf16[32,1280]{1,0:T(8,128)(2,1)S(1)}, u32[]{:S(2)}, u32[]{:S(2)}) collective-permute-start(bf16[32,1280]{1,0:T(8,128)(2,1)S(1)} %fusion.117), channel_id=1, source_target_pairs={{0,4},{1,5},{2,6},{3,7},{4,0},{5,1},{6,2},{7,3},{8,12},{9,13},{10,... | collective-permute-start | bytes 245768 | tf_op jit(solution)/shard_map/ppermute | solution.py:61
  311.6 5.9 %collective-permute-start.13 = (bf16[32,1280]{1,0:T(8,128)(2,1)S(1)}, bf16[32,1280]{1,0:T(8,128)(2,1)S(1)}, u32[]{:S(2)}, u32[]{:S(2)}) collective-permute-start(bf16[32,1280]{1,0:T(8,128)(2,1)S(1)} %fusion.116), channel_id=1, source_target_pairs={{0,4},{1,5},{2,6},{3,7},{4,0},{5,1},{6,2},{7,3},{8,12},{9,13},{10,... | collective-permute-start | bytes 245768 | tf_op jit(solution)/shard_map/ppermute | solution.py:61
  312.8 7.7 %collective-permute-start.21 = (bf16[2,48,1280]{2,1,0:T(8,128)(2,1)S(1)}, bf16[2,48,1280]{2,1,0:T(8,128)(2,1)S(1)}, u32[]{:S(2)}, u32[]{:S(2)}) collective-permute-start(bf16[2,48,1280]{2,1,0:T(8,128)(2,1)S(1)} %fusion.99), channel_id=1, source_target_pairs={{0,2},{1,3},{2,0},{3,1},{4,6},{5,7},{6,4},{7,5},{8,10},{9,11},{10,... | collective-permute-start | bytes 737288 | tf_op jit(solution)/shard_map/ppermute | solution.py:61
  313.9 9.0 %collective-permute-start.18 = (bf16[2,48,1280]{2,1,0:T(8,128)(2,1)S(1)}, bf16[2,48,1280]{2,1,0:T(8,128)(2,1)S(1)}, u32[]{:S(2)}, u32[]{:S(2)}) collective-permute-start(bf16[2,48,1280]{2,1,0:T(8,128)(2,1)S(1)} %fusion.98), channel_id=1, source_target_pairs={{0,4},{1,5},{2,6},{3,7},{4,0},{5,1},{6,2},{7,3},{8,12},{9,13},{10,... | collective-permute-start | bytes 737288 | tf_op jit(solution)/shard_map/ppermute | solution.py:61
  315.7 8.7 %collective-permute-start.9 = (bf16[2,48,1280]{2,1,0:T(8,128)(2,1)S(1)}, bf16[2,48,1280]{2,1,0:T(8,128)(2,1)S(1)}, u32[]{:S(2)}, u32[]{:S(2)}) collective-permute-start(bf16[2,48,1280]{2,1,0:T(8,128)(2,1)S(1)} %fusion.97), channel_id=1, source_target_pairs={{0,2},{1,3},{2,0},{3,1},{4,6},{5,7},{6,4},{7,5},{8,10},{9,11},{10,... | collective-permute-start | bytes 737288 | tf_op jit(solution)/shard_map/ppermute | solution.py:61
  317.5 8.2 %collective-permute-start.6 = (bf16[2,48,1280]{2,1,0:T(8,128)(2,1)S(1)}, bf16[2,48,1280]{2,1,0:T(8,128)(2,1)S(1)}, u32[]{:S(2)}, u32[]{:S(2)}) collective-permute-start(bf16[2,48,1280]{2,1,0:T(8,128)(2,1)S(1)} %fusion.96), channel_id=1, source_target_pairs={{0,4},{1,5},{2,6},{3,7},{4,0},{5,1},{6,2},{7,3},{8,12},{9,13},{10,... | collective-permute-start | bytes 737288 | tf_op jit(solution)/shard_map/ppermute | solution.py:61
  320.5 6.4 %collective-permute-start.22 = (bf16[48,1280]{1,0:T(8,128)(2,1)S(1)}, bf16[48,1280]{1,0:T(8,128)(2,1)S(1)}, u32[]{:S(2)}, u32[]{:S(2)}) collective-permute-start(bf16[48,1280]{1,0:T(8,128)(2,1)S(1)} %fusion.113), channel_id=1, source_target_pairs={{0,8},{1,9},{2,10},{3,11},{4,12},{5,13},{6,14},{7,15},{8,0},{9,1},... | collective-permute-start | bytes 368648 | tf_op jit(solution)/shard_map/ppermute | solution.py:61
  323.0 5.7 %collective-permute-start.19 = (bf16[48,1280]{1,0:T(8,128)(2,1)S(1)}, bf16[48,1280]{1,0:T(8,128)(2,1)S(1)}, u32[]{:S(2)}, u32[]{:S(2)}) collective-permute-start(bf16[48,1280]{1,0:T(8,128)(2,1)S(1)} %fusion.112), channel_id=1, source_target_pairs={{0,2},{1,3},{2,0},{3,1},{4,6},{5,7},{6,4},{7,5},{8,10},{9,11},{10,... | collective-permute-start | bytes 368648 | tf_op jit(solution)/shard_map/ppermute | solution.py:61
  324.5 4.9 collective-permute-start.10
  325.8 4.9 collective-permute-start.7
  336.8 12.0 %all-to-all-start.3 = ((bf16[16,80,128]{2,1,0:T(8,128)(2,1)}), bf16[16,80,128]{2,1,0:T(8,128)(2,1)S(1)}, u32[]{:S(2)}, u32[]{:S(2)}) async-start(bf16[16,80,128]{2,1,0:T(8,128)(2,1)} %bitcast.61), calls=%async_computation.3 | async-start | bytes 655360 | tf_op jit(solution)/shard_map/all_to_all | solution.py:99
  340.8 24.0 %copy-start.63 = (f32[128]{0:T(128)}, f32[128]{0:T(128)S(1)}, u32[]{:S(2)}) copy-start(f32[128]{0:T(128)S(1)} %fusion.61) | copy-start | bytes 1540
  369.0 53.8 %collective-permute-start.26 = (bf16[8,128,1280]{2,1,0:T(8,128)(2,1)}, bf16[8,128,1280]{2,1,0:T(8,128)(2,1)}, u32[]{:S(2)}, u32[]{:S(2)}) collective-permute-start(bf16[8,128,1280]{2,1,0:T(8,128)(2,1)} %convolution_convert_fusion), channel_id=1, source_target_pairs={{0,1},{1,0},{2,3},{3,2},{4,5},{5,4},{6,7},{7,6},{8,9},{9,8},{10,11... | collective-permute-start | bytes 7864328 | tf_op jit(solution)/shard_map/ppermute | solution.py:61
  408.9 41.7 %all-to-all-start.5 = ((bf16[32,40,560]{2,1,0:T(8,128)(2,1)}), bf16[32,40,560]{2,1,0:T(8,128)(2,1)}, u32[]{:S(2)}, u32[]{:S(2)}) async-start(bf16[32,40,560]{2,1,0:T(8,128)(2,1)} %pad_maximum_fusion), calls=%async_computation.5 | async-start | bytes 3276800 | tf_op jit(solution)/shard_map/all_to_all | solution.py:102
  412.3 118.9 %all-gather.18.cloned.1.call-start = ((), (), s32[]{:S(2)}) async-start(), calls=%async_computation.9 | async-start | bytes 5570560 | tf_op jit(solution)/shard_map/all_gather | solution.py:96
  427.3 29.0 %collective-permute-start.33 = (bf16[2,2,32,1280]{3,2,1,0:T(8,128)(2,1)}, bf16[2,2,32,1280]{3,2,1,0:T(8,128)(2,1)}, u32[]{:S(2)}, u32[]{:S(2)}) collective-permute-start(bf16[2,2,32,1280]{3,2,1,0:T(8,128)(2,1)} %fusion.91), channel_id=1, source_target_pairs={{0,2},{1,3},{2,0},{3,1},{4,6},{5,7},{6,4},{7,5},{8,10},{9,11},{10,... | collective-permute-start | bytes 983048 | tf_op jit(solution)/shard_map/ppermute | solution.py:61
  430.1 45.2 %collective-permute-start.30 = (bf16[2,2,48,1280]{3,2,0,1:T(8,128)(2,1)}, bf16[2,2,48,1280]{3,2,0,1:T(8,128)(2,1)}, u32[]{:S(2)}, u32[]{:S(2)}) collective-permute-start(bf16[2,2,48,1280]{3,2,0,1:T(8,128)(2,1)} %fusion.87), channel_id=1, source_target_pairs={{0,4},{1,5},{2,6},{3,7},{4,0},{5,1},{6,2},{7,3},{8,12},{9,13},{10,... | collective-permute-start | bytes 1474568 | tf_op jit(solution)/shard_map/ppermute | solution.py:61
  432.4 44.2 %collective-permute-start.27 = (bf16[2,2,48,1280]{3,2,1,0:T(8,128)(2,1)}, bf16[2,2,48,1280]{3,2,1,0:T(8,128)(2,1)}, u32[]{:S(2)}, u32[]{:S(2)}) collective-permute-start(bf16[2,2,48,1280]{3,2,1,0:T(8,128)(2,1)} %fusion.84), channel_id=1, source_target_pairs={{0,8},{1,9},{2,10},{3,11},{4,12},{5,13},{6,14},{7,15},{8,0},{9,1},... | collective-permute-start | bytes 1474568 | tf_op jit(solution)/shard_map/ppermute | solution.py:61
  457.5 15.0 %collective-permute-start.34 = (bf16[2,32,1280]{2,1,0:T(8,128)(2,1)S(1)}, bf16[2,32,1280]{2,1,0:T(8,128)(2,1)S(1)}, u32[]{:S(2)}, u32[]{:S(2)}) collective-permute-start(bf16[2,32,1280]{2,1,0:T(8,128)(2,1)S(1)} %fusion.109), channel_id=1, source_target_pairs={{0,8},{1,9},{2,10},{3,11},{4,12},{5,13},{6,14},{7,15},{8,0},{9,1},... | collective-permute-start | bytes 491528 | tf_op jit(solution)/shard_map/ppermute | solution.py:61
  472.6 5.4 collective-permute-start.35
  476.5 7.8 %collective-permute-start.31 = (bf16[2,48,1280]{2,1,0:T(8,128)(2,1)S(1)}, bf16[2,48,1280]{2,1,0:T(8,128)(2,1)S(1)}, u32[]{:S(2)}, u32[]{:S(2)}) collective-permute-start(bf16[2,48,1280]{2,1,0:T(8,128)(2,1)S(1)} %fusion.101), channel_id=1, source_target_pairs={{0,2},{1,3},{2,0},{3,1},{4,6},{5,7},{6,4},{7,5},{8,10},{9,11},{10,... | collective-permute-start | bytes 737288 | tf_op jit(solution)/shard_map/ppermute | solution.py:61
  477.8 7.8 %collective-permute-start.28 = (bf16[2,48,1280]{2,1,0:T(8,128)(2,1)S(1)}, bf16[2,48,1280]{2,1,0:T(8,128)(2,1)S(1)}, u32[]{:S(2)}, u32[]{:S(2)}) collective-permute-start(bf16[2,48,1280]{2,1,0:T(8,128)(2,1)S(1)} %fusion.100), channel_id=1, source_target_pairs={{0,4},{1,5},{2,6},{3,7},{4,0},{5,1},{6,2},{7,3},{8,12},{9,13},{10,... | collective-permute-start | bytes 737288 | tf_op jit(solution)/shard_map/ppermute | solution.py:61
  478.6 20.6 %copy-start.48 = (f32[32,160]{1,0:T(8,128)S(1)}, f32[32,160]{1,0:T(8,128)}, u32[]{:S(2)}) copy-start(f32[32,160]{1,0:T(8,128)} %reshape_reshape.3) | copy-start | bytes 61444
  484.4 4.9 collective-permute-start.32
  485.6 23.2 %copy-start.11 = (f32[128,1280]{1,0:T(8,128)S(1)}, f32[128,1280]{1,0:T(8,128)}, u32[]{:S(2)}) copy-start(f32[128,1280]{1,0:T(8,128)} %copy-done.10) | copy-start | bytes 1966084
  485.6 23.2 %copy-start.25 = (bf16[64,1280]{1,0:T(8,128)(2,1)S(1)}, bf16[64,1280]{1,0:T(8,128)(2,1)}, u32[]{:S(2)}) copy-start(bf16[64,1280]{1,0:T(8,128)(2,1)} %copy-done.23) | copy-start | bytes 491524
  485.7 23.2 %copy-start.28 = (bf16[64,1280]{1,0:T(8,128)(2,1)S(1)}, bf16[64,1280]{1,0:T(8,128)(2,1)}, u32[]{:S(2)}) copy-start(bf16[64,1280]{1,0:T(8,128)(2,1)} %copy-done.26) | copy-start | bytes 491524
  485.7 23.2 %copy-start.59 = (f32[128]{0:T(128)S(1)}, f32[128]{0:T(128)}, u32[]{:S(2)}) copy-start(f32[128]{0:T(128)} %copy-done.58) | copy-start | bytes 1540
  485.7 4.9 collective-permute-start.29
  500.8 18.3 %all-to-all-start.4 = ((f32[32,1,480]{2,1,0:T(1,128)}), f32[32,1,480]{2,1,0:T(1,128)}, u32[]{:S(2)}, u32[]{:S(2)}) async-start(f32[32,1,480]{2,1,0:T(1,128)} %copy.139), calls=%async_computation.4 | async-start | bytes 131072 | tf_op jit(solution)/shard_map/all_to_all | solution.py:102
  510.0 11.2 %collective-permute-start.36 = (bf16[2,64,1280]{2,1,0:T(8,128)(2,1)}, bf16[2,64,1280]{2,1,0:T(8,128)(2,1)}, u32[]{:S(2)}, u32[]{:S(2)}) collective-permute-start(bf16[2,64,1280]{2,1,0:T(8,128)(2,1)} %get-tuple-element.81), channel_id=1, source_target_pairs={{0,0},{16,1},{1,2},{17,3},{2,4},{18,5},{3,6},{19,7},{4,8},{20,9},{... | collective-permute-start | bytes 983048 | tf_op jit(solution)/shard_map/ppermute | solution.py:61
  513.9 16.2 %collective-permute-start.37 = (bf16[2,64,1280]{2,1,0:T(8,128)(2,1)}, bf16[2,64,1280]{2,1,0:T(8,128)(2,1)}, u32[]{:S(2)}, u32[]{:S(2)}) collective-permute-start(bf16[2,64,1280]{2,1,0:T(8,128)(2,1)} %get-tuple-element.82), channel_id=1, source_target_pairs={{16,0},{0,1},{17,2},{1,3},{18,4},{2,5},{19,6},{3,7},{20,8},{4,9},{... | collective-permute-start | bytes 983048 | tf_op jit(solution)/shard_map/ppermute | solution.py:61
  535.0 5.8 %collective-permute-start.38 = (bf16[200,1280]{1,0:T(8,128)(2,1)S(1)}, bf16[200,1280]{1,0:T(8,128)(2,1)S(1)}, u32[]{:S(2)}, u32[]{:S(2)}) collective-permute-start(bf16[200,1280]{1,0:T(8,128)(2,1)S(1)} %get-tuple-element.75), channel_id=1, source_target_pairs={{0,0},{16,1},{1,2},{17,3},{2,4},{18,5},{3,6},{19,7},{4,8},{20,9},{... | collective-permute-start | bytes 1536008 | tf_op jit(solution)/shard_map/ppermute | solution.py:61
  535.7 25.9 %collective-permute-start.39 = (bf16[200,1280]{1,0:T(8,128)(2,1)S(1)}, bf16[200,1280]{1,0:T(8,128)(2,1)S(1)}, u32[]{:S(2)}, u32[]{:S(2)}) collective-permute-start(bf16[200,1280]{1,0:T(8,128)(2,1)S(1)} %get-tuple-element.76), channel_id=1, source_target_pairs={{16,0},{0,1},{17,2},{1,3},{18,4},{2,5},{19,6},{3,7},{20,8},{4,9},{... | collective-permute-start | bytes 1536008 | tf_op jit(solution)/shard_map/ppermute | solution.py:61
  539.1 24.4 %copy-start.1 = (s32[2,3]{1,0:T(2,128)S(1)}, s32[2,3]{1,0:T(2,128)}, u32[]{:S(2)}) copy-start(s32[2,3]{1,0:T(2,128)} %param.19) | copy-start | bytes 76
  (53 other events, 367.3 us)
Sparse Core Ops, SparseCore 0:
  26.9 76.3 all-gather.19
  105.4 30.9 all-gather.11
  145.8 55.1 all-gather.13
  202.5 34.3 all-gather.15
  418.1 64.0 all-gather.17

commit v2 on v1

v2 whole, which is shorter than its diff:
```python
import functools
import math

import jax
import jax.numpy as jnp
from jax import lax
from jax.experimental import pallas as pl
from jax.experimental.pallas import tpu as pltpu
from jax.sharding import PartitionSpec as P

eps = 1e-05
heads = 16
low = jnp.bfloat16
exact = jnp.float32
far = -1e30
lanes = 128
extra_rows = 8


def dot(a, b, ca, cb):
    return lax.dot_general(a, b, (((ca,), (cb,)), ((), ())), preferred_element_type=exact)


def normalized(v):
    mean = jnp.mean(v, axis=-1, keepdims=True)
    cent = v - mean
    inverse = lax.rsqrt(jnp.mean(cent * cent, axis=-1, keepdims=True) + eps)
    return cent * inverse, inverse


def norm_back(unit, inverse, gain, grad):
    scaled = grad * gain
    along = jnp.mean(scaled * unit, axis=-1, keepdims=True)
    return inverse * (scaled - jnp.mean(scaled, axis=-1, keepdims=True) - unit * along)


def tie(value, *others):
    return lax.optimization_barrier((value,) + others)[0]


def together(*values):
    return lax.optimization_barrier(values)


class Layout:
    def __init__(self, micro):
        self.count = lax.axis_size("dev")
        self.half = heads
        self.block = micro * heads
        self.blocks = self.count // self.block
        self.me = lax.axis_index("dev")
        self.rank = self.me % self.block
        self.mine = self.rank // self.half
        self.head = self.rank % self.half
        self.odd = self.rank % 2
        bits = [(self.me // bit) % 2 for bit in (1, 2, 4, 8)]
        self.place = jnp.stack(bits + [self.mine, self.head, self.odd]).astype(jnp.int32)
        self.halves = [list(range(s, s + self.half)) for s in range(0, self.count, self.half)]
        self.whole = [list(range(s, s + self.block)) for s in range(0, self.count, self.block)]
        self.rows = [list(range(s, s + self.blocks)) for s in range(0, self.count, self.blocks)]
        first = [d // self.half % 2 for d in range(self.count)]
        base = [d // self.block * self.block + 2 * (d % self.half) for d in range(self.count)]
        self.even_first = [(d, base[d] + first[d]) for d in range(self.count)]
        self.odd_first = [(d, base[d] + 1 - first[d]) for d in range(self.count)]

    def send(self, value, pairs):
        return lax.ppermute(value, "dev", pairs)

    def swapped(self, value, bit):
        return self.send(value, [(d, d ^ bit) for d in range(self.count)])

    def to_block(self, value):
        if self.blocks == 1:
            return value
        value = lax.all_gather(value, "dev", axis=0, tiled=True, axis_index_groups=self.rows)
        return self.send(value, [(d, d % self.blocks * self.block + d // self.blocks) for d in range(self.count)])

    def from_block(self, value):
        if self.blocks == 1:
            return value
        value = self.send(value, [(d % self.blocks * self.block + d // self.blocks, d) for d in range(self.count)])
        return lax.psum_scatter(value, "dev", scatter_dimension=0, tiled=True, axis_index_groups=self.rows)

    def partner(self, value):
        return self.swapped(value, self.half)

    def ordered(self, kept, got):
        return jnp.where(self.mine == 0, kept, got), jnp.where(self.mine == 0, got, kept)

    def exchanged(self, value):
        kept = lax.dynamic_index_in_dim(value, self.mine, 0, False)
        return kept, self.partner(lax.dynamic_index_in_dim(value, 1 - self.mine, 0, False))

    def send_rows_back(self, value):
        first = lax.dynamic_index_in_dim(value, self.mine, 0, False)
        second = lax.dynamic_index_in_dim(value, 1 - self.mine, 0, False)
        return self.send(first, self.even_first), self.send(second, self.odd_first)

    def gather_half(self, value):
        return lax.all_gather(value, "dev", axis=0, axis_index_groups=self.halves)

    def exchange_half(self, value):
        return lax.all_to_all(value, "dev", 0, 0, tiled=True, axis_index_groups=self.halves)

    def exchange_block(self, value):
        return lax.all_to_all(value, "dev", 0, 0, tiled=True, axis_index_groups=self.whole)

    def gather_tree(self, parts, marks=None):
        for stage in range(2):
            got = [self.swapped(piece, order[stage]) for piece, order in zip(parts, part_orders)]
            parts = merge(parts, got)
            if marks is not None:
                marks.append(parts[0])
        got = [self.swapped(piece, order[2]) for piece, order in zip(parts, part_orders)]
        other = [self.swapped(piece, 1) for piece in (*parts, *got)]
        return (*parts, *got), other

    def reduce_half(self, away, kept, marks=None, before=None):
        got = [self.swapped(away, 1)]
        kept = [kept]
        for stage in range(3):
            if before and stage in before:
                got = [tie(got[0], *before[stage](marks)), *got[1:]]
            away, kept = split_terms(self.place, stage, kept, got)
            if marks is not None:
                marks.append(away[0])
            got = [self.swapped(piece, order[stage]) for piece, order in zip(away, part_orders)]
        return kept, got


small_cost = pl.CostEstimate(flops=1 << 10, bytes_accessed=1 << 10, transcendentals=0)


def params(megabytes):
    return pltpu.CompilerParams(vmem_limit_bytes=megabytes << 20)


part_orders = ((8, 4, 2), (4, 2, 8), (2, 8, 4))


def part_bounds(tokens):
    cut = tokens * 3 // 8 // 16 * 16
    return ((0, cut), (cut, 2 * cut), (2 * cut, tokens))


def split_kernel(stage, place_ref, *refs):
    place = {bit: place_ref[i] for i, bit in enumerate((1, 2, 4, 8))}
    if stage == 0:
        kept_ref, got_ref = refs[:2]
        outs = refs[2:]
        bounds = part_bounds(kept_ref.shape[1])
    else:
        outs = refs[6:]
    for part, order in enumerate(part_orders):
        left = [bit for bit in (8, 4, 2) if bit not in order[:stage]]
        at = left.index(order[stage])
        below = 1 << (len(left) - 1 - at)
        for half, side in ((0, 1 - place[order[stage]]), (1, place[order[stage]])):
            out_ref = outs[part + 3 * half]
            for j in range(out_ref.shape[0]):
                index = (j // below * 2 + side) * below + j % below
                if stage == 0:
                    start, end = bounds[part]
                    term = kept_ref[index, start:end].astype(exact) + got_ref[index, start:end].astype(exact)
                else:
                    term = refs[part][index].astype(exact) + refs[3 + part][index].astype(exact)
                out_ref[j] = term.astype(out_ref.dtype)


def split_terms(place, stage, kept, got):
    width = kept[0].shape[-1]
    bounds = part_bounds(kept[0].shape[1]) if stage == 0 else [(0, k.shape[1]) for k in kept]
    count = kept[0].shape[0] // 2
    cols = 256 if stage == 0 else 640
    spec = lambda n, t: pl.BlockSpec((n, t, cols), lambda i, p: (0, 0, i))
    outs = [(count, end - start) for start, end in bounds]
    res = pl.pallas_call(
        functools.partial(split_kernel, stage),
        grid_spec=pltpu.PrefetchScalarGridSpec(
            num_scalar_prefetch=1,
            grid=(width // cols,),
            in_specs=[spec(*v.shape[:2]) for v in (*kept, *got)],
            out_specs=[spec(*o) for o in outs] * 2,
        ),
        out_shape=[jax.ShapeDtypeStruct(o + (width,), kind) for kind in (low, exact) for o in outs],
        compiler_params=params(32),
        cost_estimate=small_cost,
        name="split_terms",
    )(place, *kept, *got)
    return res[:3], res[3:]


def last_sum(refs):
    return jnp.concatenate([refs[i][0].astype(exact) + refs[3 + i][0].astype(exact) for i in range(3)], axis=0)


def pack_kernel(place_ref, x_ref, v_ref, c_ref, w_ref, first_ref, second_ref):
    rows, width = x_ref.shape[1:]
    mine = place_ref[4]
    fill = jnp.zeros((v_ref.shape[0], width - v_ref.shape[1]), exact)
    small = jnp.concatenate([v_ref[...].astype(exact), fill], axis=1)
    c = jnp.concatenate([c_ref[...].astype(exact), jnp.zeros((1, width - lanes - c_ref.shape[1]), exact)], axis=1)
    c = jnp.concatenate([jnp.zeros((1, lanes), exact), c], axis=1)
    row = lax.broadcasted_iota(jnp.int32, small.shape, 0)
    small = small + jnp.where(row == 0, c, 0.0)
    tail = jnp.concatenate([small, w_ref[...].astype(exact)], axis=0).astype(low)
    for out_ref, index in ((first_ref, mine), (second_ref, 1 - mine)):
        out_ref[:rows] = x_ref[index]
        out_ref[rows:] = tail


def pack(place, x, vectors, c, w):
    rows, width = x.shape[1:]
    out = jax.ShapeDtypeStruct((rows + extra_rows + w.shape[0], width), low)
    return pl.pallas_call(
        pack_kernel,
        grid_spec=pltpu.PrefetchScalarGridSpec(
            num_scalar_prefetch=1,
            grid=(1,),
            in_specs=[whole_spec(v) for v in (x, vectors, c, w)],
            out_specs=[whole_spec(out)] * 2,
        ),
        out_shape=[out, out],
        compiler_params=params(32),
        name="pack",
    )(place, x, vectors, c, w)


def arrange_kernel(rows, place_ref, first_ref, second_ref, x_ref, small_ref, w_ref, *part_refs):
    mine = place_ref[4]
    for side, refs in enumerate(((first_ref, second_ref), (second_ref, first_ref))):

        @pl.when(mine == side)
        def _():
            x = jnp.concatenate([ref[:rows] for ref in refs], axis=0)
            x_ref[...] = x
            tail = [ref[rows:].astype(exact) for ref in refs]
            small_ref[...] = jnp.concatenate([t[:extra_rows] for t in tail], axis=0).astype(low)
            w_ref[...] = jnp.concatenate([t[extra_rows:] for t in tail], axis=0).astype(low)
            for part_ref, (start, end) in zip(part_refs, part_bounds(2 * rows)):
                part_ref[0] = x[start:end]


def arrange(place, first, second, rows):
    width = first.shape[1]
    shapes = [(2 * rows, width), (2 * extra_rows, width), (2 * (first.shape[0] - rows - extra_rows), width)]
    shapes += [(1, end - start, width) for start, end in part_bounds(2 * rows)]
    outs = [jax.ShapeDtypeStruct(shape, low) for shape in shapes]
    return pl.pallas_call(
        functools.partial(arrange_kernel, rows),
        grid_spec=pltpu.PrefetchScalarGridSpec(
            num_scalar_prefetch=1,
            grid=(1,),
            in_specs=[whole_spec(first), whole_spec(second)],
            out_specs=[whole_spec(out) for out in outs],
        ),
        out_shape=outs,
        compiler_params=params(32),
        name="arrange",
    )(place, first, second)


def merge_kernel(*refs):
    for i in range(3):
        count = refs[i].shape[0]
        refs[6 + i][:count] = refs[i][...]
        refs[6 + i][count:] = refs[3 + i][...]


def merge(parts, got):
    width = parts[0].shape[2]
    cols = 640
    spec = lambda shape: pl.BlockSpec(shape[:2] + (cols,), lambda i: (0, 0, i))
    outs = [(2 * p.shape[0],) + p.shape[1:] for p in parts]
    return pl.pallas_call(
        merge_kernel,
        grid=(width // cols,),
        in_specs=[spec(v.shape) for v in (*parts, *got)],
        out_specs=[spec(o) for o in outs],
        out_shape=[jax.ShapeDtypeStruct(o, low) for o in outs],
        compiler_params=params(32),
        name="merge",
    )(*parts, *got)


def tree_rows(place_ref, chip, refs, fill):
    mine = place_ref[1] + 2 * place_ref[2] + 4 * place_ref[3]
    apart = chip ^ mine
    step = {8: apart // 4, 4: apart // 2 % 2, 2: apart % 2}
    for part, order in enumerate(part_orders):
        index = 2 * step[order[1]] + step[order[0]]
        for late in range(2):

            @pl.when(step[order[2]] == late)
            def _():
                fill(part, refs[part + 3 * late], index)


def fill_rows(place_ref, chip, refs, out_ref, base, own):
    bounds = part_bounds(own)

    def fill(part, ref, index):
        start, end = bounds[part]
        out_ref[pl.ds(base + start, end - start)] = ref[index, : end - start]

    tree_rows(place_ref, chip, refs, fill)


def whole_spec(v):
    return pl.BlockSpec(v.shape, lambda i, p: (0,) * len(v.shape))


def project_kernel(hd, clips, chunk, first, place_ref, *refs):
    pieces, refs = refs[:6], refs[6:]
    ids_ref, w_ref = refs[:2]
    a_ref, qkv_ref, table_ref, x_scr, bias_ref = refs[-5:]
    step, _, own, width = a_ref.shape

    @pl.when(pl.program_id(0) == 0)
    def _():
        if first:
            tail = part_bounds(own)[2]

            def fill(chip, part, ref, index):
                if part != 2:
                    return
                small = ref[index, tail[1] - tail[0] :].astype(exact)
                for far_core in range(2):
                    for slot in range(2):
                        line = (2 * far_core + slot) * extra_rows
                        piece = small[line : line + extra_rows, :chunk]
                        for core in range(2):

                            @pl.when(place_ref[0] == core)
                            def _():
                                at = (heads * slot + 2 * chip + (core ^ far_core)) * chunk
                                table_ref[:, at : at + chunk] = piece

            for chip in range(8):
                tree_rows(place_ref, chip, pieces, functools.partial(fill, chip))
        else:
            table_ref[...] = refs[2][...]
        bias_ref[...] = jnp.zeros_like(bias_ref)
        for h in range(heads):

            @pl.when(place_ref[5] == h)
            def _():
                for line, at in ((2, 0), (3, 2 * lanes)):
                    bias_ref[0:1, at : at + hd] = table_ref[line : line + 1, h * hd : (h + 1) * hd]

    for j in range(step):
        fill_rows(place_ref, pl.program_id(0) * step + j, pieces, x_scr, j * own, own)
    unit, _ = normalized(x_scr[...].astype(exact))
    a = (unit * table_ref[0:1] + table_ref[1:2]).astype(low)
    a_ref[...] = a.reshape(a_ref.shape)
    qkv = dot(a, w_ref[...], 1, 0)
    fill = jnp.zeros((step * own, lanes - hd), exact)
    qkv = [v for i in range(3) for v in (qkv[:, i * hd : (i + 1) * hd], fill)]
    qkv = jnp.concatenate(qkv, axis=1) + bias_ref[0:1]
    column = lax.broadcasted_iota(jnp.int32, (step * own, lanes), 1) - hd
    match = ids_ref[...].reshape(step * own, 1) == column
    marked = (column >= 0) & (column <= clips)
    q = qkv[:, :lanes] + jnp.where(marked & ~match, far, 0.0)
    k = qkv[:, lanes : 2 * lanes] + jnp.where(marked & match, 1.0, 0.0)
    qkv = jnp.concatenate([q, k, qkv[:, 2 * lanes :]], axis=1).astype(low)
    qkv_ref[...] = qkv.reshape(qkv_ref.shape)


def project(place, other, pieces, ids, w, before, hd, clips, own, chunk):
    width = w.shape[0]
    step = 4
    side = (lambda p: 1 - p[0]) if other else (lambda p: p[0])
    pick = lambda size: pl.BlockSpec((step, 1, own, size), lambda i, p: (i, side(p), 0, 0))
    table = jax.ShapeDtypeStruct((extra_rows, width), exact)
    ahead = [before[2], *before[:2]] if before else []
    return pl.pallas_call(
        functools.partial(project_kernel, hd, clips, chunk, not before),
        grid_spec=pltpu.PrefetchScalarGridSpec(
            num_scalar_prefetch=1,
            grid=(8 // step,),
            in_specs=[whole_spec(v) for v in pieces]
            + [pick(1), whole_spec(w)]
            + ([whole_spec(table)] + [pl.BlockSpec(memory_space=pl.ANY)] * 2 if before else []),
            out_specs=[pick(width), pick(3 * lanes), whole_spec(table)],
            scratch_shapes=[pltpu.VMEM((step * own, width), low), pltpu.VMEM((8, 3 * lanes), exact)],
        ),
        out_shape=[
            jax.ShapeDtypeStruct((8, 2, own, width), low),
            jax.ShapeDtypeStruct((8, 2, own, 3 * lanes), low),
            table,
        ],
        input_output_aliases={10: 0, 11: 1} if before else {},
        compiler_params=params(48),
        cost_estimate=small_cost,
        name="project",
    )(place, *pieces, ids, w, *ahead)


def join_kernel(x_ref, o_ref, w_ref, table_ref, x2_ref, *part_refs):
    o = o_ref[...].reshape(w_ref.shape[0], o_ref.shape[2])
    x2 = x_ref[...].astype(exact) + (dot(o, w_ref[...], 0, 0) + table_ref[4:5])
    x2_ref[...] = x2
    unit, _ = normalized(x2)
    a2 = (unit * table_ref[5:6] + table_ref[6:7]).astype(low)
    for part_ref, (start, end) in zip(part_refs, part_bounds(x2.shape[0])):
        part_ref[0] = a2[start:end]


def join(x, o, w, table):
    own, width = x.shape
    parts = [jax.ShapeDtypeStruct((1, end - start, width), low) for start, end in part_bounds(own)]
    return pl.pallas_call(
        join_kernel,
        out_shape=[jax.ShapeDtypeStruct(x.shape, exact)] + parts,
        compiler_params=params(32),
        cost_estimate=small_cost,
        name="join",
    )(x, o, w, table)


def assemble_kernel(place_ref, *refs):
    mine, others, out_ref = refs[:6], refs[6:12], refs[12]
    chips, _, own, _ = out_ref.shape
    for j in range(chips):
        chip = pl.program_id(0) * chips + j
        for core, pieces in ((place_ref[0], mine), (1 - place_ref[0], others)):
            bounds = part_bounds(own)

            def fill(part, ref, index):
                start, end = bounds[part]
                out_ref[j, core, start:end] = ref[index]

            tree_rows(place_ref, chip, pieces, fill)


def assemble(place, mine, others, own):
    width = mine[0].shape[2]
    step = 2
    return pl.pallas_call(
        assemble_kernel,
        grid_spec=pltpu.PrefetchScalarGridSpec(
            num_scalar_prefetch=1,
            grid=(8 // step,),
            in_specs=[whole_spec(v) for v in (*mine, *others)],
            out_specs=pl.BlockSpec((step, 2, own, width), lambda i, p: (i, 0, 0, 0)),
        ),
        out_shape=jax.ShapeDtypeStruct((8, 2, own, width), low),
        compiler_params=params(40),
        cost_estimate=small_cost,
        name="assemble",
    )(place, *mine, *others)


def feed_kernel(place_ref, *refs):
    pieces, (g_ref, w1_ref, w2_ref, c_ref) = refs[:6], refs[6:10]
    hid_ref, du_ref, da_ref, sum_ref, a_scr = refs[-5:]
    step, own, width = da_ref.shape
    rows = step * own
    for j in range(step):
        fill_rows(place_ref, pl.program_id(0) * step + j, pieces, a_scr, j * own, own)
    w1 = w1_ref[...]
    u = dot(a_scr[...], w1, 1, 0) + c_ref[...]
    d_hid = dot(g_ref[...].reshape(rows, width), w2_ref[...], 1, 1)
    below = 0.5 * (1.0 + lax.erf(u * math.sqrt(0.5)))
    hid_ref[...] = (u * below).astype(low).reshape(hid_ref.shape)
    slope = below + u * (jnp.exp(-0.5 * u * u) * (1.0 / math.sqrt(2.0 * math.pi)))
    du = (d_hid * slope).astype(low)
    du_ref[...] = du.reshape(du_ref.shape)
    da_ref[...] = dot(du, w1, 1, 1).reshape(da_ref.shape).astype(da_ref.dtype)

    @pl.when(pl.program_id(0) == 0)
    def _():
        sum_ref[...] = jnp.zeros_like(sum_ref)

    sum_ref[...] += jnp.sum(du.astype(exact), axis=0, keepdims=True)


def feed(place, other, pieces, g, w1, w2, c1, before, own, kind):
    width, ff = w1.shape
    step = 4
    tokens = 8 * own
    side = (lambda p: 1 - p[0]) if other else (lambda p: p[0])
    pick = lambda size: pl.BlockSpec((step, 1, own, size), lambda i, p: (i, side(p), 0, 0))
    pair = jax.ShapeDtypeStruct((8, 2, own, ff), low)
    row = pl.BlockSpec((1, ff), lambda i, p: (0, 0))
    return pl.pallas_call(
        feed_kernel,
        grid_spec=pltpu.PrefetchScalarGridSpec(
            num_scalar_prefetch=1,
            grid=(8 // step,),
            in_specs=[whole_spec(v) for v in pieces]
            + [pick(width), whole_spec(w1), whole_spec(w2), row]
            + [pl.BlockSpec(memory_space=pl.ANY)] * len(before),
            out_specs=[pick(ff), pick(ff), pl.BlockSpec((step, own, width), lambda i, p: (i, 0, 0)), row],
            scratch_shapes=[pltpu.VMEM((step * own, width), low)],
        ),
        out_shape=[
            pair,
            pair,
            jax.ShapeDtypeStruct((8, own, width), kind),
            jax.ShapeDtypeStruct((1, ff), exact),
        ],
        input_output_aliases={11: 0, 12: 1} if before else {},
        compiler_params=params(56),
        cost_estimate=small_cost,
        name="feed",
    )(place, *pieces, g, w1, w2, c1, *before)


def terms_kernel(contract, place_ref, left_ref, right_ref, out_ref):
    rows = out_ref.shape[0] * out_ref.shape[1]
    left = left_ref[...].reshape(rows, left_ref.shape[-1])
    out_ref[...] = dot(left, right_ref[...], 1, contract).reshape(out_ref.shape).astype(out_ref.dtype)


def terms(place, other, left, right, contract, kind):
    eight, two, own, depth = left.shape
    width = right.shape[1 - contract]
    step = 2
    side = (lambda p: 1 - p[0]) if other else (lambda p: p[0])
    return pl.pallas_call(
        functools.partial(terms_kernel, contract),
        grid_spec=pltpu.PrefetchScalarGridSpec(
            num_scalar_prefetch=1,
            grid=(eight // step,),
            in_specs=[
                pl.BlockSpec((step, 1, own, depth), lambda i, p: (i, side(p), 0, 0)),
                pl.BlockSpec(right.shape, lambda i, p: (0, 0)),
            ],
            out_specs=pl.BlockSpec((step, own, width), lambda i, p: (i, 0, 0)),
        ),
        out_shape=jax.ShapeDtypeStruct((eight, own, width), kind),
        compiler_params=params(40),
        cost_estimate=small_cost,
        name="terms",
    )(place, left, right)


def rows_of(values, width):
    fill = jnp.zeros((8 - len(values), width), exact)
    return jnp.concatenate(values + [fill], axis=0)


def second_back_kernel(*refs):
    da2 = last_sum(refs[:6])
    x2_ref, g_ref, table_ref, w_ref, dx2_ref, ga_ref, do_ref, sum_ref = refs[6:]
    unit, inverse = normalized(x2_ref[...])
    g = g_ref[...].astype(exact)
    dx2 = g + norm_back(unit, inverse, table_ref[5:6], da2)
    dx2_ref[...] = dx2
    ga = dx2.astype(low)
    ga_ref[...] = ga
    do_ref[...] = dot(w_ref[...], ga, 1, 1).astype(low).reshape(do_ref.shape)
    total = lambda v: jnp.sum(v, axis=0, keepdims=True)
    sum_ref[...] = rows_of([total(da2 * unit), total(da2), total(ga.astype(exact)), total(g)], ga.shape[1])


def second_back(kept, got, x2, g, table, w, hd):
    own, width = x2.shape
    return pl.pallas_call(
        second_back_kernel,
        out_shape=[
            jax.ShapeDtypeStruct((own, width), exact),
            jax.ShapeDtypeStruct((own, width), low),
            jax.ShapeDtypeStruct((heads, hd, own), low),
            jax.ShapeDtypeStruct((8, width), exact),
        ],
        compiler_params=params(40),
        cost_estimate=small_cost,
        name="second_back",
    )(*kept, *got, x2, g, table, w)


def first_back_kernel(chunk, *refs):
    da1 = last_sum(refs[:6])
    x_ref, dx2_ref, table_ref, dx_ref, vec_ref = refs[6:]
    unit, inverse = normalized(x_ref[...].astype(exact))
    dx = dx2_ref[...] + norm_back(unit, inverse, table_ref[0:1], da1)
    dx_ref[...] = dx.astype(low)
    total = lambda v: jnp.sum(v, axis=0, keepdims=True)
    rows = [total(da1 * unit), total(da1)]
    fill = jnp.zeros((1, lanes // 2 - chunk), exact)
    for device in range(vec_ref.shape[0]):
        part = slice(device * chunk, (device + 1) * chunk)
        vec_ref[device] = jnp.concatenate([rows[0][:, part], fill, rows[1][:, part], fill], axis=1)


def first_back(kept, got, x, dx2, table, chunk, block):
    return pl.pallas_call(
        functools.partial(first_back_kernel, chunk),
        out_shape=[jax.ShapeDtypeStruct(x.shape, low), jax.ShapeDtypeStruct((block, 1, lanes), exact)],
        compiler_params=params(32),
        name="first_back",
    )(*kept, *got, x, dx2, table)


def lay_out_kernel(hd, chunk, place_ref, in_ref, sum2_ref, sum_in_ref, sum_c_ref, sum_c2_ref, out_ref):
    block = out_ref.shape[0]
    head = place_ref[5]
    c = sum_c_ref[...] + sum_c2_ref[...]
    ff_rows = c.shape[1] // 2
    rest = jnp.zeros((8, 3 * hd - chunk), exact)
    zeros = jnp.zeros((2, chunk), exact)
    narrow = jnp.concatenate([in_ref[:, i * lanes : i * lanes + hd] for i in range(3)], axis=1)
    pad = jnp.zeros((1, 3 * hd - chunk - ff_rows), exact)
    row = lax.broadcasted_iota(jnp.int32, (8, 3 * hd), 0)
    for device in range(block):
        part = slice(device * chunk, (device + 1) * chunk)
        small = jnp.concatenate([sum2_ref[0:4, part], zeros, zeros], axis=0)
        small = jnp.concatenate([small, rest], axis=1)
        slot = device % 2
        cols = slice(slot * chunk, (slot + 1) * chunk)
        for line, at in ((4, 0), (5, 2 * lanes)):
            own = jnp.concatenate([sum_in_ref[0:1, at : at + hd][:, cols], rest[0:1]], axis=1)
            small += jnp.where((row == line) & (head == device // 2), own, 0.0)
        slot = device // heads
        own = jnp.concatenate([zeros[0:1], c[:, slot * ff_rows : (slot + 1) * ff_rows], pad], axis=1)
        small += jnp.where((row == 0) & (head == device % heads), own, 0.0)
        out_ref[device] = jnp.concatenate([narrow[part], small], axis=0).astype(low)


def lay_out(place, d_in, sum2, sum_in, sum_c, sum_c2, hd, chunk, block):
    smem = pl.BlockSpec(memory_space=pltpu.SMEM)
    vmem = pl.BlockSpec(memory_space=pltpu.VMEM)
    return pl.pallas_call(
        functools.partial(lay_out_kernel, hd, chunk),
        in_specs=[smem] + [vmem] * 5,
        out_shape=jax.ShapeDtypeStruct((block, chunk + 8, 3 * hd), low),
        compiler_params=params(32),
        name="lay_out",
    )(place, d_in, sum2, sum_in, sum_c, sum_c2)


def collect_kernel(hd, *refs):
    in_ref, *out_refs, small_ref = refs
    chunk = out_refs[0].shape[0]
    block = in_ref.shape[0]
    small = jnp.zeros(small_ref.shape, exact)
    for head in range(block // 2):
        first, second = in_ref[head].astype(exact), in_ref[block // 2 + head].astype(exact)
        total = first + second
        small += total[chunk:]
        for i, out_ref in enumerate(out_refs):
            out_ref[:, head * hd : (head + 1) * hd] = total[:chunk, i * hd : (i + 1) * hd]
    small_ref[...] = small


def collect(terms_in, hd, chunk):
    block = terms_in.shape[0]
    matrix = jax.ShapeDtypeStruct((chunk, block // 2 * hd), exact)
    return pl.pallas_call(
        functools.partial(collect_kernel, hd),
        out_shape=[matrix] * 3 + [jax.ShapeDtypeStruct((8, 3 * hd), exact)],
        compiler_params=params(32),
        name="collect",
    )(terms_in)


def collect_hidden_kernel(in_ref, out_ref):
    block, _, ff = in_ref.shape
    for slice_at in range(block // 2):
        total = in_ref[slice_at].astype(exact) + in_ref[block // 2 + slice_at].astype(exact)
        for slot in range(2):
            at = (slot * (block // 2) + slice_at) * (ff // 2)
            out_ref[:, at : at + ff // 2] = total[:, slot * (ff // 2) : (slot + 1) * (ff // 2)]


def collect_hidden(terms_in):
    block, chunk, ff = terms_in.shape
    return pl.pallas_call(
        collect_hidden_kernel,
        out_shape=jax.ShapeDtypeStruct((chunk, block // 2 * ff), exact),
        compiler_params=params(32),
        name="collect_hidden",
    )(terms_in)


def attend_kernel(hd, coef, q_ref, k_ref, v_ref, o_ref, lse_ref, vt_ref):
    @pl.when(pl.program_id(0) == 0)
    def _():
        vt_ref[...] = v_ref[...].T

    s = dot(k_ref[...], q_ref[...], 1, 1)
    top = jnp.max(s, axis=0, keepdims=True)
    e = jnp.exp2((s - top) * coef)
    total = jnp.sum(e, axis=0, keepdims=True)
    o = dot(vt_ref[...], e.astype(low), 1, 0) / total
    o = o.astype(low)
    for piece in range(o_ref.shape[0]):
        o_ref[piece] = o[:hd, piece * lanes : (piece + 1) * lanes]
    lse_ref[0] = top * coef + jnp.log2(total)


def attend(q, q_at, k, k_at, v, v_at, hd, rows):
    tokens, keys = q.shape[0], k.shape[0]
    coef = math.log2(math.e) / hd**0.5
    steps = tokens // rows
    return pl.pallas_call(
        functools.partial(attend_kernel, hd, coef),
        grid=(steps,),
        in_specs=[
            pl.BlockSpec((rows, lanes), lambda i: (i, q_at)),
            pl.BlockSpec((keys, lanes), lambda i: (0, k_at)),
            pl.BlockSpec((keys, lanes), lambda i: (0, v_at)),
        ],
        out_specs=[
            pl.BlockSpec((rows // lanes, hd, lanes), lambda i: (i, 0, 0)),
            pl.BlockSpec((1, 1, rows), lambda i: (i, 0, 0)),
        ],
        out_shape=[
            jax.ShapeDtypeStruct((tokens // lanes, hd, lanes), low),
            jax.ShapeDtypeStruct((steps, 1, rows), exact),
        ],
        scratch_shapes=[pltpu.VMEM((lanes, keys), low)],
        compiler_params=params(48),
        cost_estimate=small_cost,
        name="attend",
    )(q, k, v)


def attend_back_kernel(hd, coef, scale, span, q_ref, k_ref, v_ref, do_ref, lse_ref, out_ref, sum_ref, kt_ref, dk_sum, dv_sum):
    step = pl.program_id(0)
    rows = q_ref.shape[0]

    @pl.when(step == 0)
    def _():
        kt_ref[...] = k_ref[...].T
        dk_sum[...] = jnp.zeros_like(dk_sum)
        dv_sum[...] = jnp.zeros_like(dv_sum)
        sum_ref[...] = jnp.zeros_like(sum_ref)

    pieces = do_ref.shape[0]
    dot_t = jnp.concatenate([do_ref[piece] for piece in range(pieces)], axis=1)
    fill = jnp.zeros((lanes - hd, dot_t.shape[1]), low)
    dot_t = jnp.concatenate([dot_t, fill], axis=0)
    q = q_ref[...]
    s = dot(k_ref[...], q, 1, 1)
    p = jnp.exp2(s * coef - lse_ref[0])
    dp = dot(v_ref[...], dot_t, 1, 0)
    r = jnp.sum(p * dp, axis=0, keepdims=True)
    ds = (p * (dp - r)).astype(low)
    dv_sum[...] += dot(p.astype(low), dot_t.T, 1, 0)
    dk_sum[...] += dot(ds, q, 1, 0)
    dq = dot(kt_ref[...], ds, 1, 0) * scale
    head = lax.broadcasted_iota(jnp.int32, dq.shape, 0) < hd
    dq = jnp.where(head, dq, 0.0).T.astype(low)
    out_ref[pl.ds(pl.multiple_of(span + step * rows, rows), rows), :lanes] = dq.astype(out_ref.dtype)
    sum_ref[0:1, :lanes] += jnp.sum(dq.astype(exact), axis=0, keepdims=True)

    @pl.when(step == pl.num_programs(0) - 1)
    def _():
        head = lax.broadcasted_iota(jnp.int32, dk_sum.shape, 1) < hd
        dk = jnp.where(head, dk_sum[...] * scale, 0.0)
        dv = dv_sum[...].astype(out_ref.dtype)
        out_ref[:, lanes : 2 * lanes] = dk.astype(out_ref.dtype)
        out_ref[:, 2 * lanes :] = dv
        sum_ref[0:1, 2 * lanes :] = jnp.sum(dv.astype(exact), axis=0, keepdims=True)


def attend_back(q, q_at, k, k_at, v, v_at, do, lse, hd, rows, span, kind):
    tokens, keys = q.shape[0], k.shape[0]
    scale = 1.0 / hd**0.5
    coef = math.log2(math.e) * scale
    steps = tokens // rows
    return pl.pallas_call(
        functools.partial(attend_back_kernel, hd, coef, scale, span),
        grid=(steps,),
        in_specs=[
            pl.BlockSpec((rows, lanes), lambda i: (i, q_at)),
            pl.BlockSpec((keys, lanes), lambda i: (0, k_at)),
            pl.BlockSpec((keys, lanes), lambda i: (0, v_at)),
            pl.BlockSpec((rows // lanes, hd, lanes), lambda i: (i, 0, 0)),
            pl.BlockSpec((1, 1, rows), lambda i: (i, 0, 0)),
        ],
        out_specs=[pl.BlockSpec((keys, 3 * lanes), lambda i: (0, 0)), pl.BlockSpec((8, 3 * lanes), lambda i: (0, 0))],
        out_shape=[jax.ShapeDtypeStruct((keys, 3 * lanes), kind), jax.ShapeDtypeStruct((8, 3 * lanes), exact)],
        scratch_shapes=[
            pltpu.VMEM((lanes, keys), low),
            pltpu.VMEM((keys, lanes), exact),
            pltpu.VMEM((keys, lanes), exact),
        ],
        compiler_params=params(56),
        cost_estimate=small_cost,
        name="attend_back",
    )(q, k, v, do, lse)


def body(
    hidden_in,
    clip_lengths,
    ln1_gain,
    ln1_bias,
    w_query,
    b_query,
    w_key,
    w_value,
    b_value,
    w_out,
    b_out,
    ln2_gain,
    ln2_bias,
    w_fc1,
    b_fc1,
    w_fc2,
    b_fc2,
    cotangent,
):
    micro, rows, width = hidden_in.shape
    at = Layout(micro)
    place = at.place
    hd = width // heads
    own = 2 * rows
    tokens = at.half * own
    clips = clip_lengths.shape[1]
    chunk = width // at.block
    step_rows = 256

    vectors = [at.to_block(v) for v in (ln1_gain, ln1_bias, b_query, b_value, b_out, ln2_gain, ln2_bias, b_fc2)]
    ff_bias = at.to_block(b_fc1)
    ff_rows = ff_bias.shape[0]
    first, second = pack(place, hidden_in, jnp.stack(vectors), ff_bias[None], at.to_block(w_out))
    second = at.partner(second)
    w_in = jnp.stack([at.to_block(w) for w in (w_query, w_key, w_value)], axis=1)
    w_in = w_in.reshape(chunk, 3, heads, hd).transpose(2, 0, 1, 3).reshape(heads, chunk, 3 * hd)
    w1 = at.to_block(w_fc1)
    ff = w1.shape[1] // heads
    w1 = w1.reshape(chunk, 2, heads, ff // 2).transpose(2, 0, 1, 3).reshape(heads, chunk, ff)
    w1 = jnp.concatenate([w1] * micro, axis=0)
    w_in = jnp.concatenate([w_in] * micro, axis=0)
    lower = jnp.concatenate([lax.dynamic_index_in_dim(cotangent, 1 - at.mine, 0, False), at.to_block(w_fc2)], axis=0)

    second, w_in, w1, lower = together(second, w_in, w1, lower)
    x_own, small, wo, *parts = arrange(place, first, second, rows)
    wo = at.gather_half(wo).reshape(heads, 2, chunk, width).transpose(1, 0, 2, 3).reshape(width, width)
    w_in = at.exchange_block(w_in)
    parts[2] = jnp.concatenate([parts[2], small[None], at.swapped(small, 1)[None]], axis=1)
    c1 = small.reshape(2, extra_rows, width)[:, 0, lanes : lanes + ff_rows].reshape(1, 2 * ff_rows).astype(exact)
    marks = []
    mine, others = at.gather_tree(parts, marks)

    lower, w1 = together(lower, w1, w_in, marks[1])[:2]
    lower = at.partner(lower)
    w1 = at.exchange_block(w1)
    w_in = w_in.reshape(width, 3 * hd)

    lengths = lax.dynamic_index_in_dim(clip_lengths, at.mine, 0, False)
    ends = jnp.cumsum(lengths)
    where_at = jnp.arange(tokens, dtype=jnp.int32).reshape(2, heads, rows).transpose(1, 0, 2).reshape(tokens)
    where_at = at.me // at.block * tokens + where_at
    ids = jnp.sum((ends[None, :] <= where_at[:, None]).astype(jnp.int32), axis=1).reshape(8, 2, own, 1)

    before = project(place, False, mine, ids, w_in, (), hd, clips, own, chunk)
    a1, qkv, table = project(place, True, others, ids, w_in, before, hd, clips, own, chunk)
    a1 = a1.reshape(tokens, width)
    qkv = qkv.reshape(tokens, 3 * lanes)
    span = 0
    qkv_at = (qkv, 0, qkv, 1, qkv, 2)
    if at.blocks > 1:
        span = tokens // 2
        ahead = [(d, d + at.block) for d in range(at.count - at.block)]
        behind = [(d + at.block, d) for d in range(at.count - at.block)]
        nothing = jnp.where(jnp.arange(2 * lanes)[None] == hd + clips, 1.0, 0.0).astype(low)
        kv = qkv[:, lanes:]
        slots = kv.reshape(heads, 2, rows, 2 * lanes)
        before = at.send(slots[:, 1].reshape(span, 2 * lanes), ahead)
        after = at.send(slots[:, 0].reshape(span, 2 * lanes), behind)
        before = jnp.where(at.me < at.block, nothing, before)
        after = jnp.where(at.me >= at.count - at.block, nothing, after)
        kv = jnp.concatenate([before, kv, after], axis=0)
        qkv_at = (qkv, 0, kv, 0, kv, 1)
    o_head, lse = attend(*qkv_at, hd, step_rows)
    o_head, lse, lower, w1 = together(o_head, lse, lower, w1)
    w1 = w1.reshape(width, ff)
    g_kept = lax.dynamic_index_in_dim(cotangent, at.mine, 0, False)
    g_own = jnp.concatenate(at.ordered(g_kept, lower[:rows]), axis=0)
    w2 = jnp.concatenate(at.ordered(at.to_block(w_fc2), lower[rows:]), axis=0)
    g_all = at.gather_half(g_own)
    o_own = at.exchange_half(o_head)

    x2, *parts = join(x_own, o_own, wo, table)
    mine, others = at.gather_tree(parts)

    g_split = g_all.reshape(8, 2, own, width)
    *before, kept, sum_c = feed(place, False, mine, g_split, w1, w2, c1, (), own, exact)
    hid, du, away, sum_c2 = feed(place, True, others, g_split, w1, w2, c1, before, own, low)
    marks, terms_w1 = [], []
    low_hid, low_du = hid.reshape(tokens, ff), du.reshape(tokens, ff)

    def output_terms(marks):
        late = tie(low_hid, marks[0])
        terms_w1.append(dot(late, w2, 1, 0).astype(low))
        terms_w1.append(assemble(place, (tie(mine[0], marks[0]), *mine[1:]), others, own))
        return terms_w1

    def hidden_terms(marks):
        terms_w1.append(dot(tie(terms_w1[1], marks[1]).reshape(tokens, width), low_du, 0, 0).astype(low))
        return terms_w1[2:]

    kept, got = at.reduce_half(away, kept, marks, {1: output_terms, 2: hidden_terms})
    y = lax.psum_scatter(terms_w1[0], "dev", scatter_dimension=0, tiled=True, axis_index_groups=at.halves)
    d_w1 = at.exchange_block(terms_w1[2].reshape(at.block, chunk, ff))
    d_w2 = dot(tie(low_hid, marks[2]), g_all.reshape(tokens, width), 0, 0).astype(low)
    *sums, d_w2 = together(*kept, *got, d_w2)
    kept, got = sums[:3], sums[3:]

    dx2, ga_own, do_own, sum2 = second_back(kept, got, x2, g_own, table, wo, hd)
    do_head = at.exchange_half(do_own)
    ga_sent, d_w2 = together(ga_own, d_w2, do_own)[:2]
    ga = at.gather_half(ga_sent).reshape(tokens, width)
    do_head, d_w1, d_w2 = together(do_head, d_w1, d_w2)
    back_w2 = at.exchanged(d_w2.reshape(2, -1, width))

    kind = low if at.blocks == 1 else exact
    dqkv, sum_in = attend_back(*qkv_at, do_head, lse, hd, step_rows, span, kind)
    if at.blocks > 1:
        dkv = dqkv[:, lanes:]
        to_before = at.send(dkv[:span].astype(low), behind).astype(exact)
        to_after = at.send(dkv[span + tokens :].astype(low), ahead).astype(exact)
        halo = jnp.stack([t.reshape(heads, rows, 2 * lanes) for t in (to_after, to_before)], axis=1)
        dkv = dkv[span : span + tokens] + halo.reshape(tokens, 2 * lanes)
        dqkv = jnp.concatenate([dqkv[span : span + tokens, :lanes], dkv], axis=1).astype(low)
        sum_in = jnp.broadcast_to(jnp.sum(dqkv.astype(exact), axis=0, keepdims=True), (8, 3 * lanes))
    dqkv, sum_in, *back_w2 = together(dqkv, sum_in, *back_w2)
    split = dqkv.reshape(8, 2, own, 3 * lanes)
    w_pad = jnp.pad(w_in.reshape(width, 3, hd), ((0, 0), (0, 0), (0, lanes - hd))).reshape(width, 3 * lanes)
    away = terms(place, True, split, w_pad, 1, low)
    marks = []
    store = []

    def projections(marks):
        late = tie(dqkv, away)
        store.append(lay_out(place, dot(a1, late, 0, 0), sum2, sum_in, sum_c, sum_c2, hd, chunk, at.block))
        return store

    kept, got = at.reduce_half(away, terms(place, False, split, w_pad, 1, exact), marks, {0: projections})
    ga, o_late, y = together(ga, o_head, y, marks[1])[:3]

    d_in = at.exchange_block(store[0])
    d_wo = jnp.einsum("ckt,ctn->kn", o_late, ga.reshape(at.half, own, width), preferred_element_type=exact)
    back_wo = at.send_rows_back(d_wo.astype(low).reshape(2, chunk, width))
    layer_out = at.exchanged((x2 + (y.astype(exact) + table[7])).astype(low).reshape(2, rows, width))
    kept_first, d_in, *moved = together(kept[0], d_in, *back_wo, *layer_out)
    kept = (kept_first, *kept[1:])
    back_wo, layer_out = moved[:2], moved[2:]
    grad_w2 = at.from_block(back_w2[0].astype(exact) + back_w2[1].astype(exact))
    grad_w1 = at.from_block(collect_hidden(d_w1))
    grad_wo = at.from_block(back_wo[0].astype(exact) + back_wo[1].astype(exact))
    *grads, vec = collect(d_in, hd, chunk)
    grad_wq, grad_wk, grad_wv = (at.from_block(v) for v in grads)
    pieces = [at.from_block(vec[i, :chunk]) for i in range(6)]
    grad_g2, grad_b2, grad_bo, grad_bf2, grad_bq, grad_bv = pieces
    grad_c1 = at.from_block(vec[0, chunk : chunk + ff_rows])

    dx, vec = first_back(kept, got, x_own, dx2, table, chunk, at.block)
    input_grad = at.exchanged(dx.reshape(2, rows, width))
    layer_out, input_grad = (jnp.stack(at.ordered(*v)).astype(exact) for v in (layer_out, input_grad))
    vec = jnp.sum(at.exchange_block(vec), axis=(0, 1))
    grad_g1 = at.from_block(vec[:chunk])
    grad_b1 = at.from_block(vec[lanes // 2 : lanes // 2 + chunk])
    return (
        layer_out,
        input_grad,
        grad_g1,
        grad_b1,
        grad_wq,
        grad_bq,
        grad_wk,
        grad_wv,
        grad_bv,
        grad_wo,
        grad_bo,
        grad_g2,
        grad_b2,
        grad_w1,
        grad_c1,
        grad_w2,
        grad_bf2,
    )


def solution(mesh):
    tokens, vector, matrix = P(None, "dev", None), P("dev"), P("dev", None)
    grads = (vector, vector, matrix, vector, matrix, matrix, vector, matrix, vector, vector, vector, matrix, vector, matrix, vector)
    return jax.shard_map(
        body,
        mesh=mesh,
        in_specs=(tokens, P()) + grads + (tokens,),
        out_specs=(tokens, tokens) + grads,
        check_vma=False,
    )
```

time: 577 us -> 459 us (0.80)
  Pallas kernels: 27.1 us -> 98.6 us
  waiting for transfers between devices: 203 us -> 137 us
  matrix products: 70.3 us -> 16.9 us
  local copies, waits for them, and re-layouts: 88.7 us -> 43.3 us
  other arithmetic: 51.8 us -> 14.6 us
  blocking collectives: 0 us -> 27.5 us
  starting transfers between devices: 113 us -> 99.6 us
    pallas_call x1 -> x26, Pallas kernels: 15.9 us -> 87.1 us  [the longest x2 20.7 us: feed(): pl.pallas_call(feed_kernel, grid_spec=pltpu.PrefetchScalarGridSpec(num_sc...]
    all_to_all x4, waiting for transfers between devices: 59.4 us -> 2.41 us  [exchange_block(): lax.all_to_all(value, 'dev', 0, 0, tiled=True, axis_index_groups=self.whole)]
    dot_general x14 -> x4, matrix products: 66.7 us -> 13.2 us  [dot(): lax.dot_general(a, b, (((ca,), (cb,)), ((), ())), preferred_element_type=...]
    all_gather x5 -> x3, waiting for transfers between devices: 35.9 us -> 0.02 us  [gather_half(): return lax.all_gather(value, 'dev', axis=0, axis_index_groups=self.halves)]
    all_to_all x4, starting transfers between devices: 47.8 us -> 19 us  [exchange_block(): lax.all_to_all(value, 'dev', 0, 0, tiled=True, axis_index_groups=self.whole)]
    all_to_all x0 -> x1, blocking collectives: none -> 27.5 us  [exchange_block(): lax.all_to_all(value, 'dev', 0, 0, tiled=True, axis_index_groups=self.whole)]
    ppermute x40 -> x58, waiting for transfers between devices: 95 us -> 120 us  [send(): return lax.ppermute(value, 'dev', pairs)]
    slice x31 -> x4, local copies, waits for them, and re-layouts: 20.4 us -> 1.25 us  [the longest x1 0.63 us: body(): grad_c1 = at.from_block(vec[0, chunk:chunk + ff_rows])]
  transfers between devices with their start and end apart: 51 -> 68, of which waited for: 31 -> 31; matrix products, arithmetic and copies ran while one was open for 28% -> 10% of each run, Pallas kernels for 2% -> 18%
where the time goes in v2:
time: 459 us; the launch traced here: 452 us
  waiting for transfers between devices  137 us (30%)
  starting transfers between devices  99.6 us (22%)
  Pallas kernels  98.6 us (21%)
  local copies, waits for them, and re-layouts  43.3 us (9%)
  blocking collectives  27.5 us (6%)
  matrix products  16.9 us (4%)
  between operations  15 us (3%)
  other arithmetic  14.6 us (3%)
    ppermute x58, waiting for transfers between devices, send(): return lax.ppermute(value, 'dev', pairs)  120 us
    ppermute x58, starting transfers between devices, send(): return lax.ppermute(value, 'dev', pairs)  71.7 us
    all_to_all x1, blocking collectives, exchange_block(): lax.all_to_all(value, 'dev', 0, 0, tiled=True, axis_index_groups=self.whole)  27.5 us
    unnamed x139, local copies, waits for them, and re-layouts  24.3 us
    pallas_call x2, Pallas kernels, feed(): pl.pallas_call(feed_kernel, grid_spec=pltpu.PrefetchScalarGridSpec(num_sc...  20.7 us
    all_to_all x4, starting transfers between devices, exchange_block(): lax.all_to_all(value, 'dev', 0, 0, tiled=True, axis_index_groups=self.whole)  19 us
    pallas_call x1, Pallas kernels, attend_back(): pl.pallas_call(functools.partial(attend_back_kernel, hd, coef, scale, spa...  19 us
    pallas_call x2, Pallas kernels, project(): pl.pallas_call(functools.partial(project_kernel, hd, clips, chunk, not be...  14.4 us
  transfers between devices with their start and end apart: 68, of which 31 were waited for; matrix products, arithmetic and copies ran while one was open for 10% of the time, Pallas kernels for 18%

profile of v2, /device:TPU:0, one launch (start us, length us, event | category | flops | bytes accessed | tf_op | source)
XLA Modules:
  0.0 452.4 jit_solution(12695938050112227196)
XLA Ops:
  11.4 4.1 collective-permute-start
  25.1 3.3 collective-permute-done.second_ref
  30.5 5.8 %all-to-all-start = ((bf16[32,40,240]{2,1,0:T(8,128)(2,1)}), bf16[32,40,240]{2,1,0:T(8,128)(2,1)S(1)}, u32[]{:S(2)}, u32[]{:S(2)}) async-start(bf16[32,40,240]{2,1,0:T(8,128)(2,1)} %pad_maximum_fusion.2), calls=%async_computation | async-start | bytes 1310720 | tf_op jit(solution)/shard_map/all_to_all | solution.py:106
  37.6 1.8 collective-permute-start.4
  42.3 15.5 %collective-permute-done.2.refs_3_ = bf16[1,48,1280]{2,1,0:T(8,128)(2,1)S(1)} collective-permute-done((bf16[1,48,1280]{2,1,0:T(8,128)(2,1)S(1)}, bf16[1,48,1280]{2,1,0:T(8,128)(2,1)S(1)}, u32[]{:S(2)}, u32[]{:S(2)}) %collective-permute-start.2) | collective-permute-done | bytes 122912 | tf_op jit(solution)/shard_map/ppermute | solution.py:67
  58.5 2.9 collective-permute-start.5
  61.5 5.4 %collective-permute-done.5.refs_3_ = bf16[2,48,1280]{2,1,0:T(8,128)(2,1)S(1)} collective-permute-done((bf16[2,48,1280]{2,1,0:T(8,128)(2,1)S(1)}, bf16[2,48,1280]{2,1,0:T(8,128)(2,1)S(1)}, u32[]{:S(2)}, u32[]{:S(2)}) %collective-permute-start.5) | collective-permute-done | bytes 245792 | tf_op jit(solution)/shard_map/ppermute | solution.py:67
  66.8 7.3 %collective-permute-done.6.refs_4_ = bf16[2,48,1280]{2,1,0:T(8,128)(2,1)S(1)} collective-permute-done((bf16[2,48,1280]{2,1,0:T(8,128)(2,1)S(1)}, bf16[2,48,1280]{2,1,0:T(8,128)(2,1)S(1)}, u32[]{:S(2)}, u32[]{:S(2)}) %collective-permute-start.6) | collective-permute-done | bytes 245792 | tf_op jit(solution)/shard_map/ppermute | solution.py:67
  74.9 4.6 %all-to-all-start.1 = ((bf16[32,40,320]{2,1,0:T(8,128)(2,1)}), bf16[32,40,320]{2,1,0:T(8,128)(2,1)}, u32[]{:S(2)}, u32[]{:S(2)}) async-start(bf16[32,40,320]{2,1,0:T(8,128)(2,1)} %pad_maximum_fusion), calls=%async_computation.1 | async-start | bytes 1966080 | tf_op jit(solution)/shard_map/all_to_all | solution.py:106
  79.8 1.8 collective-permute-start.15
  85.0 18.1 %collective-permute-done.11.refs_3_ = bf16[4,48,1280]{2,1,0:T(8,128)(2,1)} collective-permute-done((bf16[4,48,1280]{2,1,0:T(8,128)(2,1)S(1)}, bf16[4,48,1280]{2,1,0:T(8,128)(2,1)}, u32[]{:S(2)}, u32[]{:S(2)}) %collective-permute-start.11) | collective-permute-done | bytes 491552 | tf_op jit(solution)/shard_map/ppermute | solution.py:67
  103.2 3.7 collective-permute-done.15.refs_5_
  106.9 1.9 collective-permute-done.13.refs_4_
  108.8 2.4 collective-permute-start.17
  116.3 8.0 %project.2 = (bf16[8,2,128,1280]{3,2,1,0:T(8,128)(2,1)}, bf16[8,2,128,384]{3,2,1,0:T(8,128)(2,1)}, f32[8,1280]{1,0:T(8,128)S(1)}) custom-call(s32[7]{0:T(128)S(1)} %stack.88.place_ref, bf16[4,48,1280]{2,1,0:T(8,128)(2,1)S(1)} %get-tuple-element.158.refs_0_, bf16[4,48,1280]{2,1,0:T(8,128)(2,1)S(1)} %copy-done.23, ...), custom_call_target="tpu_custom_call" | custom-call | flops 1024 | bytes 1024 | tf_op jit(solution)/shard_map/project/pallas_call | solution.py:376
  124.4 6.4 %project.3 = (bf16[8,2,128,1280]{3,2,1,0:T(8,128)(2,1)}, bf16[8,2,128,384]{3,2,1,0:T(8,128)(2,1)}, f32[8,1280]{1,0:T(8,128)S(1)}) custom-call(s32[7]{0:T(128)S(1)} %stack.88.place_ref, bf16[4,48,1280]{2,1,0:T(8,128)(2,1)S(1)} %copy-done.25, bf16[4,48,1280]{2,1,0:T(8,128)(2,1)S(1)} %copy-done.27, ...), custom_call_target="tpu_custom_call", output_to_operand_aliasing={{0}: (10, {}), {1}: (11, {})} | custom-call | flops 1024 | bytes 1024 | tf_op jit(solution)/shard_map/project/pallas_call | solution.py:376
  132.2 11.5 %attend.1 = (bf16[16,80,128]{2,1,0:T(8,128)(2,1)}, f32[8,1,256]{2,1,0:T(1,128)S(1)}) custom-call(bf16[2048,384]{1,0:T(8,128)(2,1)S(1)} %bitcast.114, bf16[2048,384]{1,0:T(8,128)(2,1)S(1)} %bitcast.115, bf16[2048,384]{1,0:T(8,128)(2,1)S(1)} %bitcast.116), custom_call_target="tpu_custom_call" | custom-call | flops 1024 | bytes 1024 | tf_op jit(solution)/shard_map/attend/pallas_call | solution.py:698
  145.4 4.2 all-to-all-start.2
  150.0 2.2 copy.64
  152.1 6.0 %all-to-all-done.2.o_ref = bf16[16,80,128]{2,1,0:T(8,128)(2,1)} async-done(((bf16[16,80,128]{2,1,0:T(8,128)(2,1)}), bf16[16,80,128]{2,1,0:T(8,128)(2,1)}, u32[]{:S(2)}, u32[]{:S(2)}) %all-to-all-start.2) | async-done | bytes 327712 | tf_op jit(solution)/shard_map/all_to_all | solution.py:103
  159.1 1.9 join.1
  164.4 2.2 collective-permute-start.20
  166.7 4.4 collective-permute-done.20.refs_5_
  172.4 2.9 collective-permute-start.22
  176.7 8.0 %collective-permute-done.23.refs_5_ = bf16[2,32,1280]{2,1,0:T(8,128)(2,1)S(1)} collective-permute-done((bf16[2,32,1280]{2,1,0:T(8,128)(2,1)S(1)}, bf16[2,32,1280]{2,1,0:T(8,128)(2,1)S(1)}, u32[]{:S(2)}, u32[]{:S(2)}) %collective-permute-start.23) | collective-permute-done | bytes 163872 | tf_op jit(solution)/shard_map/ppermute | solution.py:67
  184.8 1.8 collective-permute-done.22.refs_4_
  187.9 2.0 collective-permute-start.24
  192.8 5.5 %collective-permute-done.26.refs_5_ = bf16[4,32,1280]{2,1,0:T(8,128)(2,1)} collective-permute-done((bf16[4,32,1280]{2,1,0:T(8,128)(2,1)}, bf16[4,32,1280]{2,1,0:T(8,128)(2,1)}, u32[]{:S(2)}, u32[]{:S(2)}) %collective-permute-start.26) | collective-permute-done | bytes 327712 | tf_op jit(solution)/shard_map/ppermute | solution.py:67
  203.9 10.5 %feed.2 = (bf16[8,2,128,320]{3,2,1,0:T(8,128)(2,1)}, bf16[8,2,128,320]{3,2,1,0:T(8,128)(2,1)}, f32[8,128,1280]{2,1,0:T(8,128)}, f32[1,320]{1,0:T(1,128)}) custom-call(s32[7]{0:T(128)} %copy-done.37, bf16[4,48,1280]{2,1,0:T(8,128)(2,1)} %get-tuple-element.197.refs_0_, bf16[4,48,1280]{2,1,0:T(8,128)(2,1)} %get-tuple-element.183.refs_1_, ...), custom_call_target="tpu_custom_call" | custom-call | flops 1024 | bytes 1024 | tf_op jit(solution)/shard_map/feed/pallas_call | solution.py:486
  214.4 10.1 %feed.3 = (bf16[8,2,128,320]{3,2,1,0:T(8,128)(2,1)}, bf16[8,2,128,320]{3,2,1,0:T(8,128)(2,1)}, bf16[8,128,1280]{2,1,0:T(8,128)(2,1)}, f32[1,320]{1,0:T(1,128)}) custom-call(s32[7]{0:T(128)} %copy-done.37, bf16[4,48,1280]{2,1,0:T(8,128)(2,1)} %collective-permute-done.27.refs_0_.refs_6_, ...), custom_call_target="tpu_custom_call", output_to_operand_aliasing={{0}: (11, {}), {1}: (12, {})} | custom-call | flops 1024 | bytes 1024 | tf_op jit(solution)/shard_map/feed/pallas_call | solution.py:486
  225.1 4.7 %collective-permute-done.33.refs_1_ = bf16[8,128,1280]{2,1,0:T(8,128)(2,1)S(1)} collective-permute-done((bf16[8,128,1280]{2,1,0:T(8,128)(2,1)}, bf16[8,128,1280]{2,1,0:T(8,128)(2,1)S(1)}, u32[]{:S(2)}, u32[]{:S(2)}) %collective-permute-start.33) | collective-permute-done | bytes 2621472 | tf_op jit(solution)/shard_map/ppermute | solution.py:67
  229.8 2.5 copy-done.6
  232.3 1.9 split_terms.6
  238.7 4.6 %convolution_convert_fusion = bf16[2048,1280]{1,0:T(8,128)(2,1)} fusion(bf16[2048,320]{1,0:T(8,128)(2,1)S(1)} %bitcast.139, bf16[160,1280]{1,0:T(8,128)(2,1)S(1)} %copy-done.52, bf16[160,1280]{1,0:T(8,128)(2,1)S(1)} %copy-done.50), kind=kOutput, calls=%fused_computation | convolution fusion | flops 1681981440 | bytes 7372800 | tf_op jit(solution)/shard_map/dot_general | solution.py:21
  246.5 4.1 assemble.1
  250.6 11.3 %collective-permute-done.34.refs_3_ = bf16[4,48,1280]{2,1,0:T(8,128)(2,1)S(1)} collective-permute-done((bf16[4,48,1280]{2,1,0:T(8,128)(2,1)}, bf16[4,48,1280]{2,1,0:T(8,128)(2,1)S(1)}, u32[]{:S(2)}, u32[]{:S(2)}) %collective-permute-start.34) | collective-permute-done | bytes 491552 | tf_op jit(solution)/shard_map/ppermute | solution.py:67
  264.1 2.3 collective-permute-start.37
  267.7 2.9 fusion
  270.6 3.3 collective-permute-done.37.refs_3_
  273.9 4.9 %collective-permute-done.38.refs_4_ = bf16[2,48,1280]{2,1,0:T(8,128)(2,1)S(1)} collective-permute-done((bf16[2,48,1280]{2,1,0:T(8,128)(2,1)S(1)}, bf16[2,48,1280]{2,1,0:T(8,128)(2,1)S(1)}, u32[]{:S(2)}, u32[]{:S(2)}) %collective-permute-start.38) | collective-permute-done | bytes 245792 | tf_op jit(solution)/shard_map/ppermute | solution.py:67
  279.7 2.5 collective-permute-start.40
  282.8 2.8 convolution_convert_fusion.1
  285.6 2.3 collective-permute-done.42.refs_5_
  292.0 3.6 all-to-all-start.3
  297.2 8.4 %all-to-all-done.3.do_ref = bf16[16,80,128]{2,1,0:T(8,128)(2,1)S(1)} async-done(((bf16[16,80,128]{2,1,0:T(8,128)(2,1)}), bf16[16,80,128]{2,1,0:T(8,128)(2,1)S(1)}, u32[]{:S(2)}, u32[]{:S(2)}) %all-to-all-start.3) | async-done | bytes 327712 | tf_op jit(solution)/shard_map/all_to_all | solution.py:103
  305.5 27.5 %all_to_all.35.in_ref = bf16[32,40,320]{2,1,0:T(8,128)(2,1)S(1)} all-to-all(bf16[32,40,320]{2,1,0:T(8,128)(2,1)S(1)} %bitcast.135), channel_id=1, replica_groups={{0,1,2,3,4,5,6,7,8,9,10,11,12,13,14,15,16,17,18,19,20,21,22,23,24,25,26..., dimensions={0} | all-to-all | bytes 1638400 | tf_op jit(solution)/shard_map/all_to_all | solution.py:106
  333.0 2.1 dynamic-slice_bitcast_fusion
  338.8 19.0 %attend_back.1 = (bf16[2048,384]{1,0:T(8,128)(2,1)}, f32[8,384]{1,0:T(8,128)}) custom-call(bf16[2048,384]{1,0:T(8,128)(2,1)} %bitcast.111, bf16[2048,384]{1,0:T(8,128)(2,1)} %bitcast.112, bf16[2048,384]{1,0:T(8,128)(2,1)} %bitcast.113, bf16[16,80,128]{2,1,0:T(8,128)(2,1)} %copy-done.56, f32[8,1,256]{2,1,0:T(1,128)} %copy-done.41), custom_call_target="tpu_custom_call" | custom-call | flops 1024 | bytes 1024 | tf_op jit(solution)/shard_map/attend_back/pallas_call | solution.py:765
  359.2 2.8 terms.3
  362.6 2.8 terms.2.refs_0_
  365.5 2.9 fusion.6.in_ref
  368.5 1.8 lay_out.1
  370.3 1.9 split_terms.9
  375.9 8.1 %collective-permute-done.47.refs_5_ = bf16[4,32,1280]{2,1,0:T(8,128)(2,1)S(1)} collective-permute-done((bf16[4,32,1280]{2,1,0:T(8,128)(2,1)S(1)}, bf16[4,32,1280]{2,1,0:T(8,128)(2,1)S(1)}, u32[]{:S(2)}, u32[]{:S(2)}) %collective-permute-start.47) | collective-permute-done | bytes 327712 | tf_op jit(solution)/shard_map/ppermute | solution.py:67
  386.1 1.9 split_terms.10
  393.5 3.4 all-to-all-start.5
  397.7 2.4 split_terms.11
  405.5 3.7 fusion.1
  411.5 3.7 collective-permute-start.53
  415.2 8.3 %collective-permute-start.52 = (bf16[40,1280]{1,0:T(8,128)(2,1)}, bf16[40,1280]{1,0:T(8,128)(2,1)S(1)}, u32[]{:S(2)}, u32[]{:S(2)}) collective-permute-start(bf16[40,1280]{1,0:T(8,128)(2,1)} %get-tuple-element.291), channel_id=1, source_target_pairs={{0,1},{1,3},{2,5},{3,7},{4,9},{5,11},{6,13},{7,15},{8,17},{9,19},{... | collective-permute-start | bytes 307208 | tf_op jit(solution)/shard_map/ppermute | solution.py:67
  423.5 2.0 convert_add_fusion
  425.5 3.4 collective-permute-done.52
  431.6 5.2 %all-to-all-start.6 = ((f32[32,1,128]{2,1,0:T(1,128)}), f32[32,1,128]{2,1,0:T(1,128)S(1)}, u32[]{:S(2)}, u32[]{:S(2)}) async-start(f32[32,1,128]{2,1,0:T(1,128)} %get-tuple-element.268), calls=%async_computation.7 | async-start | bytes 32768 | tf_op jit(solution)/shard_map/all_to_all | solution.py:106
  441.7 2.4 all-to-all-done.6
  (303 shorter events, 103.8 us)
Async XLA Ops:
  7.2 142.8 %all-gather.7.cloned.1.call-start = ((), (), s32[]{:S(2)}) async-start(), calls=%async_computation.9 | async-start | bytes 3481600 | tf_op jit(solution)/shard_map/all_gather | solution.py:100
  11.4 17.1 %collective-permute-start = (bf16[112,1280]{1,0:T(8,128)(2,1)S(1)}, bf16[112,1280]{1,0:T(8,128)(2,1)S(1)}, u32[]{:S(2)}, u32[]{:S(2)}) collective-permute-start(bf16[112,1280]{1,0:T(8,128)(2,1)S(1)} %get-tuple-element.149), channel_id=1, source_target_pairs={{0,16},{1,17},{2,18},{3,19},{4,20},{5,21},{6,22},{7,23},{8,24},{9,... | collective-permute-start | bytes 860168 | tf_op jit(solution)/shard_map/ppermute | solution.py:67
  30.5 44.5 %all-to-all-start = ((bf16[32,40,240]{2,1,0:T(8,128)(2,1)}), bf16[32,40,240]{2,1,0:T(8,128)(2,1)S(1)}, u32[]{:S(2)}, u32[]{:S(2)}) async-start(bf16[32,40,240]{2,1,0:T(8,128)(2,1)} %pad_maximum_fusion.2), calls=%async_computation | async-start | bytes 1310720 | tf_op jit(solution)/shard_map/all_to_all | solution.py:106
  37.6 20.2 %collective-permute-start.4 = (bf16[1,64,1280]{2,1,0:T(8,128)(2,1)S(1)}, bf16[1,64,1280]{2,1,0:T(8,128)(2,1)S(1)}, u32[]{:S(2)}, u32[]{:S(2)}) collective-permute-start(bf16[1,64,1280]{2,1,0:T(8,128)(2,1)S(1)} %pad_maximum_fusion.5.refs_2_), channel_id=1, source_target_pairs={{0,2},{1,3},{2,0},{3,1},{4,6},{5,7},{6,4},{7,5},{8,10},{9,11},{10,... | collective-permute-start | bytes 491528 | tf_op jit(solution)/shard_map/ppermute | solution.py:67
  39.4 18.4 %collective-permute-start.2 = (bf16[1,48,1280]{2,1,0:T(8,128)(2,1)S(1)}, bf16[1,48,1280]{2,1,0:T(8,128)(2,1)S(1)}, u32[]{:S(2)}, u32[]{:S(2)}) collective-permute-start(bf16[1,48,1280]{2,1,0:T(8,128)(2,1)S(1)} %get-tuple-element.151.refs_0_), channel_id=1, source_target_pairs={{0,8},{1,9},{2,10},{3,11},{4,12},{5,13},{6,14},{7,15},{8,0},{9,1},... | collective-permute-start | bytes 368648 | tf_op jit(solution)/shard_map/ppermute | solution.py:67
  40.9 16.9 %collective-permute-start.3 = (bf16[1,48,1280]{2,1,0:T(8,128)(2,1)S(1)}, bf16[1,48,1280]{2,1,0:T(8,128)(2,1)S(1)}, u32[]{:S(2)}, u32[]{:S(2)}) collective-permute-start(bf16[1,48,1280]{2,1,0:T(8,128)(2,1)S(1)} %get-tuple-element.152.refs_1_), channel_id=1, source_target_pairs={{0,4},{1,5},{2,6},{3,7},{4,0},{5,1},{6,2},{7,3},{8,12},{9,13},{10,... | collective-permute-start | bytes 368648 | tf_op jit(solution)/shard_map/ppermute | solution.py:67
  58.1 16.3 %collective-permute-start.7 = (bf16[2,64,1280]{2,1,0:T(8,128)(2,1)S(1)}, bf16[2,64,1280]{2,1,0:T(8,128)(2,1)S(1)}, u32[]{:S(2)}, u32[]{:S(2)}) collective-permute-start(bf16[2,64,1280]{2,1,0:T(8,128)(2,1)S(1)} %get-tuple-element.157.refs_2_), channel_id=1, source_target_pairs={{0,8},{1,9},{2,10},{3,11},{4,12},{5,13},{6,14},{7,15},{8,0},{9,1},... | collective-permute-start | bytes 983048 | tf_op jit(solution)/shard_map/ppermute | solution.py:67
  58.5 8.3 %collective-permute-start.5 = (bf16[2,48,1280]{2,1,0:T(8,128)(2,1)S(1)}, bf16[2,48,1280]{2,1,0:T(8,128)(2,1)S(1)}, u32[]{:S(2)}, u32[]{:S(2)}) collective-permute-start(bf16[2,48,1280]{2,1,0:T(8,128)(2,1)S(1)} %get-tuple-element.155.refs_0_), channel_id=1, source_target_pairs={{0,4},{1,5},{2,6},{3,7},{4,0},{5,1},{6,2},{7,3},{8,12},{9,13},{10,... | collective-permute-start | bytes 737288 | tf_op jit(solution)/shard_map/ppermute | solution.py:67
  61.5 12.7 %collective-permute-start.6 = (bf16[2,48,1280]{2,1,0:T(8,128)(2,1)S(1)}, bf16[2,48,1280]{2,1,0:T(8,128)(2,1)S(1)}, u32[]{:S(2)}, u32[]{:S(2)}) collective-permute-start(bf16[2,48,1280]{2,1,0:T(8,128)(2,1)S(1)} %get-tuple-element.156.refs_1_), channel_id=1, source_target_pairs={{0,2},{1,3},{2,0},{3,1},{4,6},{5,7},{6,4},{7,5},{8,10},{9,11},{10,... | collective-permute-start | bytes 737288 | tf_op jit(solution)/shard_map/ppermute | solution.py:67
  74.9 68.7 %all-to-all-start.1 = ((bf16[32,40,320]{2,1,0:T(8,128)(2,1)}), bf16[32,40,320]{2,1,0:T(8,128)(2,1)}, u32[]{:S(2)}, u32[]{:S(2)}) async-start(bf16[32,40,320]{2,1,0:T(8,128)(2,1)} %pad_maximum_fusion), calls=%async_computation.1 | async-start | bytes 1966080 | tf_op jit(solution)/shard_map/all_to_all | solution.py:106
  79.6 124.3 %all-gather.9.cloned.1.call-start = ((), (), s32[]{:S(2)}) async-start(), calls=%async_computation.10 | async-start | bytes 5570560 | tf_op jit(solution)/shard_map/all_gather | solution.py:100
  79.8 27.1 %collective-permute-start.15 = (bf16[4,64,1280]{2,1,0:T(8,128)(2,1)S(1)}, bf16[4,64,1280]{2,1,0:T(8,128)(2,1)S(1)}, u32[]{:S(2)}, u32[]{:S(2)}) collective-permute-start(bf16[4,64,1280]{2,1,0:T(8,128)(2,1)S(1)} %get-tuple-element.160.refs_2_), channel_id=1, source_target_pairs={{0,4},{1,5},{2,6},{3,7},{4,0},{5,1},{6,2},{7,3},{8,12},{9,13},{10,... | collective-permute-start | bytes 1966088 | tf_op jit(solution)/shard_map/ppermute | solution.py:67
  81.6 21.6 %collective-permute-start.11 = (bf16[4,48,1280]{2,1,0:T(8,128)(2,1)S(1)}, bf16[4,48,1280]{2,1,0:T(8,128)(2,1)}, u32[]{:S(2)}, u32[]{:S(2)}) collective-permute-start(bf16[4,48,1280]{2,1,0:T(8,128)(2,1)S(1)} %get-tuple-element.158.refs_0_), channel_id=1, source_target_pairs={{0,2},{1,3},{2,0},{3,1},{4,6},{5,7},{6,4},{7,5},{8,10},{9,11},{10,... | collective-permute-start | bytes 1474568 | tf_op jit(solution)/shard_map/ppermute | solution.py:67
  83.1 25.7 %collective-permute-start.13 = (bf16[4,48,1280]{2,1,0:T(8,128)(2,1)S(1)}, bf16[4,48,1280]{2,1,0:T(8,128)(2,1)}, u32[]{:S(2)}, u32[]{:S(2)}) collective-permute-start(bf16[4,48,1280]{2,1,0:T(8,128)(2,1)S(1)} %get-tuple-element.159.refs_1_), channel_id=1, source_target_pairs={{0,8},{1,9},{2,10},{3,11},{4,12},{5,13},{6,14},{7,15},{8,0},{9,1},... | collective-permute-start | bytes 1474568 | tf_op jit(solution)/shard_map/ppermute | solution.py:67
  84.5 26.6 %collective-permute-start.8 = (bf16[4,48,1280]{2,1,0:T(8,128)(2,1)S(1)}, bf16[4,48,1280]{2,1,0:T(8,128)(2,1)S(1)}, u32[]{:S(2)}, u32[]{:S(2)}) collective-permute-start(bf16[4,48,1280]{2,1,0:T(8,128)(2,1)S(1)} %get-tuple-element.158.refs_0_), channel_id=1, source_target_pairs={{0,1},{1,0},{2,3},{3,2},{4,5},{5,4},{6,7},{7,6},{8,9},{9,8},{10,11... | collective-permute-start | bytes 1474568 | tf_op jit(solution)/shard_map/ppermute | solution.py:67
  84.5 27.4 %collective-permute-start.9 = (bf16[4,48,1280]{2,1,0:T(8,128)(2,1)S(1)}, bf16[4,48,1280]{2,1,0:T(8,128)(2,1)S(1)}, u32[]{:S(2)}, u32[]{:S(2)}) collective-permute-start(bf16[4,48,1280]{2,1,0:T(8,128)(2,1)S(1)} %get-tuple-element.159.refs_1_), channel_id=1, source_target_pairs={{0,1},{1,0},{2,3},{3,2},{4,5},{5,4},{6,7},{7,6},{8,9},{9,8},{10,11... | collective-permute-start | bytes 1474568 | tf_op jit(solution)/shard_map/ppermute | solution.py:67
  103.2 21.2 %collective-permute-start.10 = (bf16[4,64,1280]{2,1,0:T(8,128)(2,1)S(1)}, bf16[4,64,1280]{2,1,0:T(8,128)(2,1)}, u32[]{:S(2)}, u32[]{:S(2)}) collective-permute-start(bf16[4,64,1280]{2,1,0:T(8,128)(2,1)S(1)} %get-tuple-element.160.refs_2_), channel_id=1, source_target_pairs={{0,1},{1,0},{2,3},{3,2},{4,5},{5,4},{6,7},{7,6},{8,9},{9,8},{10,11... | collective-permute-start | bytes 1966088 | tf_op jit(solution)/shard_map/ppermute | solution.py:67
  106.9 17.4 %collective-permute-start.16 = (bf16[4,64,1280]{2,1,0:T(8,128)(2,1)S(1)}, bf16[4,64,1280]{2,1,0:T(8,128)(2,1)}, u32[]{:S(2)}, u32[]{:S(2)}) collective-permute-start(bf16[4,64,1280]{2,1,0:T(8,128)(2,1)S(1)} %collective-permute-done.15.refs_5_), channel_id=1, source_target_pairs={{0,1},{1,0},{2,3},{3,2},{4,5},{5,4},{6,7},{7,6},{8,9},{9,8},{10,11... | collective-permute-start | bytes 1966088 | tf_op jit(solution)/shard_map/ppermute | solution.py:67
  108.8 34.9 %collective-permute-start.17 = (bf16[224,1280]{1,0:T(8,128)(2,1)}, bf16[224,1280]{1,0:T(8,128)(2,1)}, u32[]{:S(2)}, u32[]{:S(2)}) collective-permute-start(bf16[224,1280]{1,0:T(8,128)(2,1)} %pad_maximum_fusion.3), channel_id=1, source_target_pairs={{0,16},{1,17},{2,18},{3,19},{4,20},{5,21},{6,22},{7,23},{8,24},{9,... | collective-permute-start | bytes 1720328 | tf_op jit(solution)/shard_map/ppermute | solution.py:67
  111.9 12.4 %collective-permute-start.12 = (bf16[4,48,1280]{2,1,0:T(8,128)(2,1)}, bf16[4,48,1280]{2,1,0:T(8,128)(2,1)}, u32[]{:S(2)}, u32[]{:S(2)}) collective-permute-start(bf16[4,48,1280]{2,1,0:T(8,128)(2,1)} %collective-permute-done.11.refs_3_), channel_id=1, source_target_pairs={{0,1},{1,0},{2,3},{3,2},{4,5},{5,4},{6,7},{7,6},{8,9},{9,8},{10,11... | collective-permute-start | bytes 1474568 | tf_op jit(solution)/shard_map/ppermute | solution.py:67
  112.7 11.6 %collective-permute-start.14 = (bf16[4,48,1280]{2,1,0:T(8,128)(2,1)}, bf16[4,48,1280]{2,1,0:T(8,128)(2,1)}, u32[]{:S(2)}, u32[]{:S(2)}) collective-permute-start(bf16[4,48,1280]{2,1,0:T(8,128)(2,1)} %collective-permute-done.13.refs_4_), channel_id=1, source_target_pairs={{0,1},{1,0},{2,3},{3,2},{4,5},{5,4},{6,7},{7,6},{8,9},{9,8},{10,11... | collective-permute-start | bytes 1474568 | tf_op jit(solution)/shard_map/ppermute | solution.py:67
  145.4 12.7 %all-to-all-start.2 = ((bf16[16,80,128]{2,1,0:T(8,128)(2,1)}), bf16[16,80,128]{2,1,0:T(8,128)(2,1)}, u32[]{:S(2)}, u32[]{:S(2)}) async-start(bf16[16,80,128]{2,1,0:T(8,128)(2,1)} %get-tuple-element.255), calls=%async_computation.2 | async-start | bytes 655360 | tf_op jit(solution)/shard_map/all_to_all | solution.py:103
  149.6 255.8 %reduce-scatter.2.cloned.1.call-start = ((), (), s32[]{:S(2)}) async-start(), calls=%async_computation.8 | async-start | bytes 5570560 | tf_op jit(solution)/shard_map/reduce_scatter | solution.py:900
  161.9 9.2 %collective-permute-start.18 = (bf16[1,48,1280]{2,1,0:T(8,128)(2,1)S(1)}, bf16[1,48,1280]{2,1,0:T(8,128)(2,1)S(1)}, u32[]{:S(2)}, u32[]{:S(2)}) collective-permute-start(bf16[1,48,1280]{2,1,0:T(8,128)(2,1)S(1)} %get-tuple-element.176.refs_0_), channel_id=1, source_target_pairs={{0,8},{1,9},{2,10},{3,11},{4,12},{5,13},{6,14},{7,15},{8,0},{9,1},... | collective-permute-start | bytes 368648 | tf_op jit(solution)/shard_map/ppermute | solution.py:67
  163.0 8.1 %collective-permute-start.19 = (bf16[1,48,1280]{2,1,0:T(8,128)(2,1)S(1)}, bf16[1,48,1280]{2,1,0:T(8,128)(2,1)S(1)}, u32[]{:S(2)}, u32[]{:S(2)}) collective-permute-start(bf16[1,48,1280]{2,1,0:T(8,128)(2,1)S(1)} %get-tuple-element.177.refs_1_), channel_id=1, source_target_pairs={{0,4},{1,5},{2,6},{3,7},{4,0},{5,1},{6,2},{7,3},{8,12},{9,13},{10,... | collective-permute-start | bytes 368648 | tf_op jit(solution)/shard_map/ppermute | solution.py:67
  164.4 6.6 %collective-permute-start.20 = (bf16[1,32,1280]{2,1,0:T(8,128)(2,1)S(1)}, bf16[1,32,1280]{2,1,0:T(8,128)(2,1)S(1)}, u32[]{:S(2)}, u32[]{:S(2)}) collective-permute-start(bf16[1,32,1280]{2,1,0:T(8,128)(2,1)S(1)} %get-tuple-element.178.refs_2_), channel_id=1, source_target_pairs={{0,2},{1,3},{2,0},{3,1},{4,6},{5,7},{6,4},{7,5},{8,10},{9,11},{10,... | collective-permute-start | bytes 245768 | tf_op jit(solution)/shard_map/ppermute | solution.py:67
  171.3 13.5 %collective-permute-start.21 = (bf16[2,48,1280]{2,1,0:T(8,128)(2,1)S(1)}, bf16[2,48,1280]{2,1,0:T(8,128)(2,1)S(1)}, u32[]{:S(2)}, u32[]{:S(2)}) collective-permute-start(bf16[2,48,1280]{2,1,0:T(8,128)(2,1)S(1)} %get-tuple-element.179.refs_0_), channel_id=1, source_target_pairs={{0,4},{1,5},{2,6},{3,7},{4,0},{5,1},{6,2},{7,3},{8,12},{9,13},{10,... | collective-permute-start | bytes 737288 | tf_op jit(solution)/shard_map/ppermute | solution.py:67
  172.4 14.2 %collective-permute-start.22 = (bf16[2,48,1280]{2,1,0:T(8,128)(2,1)S(1)}, bf16[2,48,1280]{2,1,0:T(8,128)(2,1)S(1)}, u32[]{:S(2)}, u32[]{:S(2)}) collective-permute-start(bf16[2,48,1280]{2,1,0:T(8,128)(2,1)S(1)} %get-tuple-element.180.refs_1_), channel_id=1, source_target_pairs={{0,2},{1,3},{2,0},{3,1},{4,6},{5,7},{6,4},{7,5},{8,10},{9,11},{10,... | collective-permute-start | bytes 737288 | tf_op jit(solution)/shard_map/ppermute | solution.py:67
  175.3 9.4 %collective-permute-start.23 = (bf16[2,32,1280]{2,1,0:T(8,128)(2,1)S(1)}, bf16[2,32,1280]{2,1,0:T(8,128)(2,1)S(1)}, u32[]{:S(2)}, u32[]{:S(2)}) collective-permute-start(bf16[2,32,1280]{2,1,0:T(8,128)(2,1)S(1)} %get-tuple-element.181.refs_2_), channel_id=1, source_target_pairs={{0,8},{1,9},{2,10},{3,11},{4,12},{5,13},{6,14},{7,15},{8,0},{9,1},... | collective-permute-start | bytes 491528 | tf_op jit(solution)/shard_map/ppermute | solution.py:67
  187.9 11.9 %collective-permute-start.24 = (bf16[4,48,1280]{2,1,0:T(8,128)(2,1)}, bf16[4,48,1280]{2,1,0:T(8,128)(2,1)}, u32[]{:S(2)}, u32[]{:S(2)}) collective-permute-start(bf16[4,48,1280]{2,1,0:T(8,128)(2,1)} %get-tuple-element.197.refs_0_), channel_id=1, source_target_pairs={{0,2},{1,3},{2,0},{3,1},{4,6},{5,7},{6,4},{7,5},{8,10},{9,11},{10,... | collective-permute-start | bytes 1474568 | tf_op jit(solution)/shard_map/ppermute | solution.py:67
  189.9 11.0 %collective-permute-start.25 = (bf16[4,48,1280]{2,1,0:T(8,128)(2,1)}, bf16[4,48,1280]{2,1,0:T(8,128)(2,1)}, u32[]{:S(2)}, u32[]{:S(2)}) collective-permute-start(bf16[4,48,1280]{2,1,0:T(8,128)(2,1)} %get-tuple-element.183.refs_1_), channel_id=1, source_target_pairs={{0,8},{1,9},{2,10},{3,11},{4,12},{5,13},{6,14},{7,15},{8,0},{9,1},... | collective-permute-start | bytes 1474568 | tf_op jit(solution)/shard_map/ppermute | solution.py:67
  190.9 7.4 %collective-permute-start.26 = (bf16[4,32,1280]{2,1,0:T(8,128)(2,1)}, bf16[4,32,1280]{2,1,0:T(8,128)(2,1)}, u32[]{:S(2)}, u32[]{:S(2)}) collective-permute-start(bf16[4,32,1280]{2,1,0:T(8,128)(2,1)} %get-tuple-element.184.refs_2_), channel_id=1, source_target_pairs={{0,4},{1,5},{2,6},{3,7},{4,0},{5,1},{6,2},{7,3},{8,12},{9,13},{10,... | collective-permute-start | bytes 983048 | tf_op jit(solution)/shard_map/ppermute | solution.py:67
  191.6 6.7 %collective-permute-start.29 = (bf16[4,32,1280]{2,1,0:T(8,128)(2,1)}, bf16[4,32,1280]{2,1,0:T(8,128)(2,1)}, u32[]{:S(2)}, u32[]{:S(2)}) collective-permute-start(bf16[4,32,1280]{2,1,0:T(8,128)(2,1)} %get-tuple-element.184.refs_2_), channel_id=1, source_target_pairs={{0,1},{1,0},{2,3},{3,2},{4,5},{5,4},{6,7},{7,6},{8,9},{9,8},{10,11... | collective-permute-start | bytes 983048 | tf_op jit(solution)/shard_map/ppermute | solution.py:67
  192.3 22.1 %collective-permute-start.27 = (bf16[4,48,1280]{2,1,0:T(8,128)(2,1)}, bf16[4,48,1280]{2,1,0:T(8,128)(2,1)}, u32[]{:S(2)}, u32[]{:S(2)}) collective-permute-start(bf16[4,48,1280]{2,1,0:T(8,128)(2,1)} %get-tuple-element.197.refs_0_), channel_id=1, source_target_pairs={{0,1},{1,0},{2,3},{3,2},{4,5},{5,4},{6,7},{7,6},{8,9},{9,8},{10,11... | collective-permute-start | bytes 1474568 | tf_op jit(solution)/shard_map/ppermute | solution.py:67
  198.3 16.1 %collective-permute-start.28 = (bf16[4,48,1280]{2,1,0:T(8,128)(2,1)}, bf16[4,48,1280]{2,1,0:T(8,128)(2,1)}, u32[]{:S(2)}, u32[]{:S(2)}) collective-permute-start(bf16[4,48,1280]{2,1,0:T(8,128)(2,1)} %get-tuple-element.183.refs_1_), channel_id=1, source_target_pairs={{0,1},{1,0},{2,3},{3,2},{4,5},{5,4},{6,7},{7,6},{8,9},{9,8},{10,11... | collective-permute-start | bytes 1474568 | tf_op jit(solution)/shard_map/ppermute | solution.py:67
  198.3 16.1 %collective-permute-start.32 = (bf16[4,32,1280]{2,1,0:T(8,128)(2,1)}, bf16[4,32,1280]{2,1,0:T(8,128)(2,1)}, u32[]{:S(2)}, u32[]{:S(2)}) collective-permute-start(bf16[4,32,1280]{2,1,0:T(8,128)(2,1)} %collective-permute-done.26.refs_5_), channel_id=1, source_target_pairs={{0,1},{1,0},{2,3},{3,2},{4,5},{5,4},{6,7},{7,6},{8,9},{9,8},{10,11... | collective-permute-start | bytes 983048 | tf_op jit(solution)/shard_map/ppermute | solution.py:67
  199.8 14.6 %collective-permute-start.30 = (bf16[4,48,1280]{2,1,0:T(8,128)(2,1)}, bf16[4,48,1280]{2,1,0:T(8,128)(2,1)}, u32[]{:S(2)}, u32[]{:S(2)}) collective-permute-start(bf16[4,48,1280]{2,1,0:T(8,128)(2,1)} %collective-permute-done.24.refs_3_), channel_id=1, source_target_pairs={{0,1},{1,0},{2,3},{3,2},{4,5},{5,4},{6,7},{7,6},{8,9},{9,8},{10,11... | collective-permute-start | bytes 1474568 | tf_op jit(solution)/shard_map/ppermute | solution.py:67
  200.9 13.6 %collective-permute-start.31 = (bf16[4,48,1280]{2,1,0:T(8,128)(2,1)}, bf16[4,48,1280]{2,1,0:T(8,128)(2,1)}, u32[]{:S(2)}, u32[]{:S(2)}) collective-permute-start(bf16[4,48,1280]{2,1,0:T(8,128)(2,1)} %collective-permute-done.25.refs_4_), channel_id=1, source_target_pairs={{0,1},{1,0},{2,3},{3,2},{4,5},{5,4},{6,7},{7,6},{8,9},{9,8},{10,11... | collective-permute-start | bytes 1474568 | tf_op jit(solution)/shard_map/ppermute | solution.py:67
  243.3 162.2 %all-gather.11.cloned.1.call-start = ((), (), s32[]{:S(2)}) async-start(), calls=%async_computation.11 | async-start | bytes 5570560 | tf_op jit(solution)/shard_map/all_gather | solution.py:100
  243.8 18.2 %collective-permute-start.34 = (bf16[4,48,1280]{2,1,0:T(8,128)(2,1)}, bf16[4,48,1280]{2,1,0:T(8,128)(2,1)S(1)}, u32[]{:S(2)}, u32[]{:S(2)}) collective-permute-start(bf16[4,48,1280]{2,1,0:T(8,128)(2,1)} %copy-done.45), channel_id=1, source_target_pairs={{0,8},{1,9},{2,10},{3,11},{4,12},{5,13},{6,14},{7,15},{8,0},{9,1},... | collective-permute-start | bytes 1474568 | tf_op jit(solution)/shard_map/ppermute | solution.py:67
  244.6 18.1 %collective-permute-start.35 = (bf16[4,48,1280]{2,1,0:T(8,128)(2,1)}, bf16[4,48,1280]{2,1,0:T(8,128)(2,1)S(1)}, u32[]{:S(2)}, u32[]{:S(2)}) collective-permute-start(bf16[4,48,1280]{2,1,0:T(8,128)(2,1)} %copy-done.44), channel_id=1, source_target_pairs={{0,4},{1,5},{2,6},{3,7},{4,0},{5,1},{6,2},{7,3},{8,12},{9,13},{10,... | collective-permute-start | bytes 1474568 | tf_op jit(solution)/shard_map/ppermute | solution.py:67
  245.8 16.9 %collective-permute-start.36 = (bf16[4,32,1280]{2,1,0:T(8,128)(2,1)}, bf16[4,32,1280]{2,1,0:T(8,128)(2,1)S(1)}, u32[]{:S(2)}, u32[]{:S(2)}) collective-permute-start(bf16[4,32,1280]{2,1,0:T(8,128)(2,1)} %copy-done.46), channel_id=1, source_target_pairs={{0,2},{1,3},{2,0},{3,1},{4,6},{5,7},{6,4},{7,5},{8,10},{9,11},{10,... | collective-permute-start | bytes 983048 | tf_op jit(solution)/shard_map/ppermute | solution.py:67
  264.1 9.8 %collective-permute-start.37 = (bf16[2,48,1280]{2,1,0:T(8,128)(2,1)S(1)}, bf16[2,48,1280]{2,1,0:T(8,128)(2,1)S(1)}, u32[]{:S(2)}, u32[]{:S(2)}) collective-permute-start(bf16[2,48,1280]{2,1,0:T(8,128)(2,1)S(1)} %get-tuple-element.204), channel_id=1, source_target_pairs={{0,4},{1,5},{2,6},{3,7},{4,0},{5,1},{6,2},{7,3},{8,12},{9,13},{10,... | collective-permute-start | bytes 737288 | tf_op jit(solution)/shard_map/ppermute | solution.py:67
  266.4 12.3 %collective-permute-start.38 = (bf16[2,48,1280]{2,1,0:T(8,128)(2,1)S(1)}, bf16[2,48,1280]{2,1,0:T(8,128)(2,1)S(1)}, u32[]{:S(2)}, u32[]{:S(2)}) collective-permute-start(bf16[2,48,1280]{2,1,0:T(8,128)(2,1)S(1)} %get-tuple-element.208), channel_id=1, source_target_pairs={{0,2},{1,3},{2,0},{3,1},{4,6},{5,7},{6,4},{7,5},{8,10},{9,11},{10,... | collective-permute-start | bytes 737288 | tf_op jit(solution)/shard_map/ppermute | solution.py:67
  266.4 7.4 %collective-permute-start.39 = (bf16[2,32,1280]{2,1,0:T(8,128)(2,1)S(1)}, bf16[2,32,1280]{2,1,0:T(8,128)(2,1)S(1)}, u32[]{:S(2)}, u32[]{:S(2)}) collective-permute-start(bf16[2,32,1280]{2,1,0:T(8,128)(2,1)S(1)} %get-tuple-element.209), channel_id=1, source_target_pairs={{0,8},{1,9},{2,10},{3,11},{4,12},{5,13},{6,14},{7,15},{8,0},{9,1},... | collective-permute-start | bytes 491528 | tf_op jit(solution)/shard_map/ppermute | solution.py:67
  279.7 8.4 %collective-permute-start.40 = (bf16[1,48,1280]{2,1,0:T(8,128)(2,1)S(1)}, bf16[1,48,1280]{2,1,0:T(8,128)(2,1)S(1)}, u32[]{:S(2)}, u32[]{:S(2)}) collective-permute-start(bf16[1,48,1280]{2,1,0:T(8,128)(2,1)S(1)} %get-tuple-element.213), channel_id=1, source_target_pairs={{0,2},{1,3},{2,0},{3,1},{4,6},{5,7},{6,4},{7,5},{8,10},{9,11},{10,... | collective-permute-start | bytes 368648 | tf_op jit(solution)/shard_map/ppermute | solution.py:67
  282.3 5.8 %collective-permute-start.41 = (bf16[1,48,1280]{2,1,0:T(8,128)(2,1)S(1)}, bf16[1,48,1280]{2,1,0:T(8,128)(2,1)S(1)}, u32[]{:S(2)}, u32[]{:S(2)}) collective-permute-start(bf16[1,48,1280]{2,1,0:T(8,128)(2,1)S(1)} %get-tuple-element.214), channel_id=1, source_target_pairs={{0,8},{1,9},{2,10},{3,11},{4,12},{5,13},{6,14},{7,15},{8,0},{9,1},... | collective-permute-start | bytes 368648 | tf_op jit(solution)/shard_map/ppermute | solution.py:67
  292.0 13.6 %all-to-all-start.3 = ((bf16[16,80,128]{2,1,0:T(8,128)(2,1)}), bf16[16,80,128]{2,1,0:T(8,128)(2,1)S(1)}, u32[]{:S(2)}, u32[]{:S(2)}) async-start(bf16[16,80,128]{2,1,0:T(8,128)(2,1)} %copy-done.29), calls=%async_computation.3 | async-start | bytes 655360 | tf_op jit(solution)/shard_map/all_to_all | solution.py:103
  335.1 22.7 %collective-permute-start.43 = (bf16[160,1280]{1,0:T(8,128)(2,1)}, bf16[160,1280]{1,0:T(8,128)(2,1)}, u32[]{:S(2)}, u32[]{:S(2)}) collective-permute-start(bf16[160,1280]{1,0:T(8,128)(2,1)} %get-tuple-element.283), channel_id=1, source_target_pairs={{0,16},{1,17},{2,18},{3,19},{4,20},{5,21},{6,22},{7,23},{8,24},{9,... | collective-permute-start | bytes 1228808 | tf_op jit(solution)/shard_map/ppermute | solution.py:67
  362.0 8.3 %collective-permute-start.44 = (bf16[8,128,1280]{2,1,0:T(8,128)(2,1)S(1)}, bf16[8,128,1280]{2,1,0:T(8,128)(2,1)S(1)}, u32[]{:S(2)}, u32[]{:S(2)}) collective-permute-start(bf16[8,128,1280]{2,1,0:T(8,128)(2,1)S(1)} %terms.3), channel_id=1, source_target_pairs={{0,1},{1,0},{2,3},{3,2},{4,5},{5,4},{6,7},{7,6},{8,9},{9,8},{10,11... | collective-permute-start | bytes 7864328 | tf_op jit(solution)/shard_map/ppermute | solution.py:67
  372.2 13.2 %collective-permute-start.45 = (bf16[4,48,1280]{2,1,0:T(8,128)(2,1)S(1)}, bf16[4,48,1280]{2,1,0:T(8,128)(2,1)S(1)}, u32[]{:S(2)}, u32[]{:S(2)}) collective-permute-start(bf16[4,48,1280]{2,1,0:T(8,128)(2,1)S(1)} %get-tuple-element.244), channel_id=1, source_target_pairs={{0,8},{1,9},{2,10},{3,11},{4,12},{5,13},{6,14},{7,15},{8,0},{9,1},... | collective-permute-start | bytes 1474568 | tf_op jit(solution)/shard_map/ppermute | solution.py:67
  372.8 13.3 %collective-permute-start.46 = (bf16[4,48,1280]{2,1,0:T(8,128)(2,1)S(1)}, bf16[4,48,1280]{2,1,0:T(8,128)(2,1)S(1)}, u32[]{:S(2)}, u32[]{:S(2)}) collective-permute-start(bf16[4,48,1280]{2,1,0:T(8,128)(2,1)S(1)} %get-tuple-element.245), channel_id=1, source_target_pairs={{0,4},{1,5},{2,6},{3,7},{4,0},{5,1},{6,2},{7,3},{8,12},{9,13},{10,... | collective-permute-start | bytes 1474568 | tf_op jit(solution)/shard_map/ppermute | solution.py:67
  374.4 9.5 %collective-permute-start.47 = (bf16[4,32,1280]{2,1,0:T(8,128)(2,1)S(1)}, bf16[4,32,1280]{2,1,0:T(8,128)(2,1)S(1)}, u32[]{:S(2)}, u32[]{:S(2)}) collective-permute-start(bf16[4,32,1280]{2,1,0:T(8,128)(2,1)S(1)} %get-tuple-element.246), channel_id=1, source_target_pairs={{0,2},{1,3},{2,0},{3,1},{4,6},{5,7},{6,4},{7,5},{8,10},{9,11},{10,... | collective-permute-start | bytes 983048 | tf_op jit(solution)/shard_map/ppermute | solution.py:67
  388.7 8.5 %collective-permute-start.48 = (bf16[2,48,1280]{2,1,0:T(8,128)(2,1)}, bf16[2,48,1280]{2,1,0:T(8,128)(2,1)}, u32[]{:S(2)}, u32[]{:S(2)}) collective-permute-start(bf16[2,48,1280]{2,1,0:T(8,128)(2,1)} %get-tuple-element.250), channel_id=1, source_target_pairs={{0,4},{1,5},{2,6},{3,7},{4,0},{5,1},{6,2},{7,3},{8,12},{9,13},{10,... | collective-permute-start | bytes 737288 | tf_op jit(solution)/shard_map/ppermute | solution.py:67
  390.4 7.3 %collective-permute-start.49 = (bf16[2,48,1280]{2,1,0:T(8,128)(2,1)}, bf16[2,48,1280]{2,1,0:T(8,128)(2,1)}, u32[]{:S(2)}, u32[]{:S(2)}) collective-permute-start(bf16[2,48,1280]{2,1,0:T(8,128)(2,1)} %get-tuple-element.251), channel_id=1, source_target_pairs={{0,2},{1,3},{2,0},{3,1},{4,6},{5,7},{6,4},{7,5},{8,10},{9,11},{10,... | collective-permute-start | bytes 737288 | tf_op jit(solution)/shard_map/ppermute | solution.py:67
  393.5 32.0 %all-to-all-start.5 = ((bf16[32,48,240]{2,1,0:T(8,128)(2,1)}), bf16[32,48,240]{2,1,0:T(8,128)(2,1)S(1)}, u32[]{:S(2)}, u32[]{:S(2)}) async-start(bf16[32,48,240]{2,1,0:T(8,128)(2,1)} %lay_out.1), calls=%async_computation.5 | async-start | bytes 1572864 | tf_op jit(solution)/shard_map/all_to_all | solution.py:106
  401.5 27.4 %collective-permute-start.54 = (bf16[1,48,1280]{2,1,0:T(8,128)(2,1)}, bf16[1,48,1280]{2,1,0:T(8,128)(2,1)S(1)}, u32[]{:S(2)}, u32[]{:S(2)}) collective-permute-start(bf16[1,48,1280]{2,1,0:T(8,128)(2,1)} %get-tuple-element.263), channel_id=1, source_target_pairs={{0,2},{1,3},{2,0},{3,1},{4,6},{5,7},{6,4},{7,5},{8,10},{9,11},{10,... | collective-permute-start | bytes 368648 | tf_op jit(solution)/shard_map/ppermute | solution.py:67
  403.0 26.0 %collective-permute-start.55 = (bf16[1,48,1280]{2,1,0:T(8,128)(2,1)S(1)}, bf16[1,48,1280]{2,1,0:T(8,128)(2,1)S(1)}, u32[]{:S(2)}, u32[]{:S(2)}) collective-permute-start(bf16[1,48,1280]{2,1,0:T(8,128)(2,1)S(1)} %get-tuple-element.264), channel_id=1, source_target_pairs={{0,8},{1,9},{2,10},{3,11},{4,12},{5,13},{6,14},{7,15},{8,0},{9,1},... | collective-permute-start | bytes 368648 | tf_op jit(solution)/shard_map/ppermute | solution.py:67
  404.0 24.9 %collective-permute-start.56 = (bf16[1,32,1280]{2,1,0:T(8,128)(2,1)}, bf16[1,32,1280]{2,1,0:T(8,128)(2,1)S(1)}, u32[]{:S(2)}, u32[]{:S(2)}) collective-permute-start(bf16[1,32,1280]{2,1,0:T(8,128)(2,1)} %get-tuple-element.265), channel_id=1, source_target_pairs={{0,4},{1,5},{2,6},{3,7},{4,0},{5,1},{6,2},{7,3},{8,12},{9,13},{10,... | collective-permute-start | bytes 245768 | tf_op jit(solution)/shard_map/ppermute | solution.py:67
  409.9 5.3 %collective-permute-start.51 = (bf16[40,1280]{1,0:T(8,128)(2,1)S(1)}, bf16[40,1280]{1,0:T(8,128)(2,1)S(1)}, u32[]{:S(2)}, u32[]{:S(2)}) collective-permute-start(bf16[40,1280]{1,0:T(8,128)(2,1)S(1)} %get-tuple-element.292), channel_id=1, source_target_pairs={{0,0},{1,2},{2,4},{3,6},{4,8},{5,10},{6,12},{7,14},{8,16},{9,18},{... | collective-permute-start | bytes 307208 | tf_op jit(solution)/shard_map/ppermute | solution.py:67
  411.5 17.5 %collective-permute-start.53 = (bf16[64,1280]{1,0:T(8,128)(2,1)S(1)}, bf16[64,1280]{1,0:T(8,128)(2,1)S(1)}, u32[]{:S(2)}, u32[]{:S(2)}) collective-permute-start(bf16[64,1280]{1,0:T(8,128)(2,1)S(1)} %get-tuple-element.289), channel_id=1, source_target_pairs={{0,16},{1,17},{2,18},{3,19},{4,20},{5,21},{6,22},{7,23},{8,24},{9,... | collective-permute-start | bytes 491528 | tf_op jit(solution)/shard_map/ppermute | solution.py:67
  415.2 13.7 %collective-permute-start.52 = (bf16[40,1280]{1,0:T(8,128)(2,1)}, bf16[40,1280]{1,0:T(8,128)(2,1)S(1)}, u32[]{:S(2)}, u32[]{:S(2)}) collective-permute-start(bf16[40,1280]{1,0:T(8,128)(2,1)} %get-tuple-element.291), channel_id=1, source_target_pairs={{0,1},{1,3},{2,5},{3,7},{4,9},{5,11},{6,13},{7,15},{8,17},{9,19},{... | collective-permute-start | bytes 307208 | tf_op jit(solution)/shard_map/ppermute | solution.py:67
  430.8 13.9 %collective-permute-start.57 = (bf16[64,1280]{1,0:T(8,128)(2,1)S(1)}, bf16[64,1280]{1,0:T(8,128)(2,1)S(1)}, u32[]{:S(2)}, u32[]{:S(2)}) collective-permute-start(bf16[64,1280]{1,0:T(8,128)(2,1)S(1)} %dynamic-slice_bitcast_fusion.2), channel_id=1, source_target_pairs={{0,16},{1,17},{2,18},{3,19},{4,20},{5,21},{6,22},{7,23},{8,24},{9,... | collective-permute-start | bytes 491528 | tf_op jit(solution)/shard_map/ppermute | solution.py:67
  431.6 12.5 %all-to-all-start.6 = ((f32[32,1,128]{2,1,0:T(1,128)}), f32[32,1,128]{2,1,0:T(1,128)S(1)}, u32[]{:S(2)}, u32[]{:S(2)}) async-start(f32[32,1,128]{2,1,0:T(1,128)} %get-tuple-element.268), calls=%async_computation.7 | async-start | bytes 32768 | tf_op jit(solution)/shard_map/all_to_all | solution.py:106
  (73 other events, 762.3 us)
Sparse Core Ops, SparseCore 0:
  30.6 45.8 all-gather.6
  145.6 45.6 all-gather.8
  243.4 87.6 reduce-scatter.1
  332.6 43.4 all-gather.10
